TPU v7x, 32 devices: a whole 2x2x4 slice. The times are simulated.
32 devices in a mesh: rcv: 4 (over y, core), src: 8 (over z, x).
Axes of the slice: x: 2, y: 2, z: 4, core: 2. Of those that a mesh axis runs over, the one named last changes fastest.
Arguments:
- pplus: bfloat16 [2048, 2, 1024], P('rcv', None, 'src'), may hold values from -0.125 to 0.125
- pminus: bfloat16 [2048, 2, 1024], P('rcv', None, 'src')
- band: int32 [8, 3], P('rcv'), may hold values from 0 to 7, as said below
Outputs:
- reflectivity: float32 [256, 8, 3, 2, 256], P('src', 'rcv')
- misfit: float32 [2048, 2, 1024], P('rcv', None, 'src')
Inputs may be any that keep to these rules, and one draw needn't show every extreme that they name: `band`: row b names block b first and then 3 - 1 other distinct blocks, each at most 2 blocks from b.
All inputs are finite; a program needn't handle non-finite values.
Results may differ from a plain program's by a relative error of at most 0.024.
Values may be sent and summed in bfloat16 or wider, within the bound.
No kernel may reach another device: no remote copies, remote signals or barrier semaphores. Data moves between devices by JAX's collectives and lax.ppermute only.
A program may use at most 64 MiB of HBM per device.

v0:
```python
import functools

import jax
import jax.numpy as jnp
from jax import lax
from jax.experimental import pallas as pl
from jax.experimental.pallas import tpu as pltpu
from jax.sharding import PartitionSpec as P

BLOCK = 256
NEIGH = 3
HALO_BLK = 2
ROWS_X = 2
SHARE_ROWS = 16
PAIR = 2


def ring_order(count):
    if count % ROWS_X or count < 2 * ROWS_X:
        return list(range(count))
    half = count // ROWS_X
    return [ROWS_X * p for p in range(half)] + [ROWS_X * p + 1 for p in reversed(range(half))]


def ring_place(count, index, shift):
    if count % ROWS_X or count < 2 * ROWS_X:
        return lax.rem(index + shift + count, count)
    half, odd = count // ROWS_X, lax.rem(index, ROWS_X)
    step = (index - odd) // ROWS_X
    place = lax.rem(jnp.where(odd == 1, count - 1 - step, step) + shift + count, count)
    return jnp.where(place < half, ROWS_X * place, ROWS_X * (count - 1 - place) + 1)


def along(sums):
    total = jnp.sum(sums, axis=1, keepdims=True)
    qq, qw = total[1:2], total[4:5]
    return jnp.where(qq > 0, qw / jnp.where(qq > 0, qq, 1.0), 0.0)


def maps_kernel(n_src, shifts, *refs):
    band_in, field = refs[:2]
    ends = [2, 2 + n_src, 2 + 2 * n_src, 2 + 3 * n_src]
    sources = [refs[a:b] for a, b in zip(ends[:-1], ends[1:])]
    grad, hess, images, sums_out = refs[ends[3] : ends[3] + 4]
    band, held, lhs, every, factors, image0, image1, sems, band_sem = refs[ends[3] + 4 :]
    blocks_here = grad.shape[0]
    rows = grad.shape[1] // 2
    cols = field.shape[2]
    half = cols // 2
    window = blocks_here * len(sources)
    me_rcv, me_src = lax.axis_index("rcv"), lax.axis_index("src")
    odd = lax.rem(me_rcv, 2)
    where = [ring_place(n_src, me_src, shift) for shift in shifts]

    fetches = [
        [pltpu.make_async_copy(chunk, held.at[g, slot], sems.at[g, slot]) for slot, chunk in enumerate(group)]
        for g, group in enumerate(sources)
    ]
    band_fetch = pltpu.make_async_copy(band_in, band, band_sem)
    band_fetch.start()
    for fetch in sum(fetches, []):
        fetch.start()
    band_fetch.wait()

    places = {}
    for i in range(blocks_here):
        for k in range(NEIGH):
            offset = band[i, k] - me_rcv * blocks_here
            before, here = offset < 0, (offset >= 0) & (offset < blocks_here)
            group = jnp.where(here, 0, jnp.where(jnp.where(before, 1, 0) == odd, 1, 2))
            inside = jnp.where(before, offset + blocks_here, jnp.where(here, offset, offset - blocks_here))
            places[i, k] = group * blocks_here + inside

    def store(i, slot, re_bf, im_bf):
        top, low = slice(2 * i * rows, (2 * i + 1) * rows), slice((2 * i + 1) * rows, (2 * i + 2) * rows)
        left, right = slice(slot * cols, slot * cols + half), slice(slot * cols + half, (slot + 1) * cols)
        lhs[top, left] = re_bf
        lhs[top, right] = im_bf
        lhs[low, left] = im_bf
        lhs[low, right] = -re_bf

    def fold(x):
        total = x[:, :128]
        for c in range(128, x.shape[1], 128):
            total = total + x[:, c : c + 128]
        return jnp.sum(total, axis=0, keepdims=True)

    def adjoint(out, first):
        for g in range(len(sources)):
            if first:
                for fetch in fetches[g]:
                    fetch.wait()
            chunks = jnp.concatenate([held[g, slot] for slot in range(n_src)], axis=1)
            both = lax.dot_general(lhs[...], chunks, (((1,), (1,)), ((), ())), preferred_element_type=jnp.float32)
            for inside in range(blocks_here):
                every[g * blocks_here + inside] = both[:, inside * BLOCK : (inside + 1) * BLOCK]
        for i in range(blocks_here):
            mine = slice(2 * i * rows, 2 * (i + 1) * rows)
            for k in range(NEIGH):
                part = every[places[i, k], mine, :]
                out[i, :, k * BLOCK : (k + 1) * BLOCK] = part
                factors[places[i, k], mine, :] = part.astype(jnp.bfloat16)

    def forward():
        wide = jnp.concatenate([factors[place] for place in range(window)], axis=1)
        for base in range(0, n_src, PAIR):
            slots = range(base, min(base + PAIR, n_src))
            columns = [
                jnp.concatenate([held[g, slot] for g in range(len(sources))], axis=0) for slot in slots
            ]
            prod = jnp.dot(wide, jnp.concatenate(columns, axis=1), preferred_element_type=jnp.float32)
            for slot in slots:
                left = (slot - base) * cols
                for i in range(blocks_here):
                    top = prod[2 * i * rows : (2 * i + 1) * rows, left : left + cols]
                    low = prod[(2 * i + 1) * rows : 2 * (i + 1) * rows, left : left + cols]
                    yield slot, i, top[:, :half] - low[:, half:], top[:, half:] + low[:, :half]

    factors[...] = jnp.zeros_like(factors)
    for slot in range(n_src):
        for i in range(blocks_here):
            rows_bf = field[where[slot], i * rows : (i + 1) * rows, :]
            store(i, slot, rows_bf[:, :half], rows_bf[:, half:])

    zero = jnp.zeros((1, 128), jnp.float32)
    gg, qq, gh, hh, qw, ww = zero, zero, zero, zero, zero, zero
    adjoint(grad, True)
    for i in range(blocks_here):
        gg += fold(grad[i] * grad[i])
    for slot, i, re, im in forward():
        mine = slice(i * rows, (i + 1) * rows)
        qq += fold(re * re + im * im)
        image0[slot, mine, :half] = re
        image0[slot, mine, half:] = im
        store(i, slot, re.astype(jnp.bfloat16), im.astype(jnp.bfloat16))
    adjoint(hess, False)
    for i in range(blocks_here):
        gh += fold(hess[i] * grad[i])
        hh += fold(hess[i] * hess[i])
    for slot, i, re, im in forward():
        mine = slice(i * rows, (i + 1) * rows)
        ww += fold(re * re + im * im)
        qw += fold(re * image0[slot, mine, :half] + im * image0[slot, mine, half:])
        image1[slot, mine, :half] = re
        image1[slot, mine, half:] = im
    sums = jnp.concatenate([gg, qq, gh, hh, qw, ww, zero, zero], axis=0)
    sums_out[...] = sums
    share_bf = along(sums).astype(jnp.bfloat16)
    share = share_bf.astype(jnp.float32)
    height = blocks_here * rows
    for slot in range(n_src):
        first = image0[slot]
        images[where[slot], :height] = first.astype(jnp.bfloat16)
        images[where[slot], height : 2 * height] = (image1[slot] - share * first).astype(jnp.bfloat16)
        images[where[slot], 2 * height :] = jnp.broadcast_to(share_bf, (SHARE_ROWS, cols))


def combine_kernel(sums, images, grad, hess, start, refl_out, misfit_out):
    n_src, height = images.shape[0], (images.shape[1] - SHARE_ROWS) // 2
    total = jnp.sum(sums[...], axis=1, keepdims=True)
    gg, qq, gh, hh, qw, ww = [total[i : i + 1] for i in range(6)]
    step0 = gg / qq
    grad_next = gg - 2 * step0 * gh + step0 * step0 * hh
    near = 1 + grad_next / gg
    image_sq = near * near * qq - 2 * near * step0 * qw + step0 * step0 * ww
    step1 = grad_next / image_sq
    c1 = step0 + step1 * near
    c2 = -step0 * step1
    blocks_here, rows = grad.shape[0], grad.shape[1] // 2
    half = start.shape[2] // 2
    for i in range(blocks_here):
        for k in range(NEIGH):
            for t in range(2):
                part = (i, slice(t * rows, (t + 1) * rows), slice(k * BLOCK, (k + 1) * BLOCK))
                refl_out[:, i, k, t, :] = c1 * grad[part] + c2 * hess[part]
    for s in range(n_src):
        share = images[s, 2 * height :].astype(jnp.float32)[:1, :1]
        first = images[s, :height].astype(jnp.float32)
        rest = images[s, height : 2 * height].astype(jnp.float32)
        left = start[s].astype(jnp.float32) - ((c1 + c2 * share) * first + c2 * rest)
        for i in range(blocks_here):
            place = slice(i * BLOCK + s * rows, i * BLOCK + (s + 1) * rows)
            mine = left[i * rows : (i + 1) * rows]
            misfit_out[place, 0, :] = mine[:, :half]
            misfit_out[place, 1, :] = mine[:, half:]


def summed(x, axis, count):
    if count & (count - 1):
        return lax.psum(x, axis)
    bit = 1
    while bit < count:
        radix = min(4, count // bit)
        others = [lax.ppermute(x, axis, [(d, d ^ (bit * m)) for d in range(count)]) for m in range(1, radix)]
        x = (x + others[0]) + (others[1] + others[2]) if radix == 4 else x + others[0]
        bit *= radix
    return x


def per_device(n_rcv, n_src, pplus, pminus, band):
    blocks_here = band.shape[0]
    rows = BLOCK // n_src
    cols = 2 * pplus.shape[2]
    order = ring_order(n_src)
    ahead = [(order[p], order[(p + 1) % n_src]) for p in range(n_src)]
    behind = [(d, s) for s, d in ahead]

    def swaps(first):
        pairs = [(r, r + 1) for r in range(first, n_rcv - 1, 2)]
        return pairs + [(d, s) for s, d in pairs]

    start = lax.optimization_barrier(pminus.reshape(blocks_here * BLOCK, cols))
    start = jnp.transpose(start.reshape(blocks_here, n_src, rows, cols), (1, 0, 2, 3))
    start = start.reshape(n_src, blocks_here * rows, cols)
    field = lax.all_to_all(start, "src", 0, 0, tiled=True)

    own = pplus.reshape(blocks_here * BLOCK, cols)
    chunks, shifts = [own], [0]
    fwd = bwd = own
    for step in range(1, n_src // 2 + 1):
        fwd = lax.ppermute(fwd, "src", ahead)
        chunks.append(fwd)
        shifts.append(-step)
        if len(chunks) < n_src:
            bwd = lax.ppermute(bwd, "src", behind)
            chunks.append(bwd)
            shifts.append(step)
    near = [lax.ppermute(c, "rcv", swaps(0)) for c in chunks]
    far = [lax.ppermute(c, "rcv", swaps(1)) for c in chunks]
    any_spec = pl.BlockSpec(memory_space=pl.ANY)
    vmem = pl.BlockSpec(memory_space=pltpu.VMEM)
    band_cols = NEIGH * BLOCK
    grad, hess, images, sums = pl.pallas_call(
        functools.partial(maps_kernel, n_src, shifts),
        out_shape=(
            jax.ShapeDtypeStruct((blocks_here, 2 * rows, band_cols), jnp.float32),
            jax.ShapeDtypeStruct((blocks_here, 2 * rows, band_cols), jnp.float32),
            jax.ShapeDtypeStruct((n_src, 2 * blocks_here * rows + SHARE_ROWS, cols), jnp.bfloat16),
            jax.ShapeDtypeStruct((8, 128), jnp.float32),
        ),
        in_specs=[any_spec, vmem] + [any_spec] * (3 * n_src),
        out_specs=[vmem] * 4,
        scratch_shapes=[
            pltpu.SMEM(band.shape, jnp.int32),
            pltpu.VMEM((3, n_src, blocks_here * BLOCK, cols), jnp.bfloat16),
            pltpu.VMEM((blocks_here * 2 * rows, n_src * cols), jnp.bfloat16),
            pltpu.VMEM((3 * blocks_here, blocks_here * 2 * rows, BLOCK), jnp.float32),
            pltpu.VMEM((3 * blocks_here, blocks_here * 2 * rows, BLOCK), jnp.bfloat16),
            pltpu.VMEM((n_src, blocks_here * rows, cols), jnp.float32),
            pltpu.VMEM((n_src, blocks_here * rows, cols), jnp.float32),
            pltpu.SemaphoreType.DMA((3, n_src)),
            pltpu.SemaphoreType.DMA,
        ],
        compiler_params=pltpu.CompilerParams(vmem_limit_bytes=60 << 20),
        name="maps",
    )(band, field, *chunks, *near, *far)

    images = lax.all_to_all(images, "src", 0, 0, tiled=True)
    sums = summed(summed(sums, "rcv", n_rcv), "src", n_src)
    return tuple(
        pl.pallas_call(
            combine_kernel,
            out_shape=(
                jax.ShapeDtypeStruct((rows, blocks_here, NEIGH, 2, BLOCK), jnp.float32),
                jax.ShapeDtypeStruct(pminus.shape, jnp.float32),
            ),
            in_specs=[vmem] * 5,
            out_specs=[vmem] * 2,
            compiler_params=pltpu.CompilerParams(vmem_limit_bytes=16 << 20),
            name="combine",
        )(sums, images, grad, hess, start)
    )


def solution(mesh):
    return jax.shard_map(
        functools.partial(per_device, mesh.shape["rcv"], mesh.shape["src"]),
        mesh=mesh,
        in_specs=(P("rcv", None, "src"), P("rcv", None, "src"), P("rcv", None)),
        out_specs=(P("src", "rcv", None, None, None), P("rcv", None, "src")),
        check_vma=False,
    )
```

profile of v0, /device:TPU:0, one launch (start us, length us, event | category | flops | bytes accessed | tf_op | source)
XLA Modules:
  0.0 85.5 jit_solution(12466213691619698218)
XLA Ops:
  1.7 3.0 %collective-permute-start.1 = (bf16[512,256]{1,0:T(8,128)(2,1)S(1)}, bf16[512,256]{1,0:T(8,128)(2,1)S(1)}, u32[]{:S(2)}, u32[]{:S(2)}) collective-permute-start(bf16[512,256]{1,0:T(8,128)(2,1)S(1)} %bitcast.12), channel_id=1, source_target_pairs={{2,0},{4,2},{6,4},{7,6},{5,7},{3,5},{1,3},{0,1},{10,8},{12,10},{14... | collective-permute-start | bytes 786440 | tf_op jit(solution)/shard_map/ppermute | solution.py:225
  5.5 3.3 %collective-permute-start.7 = (bf16[512,256]{1,0:T(8,128)(2,1)S(1)}, bf16[512,256]{1,0:T(8,128)(2,1)S(1)}, u32[]{:S(2)}, u32[]{:S(2)}) collective-permute-start(bf16[512,256]{1,0:T(8,128)(2,1)S(1)} %bitcast.15), channel_id=1, source_target_pairs={{0,8},{16,24},{8,0},{24,16},{1,9},{17,25},{9,1},{25,17},{2,10},{18... | collective-permute-start | bytes 786440 | tf_op jit(solution)/shard_map/ppermute | solution.py:228
  8.8 2.3 %collective-permute-done.1.refs_4_ = bf16[512,256]{1,0:T(8,128)(2,1)S(1)} collective-permute-done((bf16[512,256]{1,0:T(8,128)(2,1)S(1)}, bf16[512,256]{1,0:T(8,128)(2,1)S(1)}, u32[]{:S(2)}, u32[]{:S(2)}) %collective-permute-start.1) | collective-permute-done | bytes 262176 | tf_op jit(solution)/shard_map/ppermute | solution.py:225
  11.7 1.7 %collective-permute-start.3 = (bf16[512,256]{1,0:T(8,128)(2,1)S(1)}, bf16[512,256]{1,0:T(8,128)(2,1)S(1)}, u32[]{:S(2)}, u32[]{:S(2)}) collective-permute-start(bf16[512,256]{1,0:T(8,128)(2,1)S(1)} %collective-permute-done.1.refs_4_), channel_id=1, source_target_pairs={{2,0},{4,2},{6,4},{7,6},{5,7},{3,5},{1,3},{0,1},{10,8},{12,10},{14... | collective-permute-start | bytes 786440 | tf_op jit(solution)/shard_map/ppermute | solution.py:225
  13.8 2.5 %collective-permute-start.9 = (bf16[512,256]{1,0:T(8,128)(2,1)S(1)}, bf16[512,256]{1,0:T(8,128)(2,1)S(1)}, u32[]{:S(2)}, u32[]{:S(2)}) collective-permute-start(bf16[512,256]{1,0:T(8,128)(2,1)S(1)} %collective-permute-done.1.refs_4_), channel_id=1, source_target_pairs={{0,8},{16,24},{8,0},{24,16},{1,9},{17,25},{9,1},{25,17},{2,10},{18... | collective-permute-start | bytes 786440 | tf_op jit(solution)/shard_map/ppermute | solution.py:228
  17.0 2.1 %collective-permute-start.8 = (bf16[512,256]{1,0:T(8,128)(2,1)S(1)}, bf16[512,256]{1,0:T(8,128)(2,1)S(1)}, u32[]{:S(2)}, u32[]{:S(2)}) collective-permute-start(bf16[512,256]{1,0:T(8,128)(2,1)S(1)} %collective-permute-done.refs_3_), channel_id=1, source_target_pairs={{0,8},{16,24},{8,0},{24,16},{1,9},{17,25},{9,1},{25,17},{2,10},{18... | collective-permute-start | bytes 786440 | tf_op jit(solution)/shard_map/ppermute | solution.py:228
  21.5 1.5 %collective-permute-start.5 = (bf16[512,256]{1,0:T(8,128)(2,1)S(1)}, bf16[512,256]{1,0:T(8,128)(2,1)}, u32[]{:S(2)}, u32[]{:S(2)}) collective-permute-start(bf16[512,256]{1,0:T(8,128)(2,1)S(1)} %collective-permute-done.3.refs_6_), channel_id=1, source_target_pairs={{2,0},{4,2},{6,4},{7,6},{5,7},{3,5},{1,3},{0,1},{10,8},{12,10},{14... | collective-permute-start | bytes 786440 | tf_op jit(solution)/shard_map/ppermute | solution.py:225
  23.0 1.7 %collective-permute-start.11 = (bf16[512,256]{1,0:T(8,128)(2,1)S(1)}, bf16[512,256]{1,0:T(8,128)(2,1)}, u32[]{:S(2)}, u32[]{:S(2)}) collective-permute-start(bf16[512,256]{1,0:T(8,128)(2,1)S(1)} %collective-permute-done.3.refs_6_), channel_id=1, source_target_pairs={{0,8},{16,24},{8,0},{24,16},{1,9},{17,25},{9,1},{25,17},{2,10},{18... | collective-permute-start | bytes 786440 | tf_op jit(solution)/shard_map/ppermute | solution.py:228
  24.7 1.4 %collective-permute-start.18 = (bf16[512,256]{1,0:T(8,128)(2,1)S(1)}, bf16[512,256]{1,0:T(8,128)(2,1)}, u32[]{:S(2)}, u32[]{:S(2)}) collective-permute-start(bf16[512,256]{1,0:T(8,128)(2,1)S(1)} %collective-permute-done.2.refs_5_), channel_id=1, source_target_pairs={{8,16},{16,8},{9,17},{17,9},{10,18},{18,10},{11,19},{19,11},{12,20... | collective-permute-start | bytes 786440 | tf_op jit(solution)/shard_map/ppermute | solution.py:229
  26.1 2.9 %collective-permute-start.10 = (bf16[512,256]{1,0:T(8,128)(2,1)S(1)}, bf16[512,256]{1,0:T(8,128)(2,1)}, u32[]{:S(2)}, u32[]{:S(2)}) collective-permute-start(bf16[512,256]{1,0:T(8,128)(2,1)S(1)} %collective-permute-done.2.refs_5_), channel_id=1, source_target_pairs={{0,8},{16,24},{8,0},{24,16},{1,9},{17,25},{9,1},{25,17},{2,10},{18... | collective-permute-start | bytes 786440 | tf_op jit(solution)/shard_map/ppermute | solution.py:228
  29.0 1.5 %collective-permute-start.6 = (bf16[512,256]{1,0:T(8,128)(2,1)S(1)}, bf16[512,256]{1,0:T(8,128)(2,1)}, u32[]{:S(2)}, u32[]{:S(2)}) collective-permute-start(bf16[512,256]{1,0:T(8,128)(2,1)S(1)} %collective-permute-done.4.refs_7_), channel_id=1, source_target_pairs={{0,2},{2,4},{4,6},{6,7},{7,5},{5,3},{3,1},{1,0},{8,10},{10,12},{12... | collective-permute-start | bytes 786440 | tf_op jit(solution)/shard_map/ppermute | solution.py:221
  32.6 5.3 %all-to-all-start = ((bf16[8,64,256]{2,1,0:T(8,128)(2,1)}), bf16[8,64,256]{2,1,0:T(8,128)(2,1)S(1)}, u32[]{:S(2)}, u32[]{:S(2)}) async-start(bf16[8,64,256]{2,1,0:T(8,128)(2,1)} %bitcast.2.start), calls=%async_computation | async-start | bytes 524288 | tf_op jit(solution)/shard_map/all_to_all | solution.py:215
  37.9 2.3 %collective-permute-start.13 = (bf16[512,256]{1,0:T(8,128)(2,1)}, bf16[512,256]{1,0:T(8,128)(2,1)S(1)}, u32[]{:S(2)}, u32[]{:S(2)}) collective-permute-start(bf16[512,256]{1,0:T(8,128)(2,1)} %collective-permute-done.5.refs_8_), channel_id=1, source_target_pairs={{0,8},{16,24},{8,0},{24,16},{1,9},{17,25},{9,1},{25,17},{2,10},{18... | collective-permute-start | bytes 786440 | tf_op jit(solution)/shard_map/ppermute | solution.py:228
  40.9 2.1 %collective-permute-start.12 = (bf16[512,256]{1,0:T(8,128)(2,1)S(1)}, bf16[512,256]{1,0:T(8,128)(2,1)S(1)}, u32[]{:S(2)}, u32[]{:S(2)}) collective-permute-start(bf16[512,256]{1,0:T(8,128)(2,1)S(1)} %collective-permute-done.4.refs_7_), channel_id=1, source_target_pairs={{0,8},{16,24},{8,0},{24,16},{1,9},{17,25},{9,1},{25,17},{2,10},{18... | collective-permute-start | bytes 786440 | tf_op jit(solution)/shard_map/ppermute | solution.py:228
  43.7 2.3 %collective-permute-start.14 = (bf16[512,256]{1,0:T(8,128)(2,1)}, bf16[512,256]{1,0:T(8,128)(2,1)S(1)}, u32[]{:S(2)}, u32[]{:S(2)}) collective-permute-start(bf16[512,256]{1,0:T(8,128)(2,1)} %collective-permute-done.6.refs_9_), channel_id=1, source_target_pairs={{0,8},{16,24},{8,0},{24,16},{1,9},{17,25},{9,1},{25,17},{2,10},{18... | collective-permute-start | bytes 786440 | tf_op jit(solution)/shard_map/ppermute | solution.py:228
  48.4 10.2 %maps.1 = (f32[2,64,768]{2,1,0:T(8,128)}, f32[2,64,768]{2,1,0:T(8,128)}, bf16[8,144,256]{2,1,0:T(8,128)(2,1)}, f32[8,128]{1,0:T(8,128)}) custom-call(s32[2,3]{1,0:T(2,128)} %refs_0_.1, bf16[8,64,256]{2,1,0:T(8,128)(2,1)} %copy-done.3, bf16[512,256]{1,0:T(8,128)(2,1)} %bitcast.16, bf16[512,256]{1,0:T(8,128)(2,1)} %copy-done.5, bf16[512,256]{1,0:T(8,128)(2,1)} %copy-done.4, ...), custom_call_target="tpu_custom_call" | custom-call | tf_op jit(solution)/shard_map/maps/pallas_call | solution.py:233
  58.6 5.4 %all-to-all-start.1 = ((bf16[8,144,256]{2,1,0:T(8,128)(2,1)}), bf16[8,144,256]{2,1,0:T(8,128)(2,1)S(1)}, u32[]{:S(2)}, u32[]{:S(2)}) async-start(bf16[8,144,256]{2,1,0:T(8,128)(2,1)} %get-tuple-element.7), calls=%async_computation.1 | async-start | bytes 1179648 | tf_op jit(solution)/shard_map/all_to_all | solution.py:258
  65.0 5.1 %collective-permute-start.24 = (f32[8,128]{1,0:T(8,128)S(1)}, f32[8,128]{1,0:T(8,128)S(1)}, u32[]{:S(2)}, u32[]{:S(2)}) collective-permute-start(f32[8,128]{1,0:T(8,128)S(1)} %copy-done.22), channel_id=1, source_target_pairs={{0,16},{8,24},{16,0},{24,8},{1,17},{9,25},{17,1},{25,9},{2,18},{10... | collective-permute-start | bytes 12296 | tf_op jit(solution)/shard_map/ppermute | solution.py:194
  70.1 1.6 %collective-permute-done.24 = f32[8,128]{1,0:T(8,128)S(1)} collective-permute-done((f32[8,128]{1,0:T(8,128)S(1)}, f32[8,128]{1,0:T(8,128)S(1)}, u32[]{:S(2)}, u32[]{:S(2)}) %collective-permute-start.24) | collective-permute-done | bytes 4128 | tf_op jit(solution)/shard_map/ppermute | solution.py:194
  71.7 2.6 %collective-permute-start.28 = (f32[8,128]{1,0:T(8,128)S(1)}, f32[8,128]{1,0:T(8,128)S(1)}, u32[]{:S(2)}, u32[]{:S(2)}) collective-permute-start(f32[8,128]{1,0:T(8,128)S(1)} %add_add_fusion.1), channel_id=1, source_target_pairs={{0,3},{1,2},{2,1},{3,0},{4,7},{5,6},{6,5},{7,4},{8,11},{9,10},{10,... | collective-permute-start | bytes 12296 | tf_op jit(solution)/shard_map/ppermute | solution.py:194
  76.3 1.7 %collective-permute-done.27 = f32[8,128]{1,0:T(8,128)S(1)} collective-permute-done((f32[8,128]{1,0:T(8,128)S(1)}, f32[8,128]{1,0:T(8,128)S(1)}, u32[]{:S(2)}, u32[]{:S(2)}) %collective-permute-start.27) | collective-permute-done | bytes 4128 | tf_op jit(solution)/shard_map/ppermute | solution.py:194
  78.5 2.4 %collective-permute-start.29 = (f32[8,128]{1,0:T(8,128)S(1)}, f32[8,128]{1,0:T(8,128)S(1)}, u32[]{:S(2)}, u32[]{:S(2)}) collective-permute-start(f32[8,128]{1,0:T(8,128)S(1)} %add_add_fusion), channel_id=1, source_target_pairs={{0,4},{1,5},{2,6},{3,7},{4,0},{5,1},{6,2},{7,3},{8,12},{9,13},{10,... | collective-permute-start | bytes 12296 | tf_op jit(solution)/shard_map/ppermute | solution.py:194
  81.0 2.1 %collective-permute-done.29 = f32[8,128]{1,0:T(8,128)S(1)} collective-permute-done((f32[8,128]{1,0:T(8,128)S(1)}, f32[8,128]{1,0:T(8,128)S(1)}, u32[]{:S(2)}, u32[]{:S(2)}) %collective-permute-start.29) | collective-permute-done | bytes 4128 | tf_op jit(solution)/shard_map/ppermute | solution.py:194
  83.1 2.5 %combine.1 = (f32[32,2,3,2,256]{4,3,2,1,0:T(2,128)}, f32[512,2,128]{2,1,0:T(2,128)}) custom-call(f32[8,128]{1,0:T(8,128)S(1)} %add.27.sums, bf16[8,144,256]{2,1,0:T(8,128)(2,1)S(1)} %all-to-all-done.1.images, f32[2,64,768]{2,1,0:T(8,128)S(1)} %copy-done, f32[2,64,768]{2,1,0:T(8,128)S(1)} %copy-done.1, bf16[8,64,256]{2,1,0:T(8,128)(2,1)} %bitcast.2.start), custom_call_target="tpu_custom_call" | custom-call | tf_op jit(solution)/shard_map/combine/pallas_call | solution.py:261
  (94 shorter events, 15.3 us)
Async XLA Ops:
  1.7 9.4 %collective-permute-start.1 = (bf16[512,256]{1,0:T(8,128)(2,1)S(1)}, bf16[512,256]{1,0:T(8,128)(2,1)S(1)}, u32[]{:S(2)}, u32[]{:S(2)}) collective-permute-start(bf16[512,256]{1,0:T(8,128)(2,1)S(1)} %bitcast.12), channel_id=1, source_target_pairs={{2,0},{4,2},{6,4},{7,6},{5,7},{3,5},{1,3},{0,1},{10,8},{12,10},{14... | collective-permute-start | bytes 786440 | tf_op jit(solution)/shard_map/ppermute | solution.py:225
  4.7 8.8 %collective-permute-start = (bf16[512,256]{1,0:T(8,128)(2,1)S(1)}, bf16[512,256]{1,0:T(8,128)(2,1)S(1)}, u32[]{:S(2)}, u32[]{:S(2)}) collective-permute-start(bf16[512,256]{1,0:T(8,128)(2,1)S(1)} %bitcast.13), channel_id=1, source_target_pairs={{0,2},{2,4},{4,6},{6,7},{7,5},{5,3},{3,1},{1,0},{8,10},{10,12},{12... | collective-permute-start | bytes 786440 | tf_op jit(solution)/shard_map/ppermute | solution.py:221
  4.8 9.0 %collective-permute-start.15 = (bf16[512,256]{1,0:T(8,128)(2,1)S(1)}, bf16[512,256]{1,0:T(8,128)(2,1)S(1)}, u32[]{:S(2)}, u32[]{:S(2)}) collective-permute-start(bf16[512,256]{1,0:T(8,128)(2,1)S(1)} %bitcast.14), channel_id=1, source_target_pairs={{8,16},{16,8},{9,17},{17,9},{10,18},{18,10},{11,19},{19,11},{12,20... | collective-permute-start | bytes 786440 | tf_op jit(solution)/shard_map/ppermute | solution.py:229
  5.5 10.8 %collective-permute-start.7 = (bf16[512,256]{1,0:T(8,128)(2,1)S(1)}, bf16[512,256]{1,0:T(8,128)(2,1)S(1)}, u32[]{:S(2)}, u32[]{:S(2)}) collective-permute-start(bf16[512,256]{1,0:T(8,128)(2,1)S(1)} %bitcast.15), channel_id=1, source_target_pairs={{0,8},{16,24},{8,0},{24,16},{1,9},{17,25},{9,1},{25,17},{2,10},{18... | collective-permute-start | bytes 786440 | tf_op jit(solution)/shard_map/ppermute | solution.py:228
  11.1 5.9 %collective-permute-start.17 = (bf16[512,256]{1,0:T(8,128)(2,1)S(1)}, bf16[512,256]{1,0:T(8,128)(2,1)S(1)}, u32[]{:S(2)}, u32[]{:S(2)}) collective-permute-start(bf16[512,256]{1,0:T(8,128)(2,1)S(1)} %collective-permute-done.1.refs_4_), channel_id=1, source_target_pairs={{8,16},{16,8},{9,17},{17,9},{10,18},{18,10},{11,19},{19,11},{12,20... | collective-permute-start | bytes 786440 | tf_op jit(solution)/shard_map/ppermute | solution.py:229
  11.7 7.4 %collective-permute-start.3 = (bf16[512,256]{1,0:T(8,128)(2,1)S(1)}, bf16[512,256]{1,0:T(8,128)(2,1)S(1)}, u32[]{:S(2)}, u32[]{:S(2)}) collective-permute-start(bf16[512,256]{1,0:T(8,128)(2,1)S(1)} %collective-permute-done.1.refs_4_), channel_id=1, source_target_pairs={{2,0},{4,2},{6,4},{7,6},{5,7},{3,5},{1,3},{0,1},{10,8},{12,10},{14... | collective-permute-start | bytes 786440 | tf_op jit(solution)/shard_map/ppermute | solution.py:225
  13.5 7.5 %collective-permute-start.2 = (bf16[512,256]{1,0:T(8,128)(2,1)S(1)}, bf16[512,256]{1,0:T(8,128)(2,1)S(1)}, u32[]{:S(2)}, u32[]{:S(2)}) collective-permute-start(bf16[512,256]{1,0:T(8,128)(2,1)S(1)} %collective-permute-done.refs_3_), channel_id=1, source_target_pairs={{0,2},{2,4},{4,6},{6,7},{7,5},{5,3},{3,1},{1,0},{8,10},{10,12},{12... | collective-permute-start | bytes 786440 | tf_op jit(solution)/shard_map/ppermute | solution.py:221
  13.8 7.7 %collective-permute-start.9 = (bf16[512,256]{1,0:T(8,128)(2,1)S(1)}, bf16[512,256]{1,0:T(8,128)(2,1)S(1)}, u32[]{:S(2)}, u32[]{:S(2)}) collective-permute-start(bf16[512,256]{1,0:T(8,128)(2,1)S(1)} %collective-permute-done.1.refs_4_), channel_id=1, source_target_pairs={{0,8},{16,24},{8,0},{24,16},{1,9},{17,25},{9,1},{25,17},{2,10},{18... | collective-permute-start | bytes 786440 | tf_op jit(solution)/shard_map/ppermute | solution.py:228
  16.3 6.7 %collective-permute-start.16 = (bf16[512,256]{1,0:T(8,128)(2,1)S(1)}, bf16[512,256]{1,0:T(8,128)(2,1)S(1)}, u32[]{:S(2)}, u32[]{:S(2)}) collective-permute-start(bf16[512,256]{1,0:T(8,128)(2,1)S(1)} %collective-permute-done.refs_3_), channel_id=1, source_target_pairs={{8,16},{16,8},{9,17},{17,9},{10,18},{18,10},{11,19},{19,11},{12,20... | collective-permute-start | bytes 786440 | tf_op jit(solution)/shard_map/ppermute | solution.py:229
  17.0 7.7 %collective-permute-start.8 = (bf16[512,256]{1,0:T(8,128)(2,1)S(1)}, bf16[512,256]{1,0:T(8,128)(2,1)S(1)}, u32[]{:S(2)}, u32[]{:S(2)}) collective-permute-start(bf16[512,256]{1,0:T(8,128)(2,1)S(1)} %collective-permute-done.refs_3_), channel_id=1, source_target_pairs={{0,8},{16,24},{8,0},{24,16},{1,9},{17,25},{9,1},{25,17},{2,10},{18... | collective-permute-start | bytes 786440 | tf_op jit(solution)/shard_map/ppermute | solution.py:228
  19.1 6.9 %collective-permute-start.19 = (bf16[512,256]{1,0:T(8,128)(2,1)S(1)}, bf16[512,256]{1,0:T(8,128)(2,1)S(1)}, u32[]{:S(2)}, u32[]{:S(2)}) collective-permute-start(bf16[512,256]{1,0:T(8,128)(2,1)S(1)} %collective-permute-done.3.refs_6_), channel_id=1, source_target_pairs={{8,16},{16,8},{9,17},{17,9},{10,18},{18,10},{11,19},{19,11},{12,20... | collective-permute-start | bytes 786440 | tf_op jit(solution)/shard_map/ppermute | solution.py:229
  21.0 8.0 %collective-permute-start.4 = (bf16[512,256]{1,0:T(8,128)(2,1)S(1)}, bf16[512,256]{1,0:T(8,128)(2,1)S(1)}, u32[]{:S(2)}, u32[]{:S(2)}) collective-permute-start(bf16[512,256]{1,0:T(8,128)(2,1)S(1)} %collective-permute-done.2.refs_5_), channel_id=1, source_target_pairs={{0,2},{2,4},{4,6},{6,7},{7,5},{5,3},{3,1},{1,0},{8,10},{10,12},{12... | collective-permute-start | bytes 786440 | tf_op jit(solution)/shard_map/ppermute | solution.py:221
  21.5 8.9 %collective-permute-start.5 = (bf16[512,256]{1,0:T(8,128)(2,1)S(1)}, bf16[512,256]{1,0:T(8,128)(2,1)}, u32[]{:S(2)}, u32[]{:S(2)}) collective-permute-start(bf16[512,256]{1,0:T(8,128)(2,1)S(1)} %collective-permute-done.3.refs_6_), channel_id=1, source_target_pairs={{2,0},{4,2},{6,4},{7,6},{5,7},{3,5},{1,3},{0,1},{10,8},{12,10},{14... | collective-permute-start | bytes 786440 | tf_op jit(solution)/shard_map/ppermute | solution.py:225
  23.0 14.9 %collective-permute-start.11 = (bf16[512,256]{1,0:T(8,128)(2,1)S(1)}, bf16[512,256]{1,0:T(8,128)(2,1)}, u32[]{:S(2)}, u32[]{:S(2)}) collective-permute-start(bf16[512,256]{1,0:T(8,128)(2,1)S(1)} %collective-permute-done.3.refs_6_), channel_id=1, source_target_pairs={{0,8},{16,24},{8,0},{24,16},{1,9},{17,25},{9,1},{25,17},{2,10},{18... | collective-permute-start | bytes 786440 | tf_op jit(solution)/shard_map/ppermute | solution.py:228
  24.7 15.5 %collective-permute-start.18 = (bf16[512,256]{1,0:T(8,128)(2,1)S(1)}, bf16[512,256]{1,0:T(8,128)(2,1)}, u32[]{:S(2)}, u32[]{:S(2)}) collective-permute-start(bf16[512,256]{1,0:T(8,128)(2,1)S(1)} %collective-permute-done.2.refs_5_), channel_id=1, source_target_pairs={{8,16},{16,8},{9,17},{17,9},{10,18},{18,10},{11,19},{19,11},{12,20... | collective-permute-start | bytes 786440 | tf_op jit(solution)/shard_map/ppermute | solution.py:229
  26.1 14.8 %collective-permute-start.10 = (bf16[512,256]{1,0:T(8,128)(2,1)S(1)}, bf16[512,256]{1,0:T(8,128)(2,1)}, u32[]{:S(2)}, u32[]{:S(2)}) collective-permute-start(bf16[512,256]{1,0:T(8,128)(2,1)S(1)} %collective-permute-done.2.refs_5_), channel_id=1, source_target_pairs={{0,8},{16,24},{8,0},{24,16},{1,9},{17,25},{9,1},{25,17},{2,10},{18... | collective-permute-start | bytes 786440 | tf_op jit(solution)/shard_map/ppermute | solution.py:228
  29.0 14.1 %collective-permute-start.6 = (bf16[512,256]{1,0:T(8,128)(2,1)S(1)}, bf16[512,256]{1,0:T(8,128)(2,1)}, u32[]{:S(2)}, u32[]{:S(2)}) collective-permute-start(bf16[512,256]{1,0:T(8,128)(2,1)S(1)} %collective-permute-done.4.refs_7_), channel_id=1, source_target_pairs={{0,2},{2,4},{4,6},{6,7},{7,5},{5,3},{3,1},{1,0},{8,10},{10,12},{12... | collective-permute-start | bytes 786440 | tf_op jit(solution)/shard_map/ppermute | solution.py:221
  30.4 13.3 %collective-permute-start.21 = (bf16[512,256]{1,0:T(8,128)(2,1)}, bf16[512,256]{1,0:T(8,128)(2,1)}, u32[]{:S(2)}, u32[]{:S(2)}) collective-permute-start(bf16[512,256]{1,0:T(8,128)(2,1)} %collective-permute-done.5.refs_8_), channel_id=1, source_target_pairs={{8,16},{16,8},{9,17},{17,9},{10,18},{18,10},{11,19},{19,11},{12,20... | collective-permute-start | bytes 786440 | tf_op jit(solution)/shard_map/ppermute | solution.py:229
  32.6 14.0 %all-to-all-start = ((bf16[8,64,256]{2,1,0:T(8,128)(2,1)}), bf16[8,64,256]{2,1,0:T(8,128)(2,1)S(1)}, u32[]{:S(2)}, u32[]{:S(2)}) async-start(bf16[8,64,256]{2,1,0:T(8,128)(2,1)} %bitcast.2.start), calls=%async_computation | async-start | bytes 524288 | tf_op jit(solution)/shard_map/all_to_all | solution.py:215
  37.9 8.7 %collective-permute-start.13 = (bf16[512,256]{1,0:T(8,128)(2,1)}, bf16[512,256]{1,0:T(8,128)(2,1)S(1)}, u32[]{:S(2)}, u32[]{:S(2)}) collective-permute-start(bf16[512,256]{1,0:T(8,128)(2,1)} %collective-permute-done.5.refs_8_), channel_id=1, source_target_pairs={{0,8},{16,24},{8,0},{24,16},{1,9},{17,25},{9,1},{25,17},{2,10},{18... | collective-permute-start | bytes 786440 | tf_op jit(solution)/shard_map/ppermute | solution.py:228
  40.2 6.5 %collective-permute-start.20 = (bf16[512,256]{1,0:T(8,128)(2,1)S(1)}, bf16[512,256]{1,0:T(8,128)(2,1)S(1)}, u32[]{:S(2)}, u32[]{:S(2)}) collective-permute-start(bf16[512,256]{1,0:T(8,128)(2,1)S(1)} %collective-permute-done.4.refs_7_), channel_id=1, source_target_pairs={{8,16},{16,8},{9,17},{17,9},{10,18},{18,10},{11,19},{19,11},{12,20... | collective-permute-start | bytes 786440 | tf_op jit(solution)/shard_map/ppermute | solution.py:229
  58.6 24.4 %all-to-all-start.1 = ((bf16[8,144,256]{2,1,0:T(8,128)(2,1)}), bf16[8,144,256]{2,1,0:T(8,128)(2,1)S(1)}, u32[]{:S(2)}, u32[]{:S(2)}) async-start(bf16[8,144,256]{2,1,0:T(8,128)(2,1)} %get-tuple-element.7), calls=%async_computation.1 | async-start | bytes 1179648 | tf_op jit(solution)/shard_map/all_to_all | solution.py:258
  64.1 6.0 %collective-permute-start.25 = (f32[8,128]{1,0:T(8,128)S(1)}, f32[8,128]{1,0:T(8,128)S(1)}, u32[]{:S(2)}, u32[]{:S(2)}) collective-permute-start(f32[8,128]{1,0:T(8,128)S(1)} %copy-done.22), channel_id=1, source_target_pairs={{0,24},{8,16},{16,8},{24,0},{1,25},{9,17},{17,9},{25,1},{2,26},{10... | collective-permute-start | bytes 12296 | tf_op jit(solution)/shard_map/ppermute | solution.py:194
  65.0 6.7 %collective-permute-start.24 = (f32[8,128]{1,0:T(8,128)S(1)}, f32[8,128]{1,0:T(8,128)S(1)}, u32[]{:S(2)}, u32[]{:S(2)}) collective-permute-start(f32[8,128]{1,0:T(8,128)S(1)} %copy-done.22), channel_id=1, source_target_pairs={{0,16},{8,24},{16,0},{24,8},{1,17},{9,25},{17,1},{25,9},{2,18},{10... | collective-permute-start | bytes 12296 | tf_op jit(solution)/shard_map/ppermute | solution.py:194
  (31 other events, 314.2 us)
where the time goes:
time: 86.1 us; the launch traced here: 85.5 us
  starting transfers between devices  57.3 us (67%)
  Pallas kernels  12.7 us (15%)
  waiting for transfers between devices  11.7 us (14%)
  local copies, waits for them, and re-layouts  2.9 us (3%)
  between operations  0.94 us (1%)
    ppermute x8, starting transfers between devices, per_device(): near = [lax.ppermute(c, 'rcv', swaps(0)) for c in chunks]  19.1 us
    ppermute x7, starting transfers between devices, summed(): lax.ppermute(x, axis, [(d, d ^ bit * m) for d in range(count)])  12 us
    pallas_call x1, Pallas kernels, per_device(): pl.pallas_call(functools.partial(maps_kernel, n_src, shifts), out_shape=(...  10.2 us
    ppermute x7, waiting for transfers between devices, summed(): lax.ppermute(x, axis, [(d, d ^ bit * m) for d in range(count)])  6.97 us
    ppermute x8, starting transfers between devices, per_device(): far = [lax.ppermute(c, 'rcv', swaps(1)) for c in chunks]  6.73 us
    ppermute x3, starting transfers between devices, per_device(): bwd = lax.ppermute(bwd, 'src', behind)  6.18 us
    all_to_all x1, starting transfers between devices, per_device(): images = lax.all_to_all(images, 'src', 0, 0, tiled=True)  5.44 us
    all_to_all x1, starting transfers between devices, per_device(): field = lax.all_to_all(start, 'src', 0, 0, tiled=True)  5.3 us
  transfers between devices with their start and end apart: 32, of which 9 were waited for; matrix products, arithmetic and copies ran while one was open for 1% of the time, Pallas kernels for 0%

commit v1 on v0

--- a/solution.py
+++ b/solution.py
@@ -225,8 +225,8 @@
             bwd = lax.ppermute(bwd, "src", behind)
             chunks.append(bwd)
             shifts.append(step)
+    far = [lax.ppermute(c, "rcv", swaps(1)) for c in chunks]
     near = [lax.ppermute(c, "rcv", swaps(0)) for c in chunks]
-    far = [lax.ppermute(c, "rcv", swaps(1)) for c in chunks]
     any_spec = pl.BlockSpec(memory_space=pl.ANY)
     vmem = pl.BlockSpec(memory_space=pltpu.VMEM)
     band_cols = NEIGH * BLOCK

time: 86.1 us -> 86.1 us (level)
  no operation moved by 1% of the time
where the time goes in v1:
time: 86.1 us; the launch traced here: 85.5 us
  starting transfers between devices  57.3 us (67%)
  Pallas kernels  12.7 us (15%)
  waiting for transfers between devices  11.7 us (14%)
  local copies, waits for them, and re-layouts  2.9 us (3%)
  between operations  0.94 us (1%)
    ppermute x8, starting transfers between devices, per_device(): near = [lax.ppermute(c, 'rcv', swaps(0)) for c in chunks]  19.1 us
    ppermute x7, starting transfers between devices, summed(): lax.ppermute(x, axis, [(d, d ^ bit * m) for d in range(count)])  12 us
    pallas_call x1, Pallas kernels, per_device(): pl.pallas_call(functools.partial(maps_kernel, n_src, shifts), out_shape=(...  10.2 us
    ppermute x7, waiting for transfers between devices, summed(): lax.ppermute(x, axis, [(d, d ^ bit * m) for d in range(count)])  6.97 us
    ppermute x8, starting transfers between devices, per_device(): far = [lax.ppermute(c, 'rcv', swaps(1)) for c in chunks]  6.73 us
    ppermute x3, starting transfers between devices, per_device(): bwd = lax.ppermute(bwd, 'src', behind)  6.18 us
    all_to_all x1, starting transfers between devices, per_device(): images = lax.all_to_all(images, 'src', 0, 0, tiled=True)  5.44 us
    all_to_all x1, starting transfers between devices, per_device(): field = lax.all_to_all(start, 'src', 0, 0, tiled=True)  5.3 us
  transfers between devices with their start and end apart: 32, of which 9 were waited for; matrix products, arithmetic and copies ran while one was open for 1% of the time, Pallas kernels for 0%

profile of v1, /device:TPU:0, one launch (start us, length us, event | category | flops | bytes accessed | tf_op | source)
XLA Modules:
  0.0 85.5 jit_solution(12466213691619698218)
XLA Ops:
  1.7 3.0 %collective-permute-start.1 = (bf16[512,256]{1,0:T(8,128)(2,1)S(1)}, bf16[512,256]{1,0:T(8,128)(2,1)S(1)}, u32[]{:S(2)}, u32[]{:S(2)}) collective-permute-start(bf16[512,256]{1,0:T(8,128)(2,1)S(1)} %bitcast.12), channel_id=1, source_target_pairs={{2,0},{4,2},{6,4},{7,6},{5,7},{3,5},{1,3},{0,1},{10,8},{12,10},{14... | collective-permute-start | bytes 786440 | tf_op jit(solution)/shard_map/ppermute | solution.py:225
  5.5 3.3 %collective-permute-start.7 = (bf16[512,256]{1,0:T(8,128)(2,1)S(1)}, bf16[512,256]{1,0:T(8,128)(2,1)S(1)}, u32[]{:S(2)}, u32[]{:S(2)}) collective-permute-start(bf16[512,256]{1,0:T(8,128)(2,1)S(1)} %bitcast.15), channel_id=1, source_target_pairs={{0,8},{16,24},{8,0},{24,16},{1,9},{17,25},{9,1},{25,17},{2,10},{18... | collective-permute-start | bytes 786440 | tf_op jit(solution)/shard_map/ppermute | solution.py:229
  8.8 2.3 %collective-permute-done.1.refs_4_ = bf16[512,256]{1,0:T(8,128)(2,1)S(1)} collective-permute-done((bf16[512,256]{1,0:T(8,128)(2,1)S(1)}, bf16[512,256]{1,0:T(8,128)(2,1)S(1)}, u32[]{:S(2)}, u32[]{:S(2)}) %collective-permute-start.1) | collective-permute-done | bytes 262176 | tf_op jit(solution)/shard_map/ppermute | solution.py:225
  11.7 1.7 %collective-permute-start.3 = (bf16[512,256]{1,0:T(8,128)(2,1)S(1)}, bf16[512,256]{1,0:T(8,128)(2,1)S(1)}, u32[]{:S(2)}, u32[]{:S(2)}) collective-permute-start(bf16[512,256]{1,0:T(8,128)(2,1)S(1)} %collective-permute-done.1.refs_4_), channel_id=1, source_target_pairs={{2,0},{4,2},{6,4},{7,6},{5,7},{3,5},{1,3},{0,1},{10,8},{12,10},{14... | collective-permute-start | bytes 786440 | tf_op jit(solution)/shard_map/ppermute | solution.py:225
  13.8 2.5 %collective-permute-start.9 = (bf16[512,256]{1,0:T(8,128)(2,1)S(1)}, bf16[512,256]{1,0:T(8,128)(2,1)S(1)}, u32[]{:S(2)}, u32[]{:S(2)}) collective-permute-start(bf16[512,256]{1,0:T(8,128)(2,1)S(1)} %collective-permute-done.1.refs_4_), channel_id=1, source_target_pairs={{0,8},{16,24},{8,0},{24,16},{1,9},{17,25},{9,1},{25,17},{2,10},{18... | collective-permute-start | bytes 786440 | tf_op jit(solution)/shard_map/ppermute | solution.py:229
  17.0 2.1 %collective-permute-start.8 = (bf16[512,256]{1,0:T(8,128)(2,1)S(1)}, bf16[512,256]{1,0:T(8,128)(2,1)S(1)}, u32[]{:S(2)}, u32[]{:S(2)}) collective-permute-start(bf16[512,256]{1,0:T(8,128)(2,1)S(1)} %collective-permute-done.refs_3_), channel_id=1, source_target_pairs={{0,8},{16,24},{8,0},{24,16},{1,9},{17,25},{9,1},{25,17},{2,10},{18... | collective-permute-start | bytes 786440 | tf_op jit(solution)/shard_map/ppermute | solution.py:229
  21.5 1.5 %collective-permute-start.5 = (bf16[512,256]{1,0:T(8,128)(2,1)S(1)}, bf16[512,256]{1,0:T(8,128)(2,1)}, u32[]{:S(2)}, u32[]{:S(2)}) collective-permute-start(bf16[512,256]{1,0:T(8,128)(2,1)S(1)} %collective-permute-done.3.refs_6_), channel_id=1, source_target_pairs={{2,0},{4,2},{6,4},{7,6},{5,7},{3,5},{1,3},{0,1},{10,8},{12,10},{14... | collective-permute-start | bytes 786440 | tf_op jit(solution)/shard_map/ppermute | solution.py:225
  23.0 1.7 %collective-permute-start.11 = (bf16[512,256]{1,0:T(8,128)(2,1)S(1)}, bf16[512,256]{1,0:T(8,128)(2,1)}, u32[]{:S(2)}, u32[]{:S(2)}) collective-permute-start(bf16[512,256]{1,0:T(8,128)(2,1)S(1)} %collective-permute-done.3.refs_6_), channel_id=1, source_target_pairs={{0,8},{16,24},{8,0},{24,16},{1,9},{17,25},{9,1},{25,17},{2,10},{18... | collective-permute-start | bytes 786440 | tf_op jit(solution)/shard_map/ppermute | solution.py:229
  24.7 1.4 %collective-permute-start.18 = (bf16[512,256]{1,0:T(8,128)(2,1)S(1)}, bf16[512,256]{1,0:T(8,128)(2,1)}, u32[]{:S(2)}, u32[]{:S(2)}) collective-permute-start(bf16[512,256]{1,0:T(8,128)(2,1)S(1)} %collective-permute-done.2.refs_5_), channel_id=1, source_target_pairs={{8,16},{16,8},{9,17},{17,9},{10,18},{18,10},{11,19},{19,11},{12,20... | collective-permute-start | bytes 786440 | tf_op jit(solution)/shard_map/ppermute | solution.py:228
  26.1 2.9 %collective-permute-start.10 = (bf16[512,256]{1,0:T(8,128)(2,1)S(1)}, bf16[512,256]{1,0:T(8,128)(2,1)}, u32[]{:S(2)}, u32[]{:S(2)}) collective-permute-start(bf16[512,256]{1,0:T(8,128)(2,1)S(1)} %collective-permute-done.2.refs_5_), channel_id=1, source_target_pairs={{0,8},{16,24},{8,0},{24,16},{1,9},{17,25},{9,1},{25,17},{2,10},{18... | collective-permute-start | bytes 786440 | tf_op jit(solution)/shard_map/ppermute | solution.py:229
  29.0 1.5 %collective-permute-start.6 = (bf16[512,256]{1,0:T(8,128)(2,1)S(1)}, bf16[512,256]{1,0:T(8,128)(2,1)}, u32[]{:S(2)}, u32[]{:S(2)}) collective-permute-start(bf16[512,256]{1,0:T(8,128)(2,1)S(1)} %collective-permute-done.4.refs_7_), channel_id=1, source_target_pairs={{0,2},{2,4},{4,6},{6,7},{7,5},{5,3},{3,1},{1,0},{8,10},{10,12},{12... | collective-permute-start | bytes 786440 | tf_op jit(solution)/shard_map/ppermute | solution.py:221
  32.6 5.3 %all-to-all-start = ((bf16[8,64,256]{2,1,0:T(8,128)(2,1)}), bf16[8,64,256]{2,1,0:T(8,128)(2,1)S(1)}, u32[]{:S(2)}, u32[]{:S(2)}) async-start(bf16[8,64,256]{2,1,0:T(8,128)(2,1)} %bitcast.2.start), calls=%async_computation | async-start | bytes 524288 | tf_op jit(solution)/shard_map/all_to_all | solution.py:215
  37.9 2.3 %collective-permute-start.13 = (bf16[512,256]{1,0:T(8,128)(2,1)}, bf16[512,256]{1,0:T(8,128)(2,1)S(1)}, u32[]{:S(2)}, u32[]{:S(2)}) collective-permute-start(bf16[512,256]{1,0:T(8,128)(2,1)} %collective-permute-done.5.refs_8_), channel_id=1, source_target_pairs={{0,8},{16,24},{8,0},{24,16},{1,9},{17,25},{9,1},{25,17},{2,10},{18... | collective-permute-start | bytes 786440 | tf_op jit(solution)/shard_map/ppermute | solution.py:229
  40.9 2.1 %collective-permute-start.12 = (bf16[512,256]{1,0:T(8,128)(2,1)S(1)}, bf16[512,256]{1,0:T(8,128)(2,1)S(1)}, u32[]{:S(2)}, u32[]{:S(2)}) collective-permute-start(bf16[512,256]{1,0:T(8,128)(2,1)S(1)} %collective-permute-done.4.refs_7_), channel_id=1, source_target_pairs={{0,8},{16,24},{8,0},{24,16},{1,9},{17,25},{9,1},{25,17},{2,10},{18... | collective-permute-start | bytes 786440 | tf_op jit(solution)/shard_map/ppermute | solution.py:229
  43.7 2.3 %collective-permute-start.14 = (bf16[512,256]{1,0:T(8,128)(2,1)}, bf16[512,256]{1,0:T(8,128)(2,1)S(1)}, u32[]{:S(2)}, u32[]{:S(2)}) collective-permute-start(bf16[512,256]{1,0:T(8,128)(2,1)} %collective-permute-done.6.refs_9_), channel_id=1, source_target_pairs={{0,8},{16,24},{8,0},{24,16},{1,9},{17,25},{9,1},{25,17},{2,10},{18... | collective-permute-start | bytes 786440 | tf_op jit(solution)/shard_map/ppermute | solution.py:229
  48.4 10.2 %maps.1 = (f32[2,64,768]{2,1,0:T(8,128)}, f32[2,64,768]{2,1,0:T(8,128)}, bf16[8,144,256]{2,1,0:T(8,128)(2,1)}, f32[8,128]{1,0:T(8,128)}) custom-call(s32[2,3]{1,0:T(2,128)} %refs_0_.1, bf16[8,64,256]{2,1,0:T(8,128)(2,1)} %copy-done.3, bf16[512,256]{1,0:T(8,128)(2,1)} %bitcast.16, bf16[512,256]{1,0:T(8,128)(2,1)} %copy-done.5, bf16[512,256]{1,0:T(8,128)(2,1)} %copy-done.4, ...), custom_call_target="tpu_custom_call" | custom-call | tf_op jit(solution)/shard_map/maps/pallas_call | solution.py:233
  58.6 5.4 %all-to-all-start.1 = ((bf16[8,144,256]{2,1,0:T(8,128)(2,1)}), bf16[8,144,256]{2,1,0:T(8,128)(2,1)S(1)}, u32[]{:S(2)}, u32[]{:S(2)}) async-start(bf16[8,144,256]{2,1,0:T(8,128)(2,1)} %get-tuple-element.7), calls=%async_computation.1 | async-start | bytes 1179648 | tf_op jit(solution)/shard_map/all_to_all | solution.py:258
  65.0 5.1 %collective-permute-start.24 = (f32[8,128]{1,0:T(8,128)S(1)}, f32[8,128]{1,0:T(8,128)S(1)}, u32[]{:S(2)}, u32[]{:S(2)}) collective-permute-start(f32[8,128]{1,0:T(8,128)S(1)} %copy-done.22), channel_id=1, source_target_pairs={{0,16},{8,24},{16,0},{24,8},{1,17},{9,25},{17,1},{25,9},{2,18},{10... | collective-permute-start | bytes 12296 | tf_op jit(solution)/shard_map/ppermute | solution.py:194
  70.1 1.6 %collective-permute-done.24 = f32[8,128]{1,0:T(8,128)S(1)} collective-permute-done((f32[8,128]{1,0:T(8,128)S(1)}, f32[8,128]{1,0:T(8,128)S(1)}, u32[]{:S(2)}, u32[]{:S(2)}) %collective-permute-start.24) | collective-permute-done | bytes 4128 | tf_op jit(solution)/shard_map/ppermute | solution.py:194
  71.7 2.6 %collective-permute-start.28 = (f32[8,128]{1,0:T(8,128)S(1)}, f32[8,128]{1,0:T(8,128)S(1)}, u32[]{:S(2)}, u32[]{:S(2)}) collective-permute-start(f32[8,128]{1,0:T(8,128)S(1)} %add_add_fusion.1), channel_id=1, source_target_pairs={{0,3},{1,2},{2,1},{3,0},{4,7},{5,6},{6,5},{7,4},{8,11},{9,10},{10,... | collective-permute-start | bytes 12296 | tf_op jit(solution)/shard_map/ppermute | solution.py:194
  76.3 1.7 %collective-permute-done.27 = f32[8,128]{1,0:T(8,128)S(1)} collective-permute-done((f32[8,128]{1,0:T(8,128)S(1)}, f32[8,128]{1,0:T(8,128)S(1)}, u32[]{:S(2)}, u32[]{:S(2)}) %collective-permute-start.27) | collective-permute-done | bytes 4128 | tf_op jit(solution)/shard_map/ppermute | solution.py:194
  78.5 2.4 %collective-permute-start.29 = (f32[8,128]{1,0:T(8,128)S(1)}, f32[8,128]{1,0:T(8,128)S(1)}, u32[]{:S(2)}, u32[]{:S(2)}) collective-permute-start(f32[8,128]{1,0:T(8,128)S(1)} %add_add_fusion), channel_id=1, source_target_pairs={{0,4},{1,5},{2,6},{3,7},{4,0},{5,1},{6,2},{7,3},{8,12},{9,13},{10,... | collective-permute-start | bytes 12296 | tf_op jit(solution)/shard_map/ppermute | solution.py:194
  81.0 2.1 %collective-permute-done.29 = f32[8,128]{1,0:T(8,128)S(1)} collective-permute-done((f32[8,128]{1,0:T(8,128)S(1)}, f32[8,128]{1,0:T(8,128)S(1)}, u32[]{:S(2)}, u32[]{:S(2)}) %collective-permute-start.29) | collective-permute-done | bytes 4128 | tf_op jit(solution)/shard_map/ppermute | solution.py:194
  83.1 2.5 %combine.1 = (f32[32,2,3,2,256]{4,3,2,1,0:T(2,128)}, f32[512,2,128]{2,1,0:T(2,128)}) custom-call(f32[8,128]{1,0:T(8,128)S(1)} %add.27.sums, bf16[8,144,256]{2,1,0:T(8,128)(2,1)S(1)} %all-to-all-done.1.images, f32[2,64,768]{2,1,0:T(8,128)S(1)} %copy-done, f32[2,64,768]{2,1,0:T(8,128)S(1)} %copy-done.1, bf16[8,64,256]{2,1,0:T(8,128)(2,1)} %bitcast.2.start), custom_call_target="tpu_custom_call" | custom-call | tf_op jit(solution)/shard_map/combine/pallas_call | solution.py:261
  (94 shorter events, 15.3 us)
Async XLA Ops:
  1.7 9.4 %collective-permute-start.1 = (bf16[512,256]{1,0:T(8,128)(2,1)S(1)}, bf16[512,256]{1,0:T(8,128)(2,1)S(1)}, u32[]{:S(2)}, u32[]{:S(2)}) collective-permute-start(bf16[512,256]{1,0:T(8,128)(2,1)S(1)} %bitcast.12), channel_id=1, source_target_pairs={{2,0},{4,2},{6,4},{7,6},{5,7},{3,5},{1,3},{0,1},{10,8},{12,10},{14... | collective-permute-start | bytes 786440 | tf_op jit(solution)/shard_map/ppermute | solution.py:225
  4.7 8.8 %collective-permute-start = (bf16[512,256]{1,0:T(8,128)(2,1)S(1)}, bf16[512,256]{1,0:T(8,128)(2,1)S(1)}, u32[]{:S(2)}, u32[]{:S(2)}) collective-permute-start(bf16[512,256]{1,0:T(8,128)(2,1)S(1)} %bitcast.13), channel_id=1, source_target_pairs={{0,2},{2,4},{4,6},{6,7},{7,5},{5,3},{3,1},{1,0},{8,10},{10,12},{12... | collective-permute-start | bytes 786440 | tf_op jit(solution)/shard_map/ppermute | solution.py:221
  4.8 9.0 %collective-permute-start.15 = (bf16[512,256]{1,0:T(8,128)(2,1)S(1)}, bf16[512,256]{1,0:T(8,128)(2,1)S(1)}, u32[]{:S(2)}, u32[]{:S(2)}) collective-permute-start(bf16[512,256]{1,0:T(8,128)(2,1)S(1)} %bitcast.14), channel_id=1, source_target_pairs={{8,16},{16,8},{9,17},{17,9},{10,18},{18,10},{11,19},{19,11},{12,20... | collective-permute-start | bytes 786440 | tf_op jit(solution)/shard_map/ppermute | solution.py:228
  5.5 10.8 %collective-permute-start.7 = (bf16[512,256]{1,0:T(8,128)(2,1)S(1)}, bf16[512,256]{1,0:T(8,128)(2,1)S(1)}, u32[]{:S(2)}, u32[]{:S(2)}) collective-permute-start(bf16[512,256]{1,0:T(8,128)(2,1)S(1)} %bitcast.15), channel_id=1, source_target_pairs={{0,8},{16,24},{8,0},{24,16},{1,9},{17,25},{9,1},{25,17},{2,10},{18... | collective-permute-start | bytes 786440 | tf_op jit(solution)/shard_map/ppermute | solution.py:229
  11.1 5.9 %collective-permute-start.17 = (bf16[512,256]{1,0:T(8,128)(2,1)S(1)}, bf16[512,256]{1,0:T(8,128)(2,1)S(1)}, u32[]{:S(2)}, u32[]{:S(2)}) collective-permute-start(bf16[512,256]{1,0:T(8,128)(2,1)S(1)} %collective-permute-done.1.refs_4_), channel_id=1, source_target_pairs={{8,16},{16,8},{9,17},{17,9},{10,18},{18,10},{11,19},{19,11},{12,20... | collective-permute-start | bytes 786440 | tf_op jit(solution)/shard_map/ppermute | solution.py:228
  11.7 7.4 %collective-permute-start.3 = (bf16[512,256]{1,0:T(8,128)(2,1)S(1)}, bf16[512,256]{1,0:T(8,128)(2,1)S(1)}, u32[]{:S(2)}, u32[]{:S(2)}) collective-permute-start(bf16[512,256]{1,0:T(8,128)(2,1)S(1)} %collective-permute-done.1.refs_4_), channel_id=1, source_target_pairs={{2,0},{4,2},{6,4},{7,6},{5,7},{3,5},{1,3},{0,1},{10,8},{12,10},{14... | collective-permute-start | bytes 786440 | tf_op jit(solution)/shard_map/ppermute | solution.py:225
  13.5 7.5 %collective-permute-start.2 = (bf16[512,256]{1,0:T(8,128)(2,1)S(1)}, bf16[512,256]{1,0:T(8,128)(2,1)S(1)}, u32[]{:S(2)}, u32[]{:S(2)}) collective-permute-start(bf16[512,256]{1,0:T(8,128)(2,1)S(1)} %collective-permute-done.refs_3_), channel_id=1, source_target_pairs={{0,2},{2,4},{4,6},{6,7},{7,5},{5,3},{3,1},{1,0},{8,10},{10,12},{12... | collective-permute-start | bytes 786440 | tf_op jit(solution)/shard_map/ppermute | solution.py:221
  13.8 7.7 %collective-permute-start.9 = (bf16[512,256]{1,0:T(8,128)(2,1)S(1)}, bf16[512,256]{1,0:T(8,128)(2,1)S(1)}, u32[]{:S(2)}, u32[]{:S(2)}) collective-permute-start(bf16[512,256]{1,0:T(8,128)(2,1)S(1)} %collective-permute-done.1.refs_4_), channel_id=1, source_target_pairs={{0,8},{16,24},{8,0},{24,16},{1,9},{17,25},{9,1},{25,17},{2,10},{18... | collective-permute-start | bytes 786440 | tf_op jit(solution)/shard_map/ppermute | solution.py:229
  16.3 6.7 %collective-permute-start.16 = (bf16[512,256]{1,0:T(8,128)(2,1)S(1)}, bf16[512,256]{1,0:T(8,128)(2,1)S(1)}, u32[]{:S(2)}, u32[]{:S(2)}) collective-permute-start(bf16[512,256]{1,0:T(8,128)(2,1)S(1)} %collective-permute-done.refs_3_), channel_id=1, source_target_pairs={{8,16},{16,8},{9,17},{17,9},{10,18},{18,10},{11,19},{19,11},{12,20... | collective-permute-start | bytes 786440 | tf_op jit(solution)/shard_map/ppermute | solution.py:228
  17.0 7.7 %collective-permute-start.8 = (bf16[512,256]{1,0:T(8,128)(2,1)S(1)}, bf16[512,256]{1,0:T(8,128)(2,1)S(1)}, u32[]{:S(2)}, u32[]{:S(2)}) collective-permute-start(bf16[512,256]{1,0:T(8,128)(2,1)S(1)} %collective-permute-done.refs_3_), channel_id=1, source_target_pairs={{0,8},{16,24},{8,0},{24,16},{1,9},{17,25},{9,1},{25,17},{2,10},{18... | collective-permute-start | bytes 786440 | tf_op jit(solution)/shard_map/ppermute | solution.py:229
  19.1 6.9 %collective-permute-start.19 = (bf16[512,256]{1,0:T(8,128)(2,1)S(1)}, bf16[512,256]{1,0:T(8,128)(2,1)S(1)}, u32[]{:S(2)}, u32[]{:S(2)}) collective-permute-start(bf16[512,256]{1,0:T(8,128)(2,1)S(1)} %collective-permute-done.3.refs_6_), channel_id=1, source_target_pairs={{8,16},{16,8},{9,17},{17,9},{10,18},{18,10},{11,19},{19,11},{12,20... | collective-permute-start | bytes 786440 | tf_op jit(solution)/shard_map/ppermute | solution.py:228
  21.0 8.0 %collective-permute-start.4 = (bf16[512,256]{1,0:T(8,128)(2,1)S(1)}, bf16[512,256]{1,0:T(8,128)(2,1)S(1)}, u32[]{:S(2)}, u32[]{:S(2)}) collective-permute-start(bf16[512,256]{1,0:T(8,128)(2,1)S(1)} %collective-permute-done.2.refs_5_), channel_id=1, source_target_pairs={{0,2},{2,4},{4,6},{6,7},{7,5},{5,3},{3,1},{1,0},{8,10},{10,12},{12... | collective-permute-start | bytes 786440 | tf_op jit(solution)/shard_map/ppermute | solution.py:221
  21.5 8.9 %collective-permute-start.5 = (bf16[512,256]{1,0:T(8,128)(2,1)S(1)}, bf16[512,256]{1,0:T(8,128)(2,1)}, u32[]{:S(2)}, u32[]{:S(2)}) collective-permute-start(bf16[512,256]{1,0:T(8,128)(2,1)S(1)} %collective-permute-done.3.refs_6_), channel_id=1, source_target_pairs={{2,0},{4,2},{6,4},{7,6},{5,7},{3,5},{1,3},{0,1},{10,8},{12,10},{14... | collective-permute-start | bytes 786440 | tf_op jit(solution)/shard_map/ppermute | solution.py:225
  23.0 14.9 %collective-permute-start.11 = (bf16[512,256]{1,0:T(8,128)(2,1)S(1)}, bf16[512,256]{1,0:T(8,128)(2,1)}, u32[]{:S(2)}, u32[]{:S(2)}) collective-permute-start(bf16[512,256]{1,0:T(8,128)(2,1)S(1)} %collective-permute-done.3.refs_6_), channel_id=1, source_target_pairs={{0,8},{16,24},{8,0},{24,16},{1,9},{17,25},{9,1},{25,17},{2,10},{18... | collective-permute-start | bytes 786440 | tf_op jit(solution)/shard_map/ppermute | solution.py:229
  24.7 15.5 %collective-permute-start.18 = (bf16[512,256]{1,0:T(8,128)(2,1)S(1)}, bf16[512,256]{1,0:T(8,128)(2,1)}, u32[]{:S(2)}, u32[]{:S(2)}) collective-permute-start(bf16[512,256]{1,0:T(8,128)(2,1)S(1)} %collective-permute-done.2.refs_5_), channel_id=1, source_target_pairs={{8,16},{16,8},{9,17},{17,9},{10,18},{18,10},{11,19},{19,11},{12,20... | collective-permute-start | bytes 786440 | tf_op jit(solution)/shard_map/ppermute | solution.py:228
  26.1 14.8 %collective-permute-start.10 = (bf16[512,256]{1,0:T(8,128)(2,1)S(1)}, bf16[512,256]{1,0:T(8,128)(2,1)}, u32[]{:S(2)}, u32[]{:S(2)}) collective-permute-start(bf16[512,256]{1,0:T(8,128)(2,1)S(1)} %collective-permute-done.2.refs_5_), channel_id=1, source_target_pairs={{0,8},{16,24},{8,0},{24,16},{1,9},{17,25},{9,1},{25,17},{2,10},{18... | collective-permute-start | bytes 786440 | tf_op jit(solution)/shard_map/ppermute | solution.py:229
  29.0 14.1 %collective-permute-start.6 = (bf16[512,256]{1,0:T(8,128)(2,1)S(1)}, bf16[512,256]{1,0:T(8,128)(2,1)}, u32[]{:S(2)}, u32[]{:S(2)}) collective-permute-start(bf16[512,256]{1,0:T(8,128)(2,1)S(1)} %collective-permute-done.4.refs_7_), channel_id=1, source_target_pairs={{0,2},{2,4},{4,6},{6,7},{7,5},{5,3},{3,1},{1,0},{8,10},{10,12},{12... | collective-permute-start | bytes 786440 | tf_op jit(solution)/shard_map/ppermute | solution.py:221
  30.4 13.3 %collective-permute-start.21 = (bf16[512,256]{1,0:T(8,128)(2,1)}, bf16[512,256]{1,0:T(8,128)(2,1)}, u32[]{:S(2)}, u32[]{:S(2)}) collective-permute-start(bf16[512,256]{1,0:T(8,128)(2,1)} %collective-permute-done.5.refs_8_), channel_id=1, source_target_pairs={{8,16},{16,8},{9,17},{17,9},{10,18},{18,10},{11,19},{19,11},{12,20... | collective-permute-start | bytes 786440 | tf_op jit(solution)/shard_map/ppermute | solution.py:228
  32.6 14.0 %all-to-all-start = ((bf16[8,64,256]{2,1,0:T(8,128)(2,1)}), bf16[8,64,256]{2,1,0:T(8,128)(2,1)S(1)}, u32[]{:S(2)}, u32[]{:S(2)}) async-start(bf16[8,64,256]{2,1,0:T(8,128)(2,1)} %bitcast.2.start), calls=%async_computation | async-start | bytes 524288 | tf_op jit(solution)/shard_map/all_to_all | solution.py:215
  37.9 8.7 %collective-permute-start.13 = (bf16[512,256]{1,0:T(8,128)(2,1)}, bf16[512,256]{1,0:T(8,128)(2,1)S(1)}, u32[]{:S(2)}, u32[]{:S(2)}) collective-permute-start(bf16[512,256]{1,0:T(8,128)(2,1)} %collective-permute-done.5.refs_8_), channel_id=1, source_target_pairs={{0,8},{16,24},{8,0},{24,16},{1,9},{17,25},{9,1},{25,17},{2,10},{18... | collective-permute-start | bytes 786440 | tf_op jit(solution)/shard_map/ppermute | solution.py:229
  40.2 6.5 %collective-permute-start.20 = (bf16[512,256]{1,0:T(8,128)(2,1)S(1)}, bf16[512,256]{1,0:T(8,128)(2,1)S(1)}, u32[]{:S(2)}, u32[]{:S(2)}) collective-permute-start(bf16[512,256]{1,0:T(8,128)(2,1)S(1)} %collective-permute-done.4.refs_7_), channel_id=1, source_target_pairs={{8,16},{16,8},{9,17},{17,9},{10,18},{18,10},{11,19},{19,11},{12,20... | collective-permute-start | bytes 786440 | tf_op jit(solution)/shard_map/ppermute | solution.py:228
  58.6 24.4 %all-to-all-start.1 = ((bf16[8,144,256]{2,1,0:T(8,128)(2,1)}), bf16[8,144,256]{2,1,0:T(8,128)(2,1)S(1)}, u32[]{:S(2)}, u32[]{:S(2)}) async-start(bf16[8,144,256]{2,1,0:T(8,128)(2,1)} %get-tuple-element.7), calls=%async_computation.1 | async-start | bytes 1179648 | tf_op jit(solution)/shard_map/all_to_all | solution.py:258
  64.1 6.0 %collective-permute-start.25 = (f32[8,128]{1,0:T(8,128)S(1)}, f32[8,128]{1,0:T(8,128)S(1)}, u32[]{:S(2)}, u32[]{:S(2)}) collective-permute-start(f32[8,128]{1,0:T(8,128)S(1)} %copy-done.22), channel_id=1, source_target_pairs={{0,24},{8,16},{16,8},{24,0},{1,25},{9,17},{17,9},{25,1},{2,26},{10... | collective-permute-start | bytes 12296 | tf_op jit(solution)/shard_map/ppermute | solution.py:194
  65.0 6.7 %collective-permute-start.24 = (f32[8,128]{1,0:T(8,128)S(1)}, f32[8,128]{1,0:T(8,128)S(1)}, u32[]{:S(2)}, u32[]{:S(2)}) collective-permute-start(f32[8,128]{1,0:T(8,128)S(1)} %copy-done.22), channel_id=1, source_target_pairs={{0,16},{8,24},{16,0},{24,8},{1,17},{9,25},{17,1},{25,9},{2,18},{10... | collective-permute-start | bytes 12296 | tf_op jit(solution)/shard_map/ppermute | solution.py:194
  (31 other events, 314.2 us)

commit v2 on v0

--- a/solution.py
+++ b/solution.py
@@ -227,6 +227,7 @@
             shifts.append(step)
     near = [lax.ppermute(c, "rcv", swaps(0)) for c in chunks]
     far = [lax.ppermute(c, "rcv", swaps(1)) for c in chunks]
+    near[-1], far[-1] = [pltpu.with_memory_space_constraint(x, pltpu.VMEM) for x in (near[-1], far[-1])]
     any_spec = pl.BlockSpec(memory_space=pl.ANY)
     vmem = pl.BlockSpec(memory_space=pltpu.VMEM)
     band_cols = NEIGH * BLOCK
@@ -238,7 +239,7 @@
             jax.ShapeDtypeStruct((n_src, 2 * blocks_here * rows + SHARE_ROWS, cols), jnp.bfloat16),
             jax.ShapeDtypeStruct((8, 128), jnp.float32),
         ),
-        in_specs=[any_spec, vmem] + [any_spec] * (3 * n_src),
+        in_specs=[any_spec, vmem] + [any_spec] * n_src + 2 * ([any_spec] * (n_src - 1) + [vmem]),
         out_specs=[vmem] * 4,
         scratch_shapes=[
             pltpu.SMEM(band.shape, jnp.int32),

time: 86.1 us -> 84.9 us (0.986)
    unnamed x48 -> x46, local copies, waits for them, and re-layouts: 2.19 us -> 1.44 us
where the time goes in v2:
time: 84.9 us; the launch traced here: 84.3 us
  starting transfers between devices  56.8 us (67%)
  Pallas kernels  12.7 us (15%)
  waiting for transfers between devices  11.8 us (14%)
  local copies, waits for them, and re-layouts  2.17 us (3%)
  between operations  0.95 us (1%)
    ppermute x8, starting transfers between devices, per_device(): near = [lax.ppermute(c, 'rcv', swaps(0)) for c in chunks]  19.9 us
    ppermute x7, starting transfers between devices, summed(): lax.ppermute(x, axis, [(d, d ^ bit * m) for d in range(count)])  11.3 us
    pallas_call x1, Pallas kernels, per_device(): pl.pallas_call(functools.partial(maps_kernel, n_src, shifts), out_shape=(...  10.2 us
    ppermute x7, waiting for transfers between devices, summed(): lax.ppermute(x, axis, [(d, d ^ bit * m) for d in range(count)])  6.97 us
    ppermute x3, starting transfers between devices, per_device(): bwd = lax.ppermute(bwd, 'src', behind)  6.18 us
    ppermute x8, starting transfers between devices, per_device(): far = [lax.ppermute(c, 'rcv', swaps(1)) for c in chunks]  6.03 us
    all_to_all x1, starting transfers between devices, per_device(): images = lax.all_to_all(images, 'src', 0, 0, tiled=True)  5.62 us
    all_to_all x1, starting transfers between devices, per_device(): field = lax.all_to_all(start, 'src', 0, 0, tiled=True)  5.31 us
  transfers between devices with their start and end apart: 32, of which 9 were waited for; matrix products, arithmetic and copies ran while one was open for 1% of the time, Pallas kernels for 0%

profile of v2, /device:TPU:0, one launch (start us, length us, event | category | flops | bytes accessed | tf_op | source)
XLA Modules:
  0.0 84.3 jit_solution(7051152139516390963)
XLA Ops:
  1.7 3.0 %collective-permute-start.1 = (bf16[512,256]{1,0:T(8,128)(2,1)S(1)}, bf16[512,256]{1,0:T(8,128)(2,1)S(1)}, u32[]{:S(2)}, u32[]{:S(2)}) collective-permute-start(bf16[512,256]{1,0:T(8,128)(2,1)S(1)} %bitcast.12), channel_id=1, source_target_pairs={{2,0},{4,2},{6,4},{7,6},{5,7},{3,5},{1,3},{0,1},{10,8},{12,10},{14... | collective-permute-start | bytes 786440 | tf_op jit(solution)/shard_map/ppermute | solution.py:225
  5.5 3.3 %collective-permute-start.7 = (bf16[512,256]{1,0:T(8,128)(2,1)S(1)}, bf16[512,256]{1,0:T(8,128)(2,1)S(1)}, u32[]{:S(2)}, u32[]{:S(2)}) collective-permute-start(bf16[512,256]{1,0:T(8,128)(2,1)S(1)} %bitcast.15), channel_id=1, source_target_pairs={{0,8},{16,24},{8,0},{24,16},{1,9},{17,25},{9,1},{25,17},{2,10},{18... | collective-permute-start | bytes 786440 | tf_op jit(solution)/shard_map/ppermute | solution.py:228
  8.8 2.3 %collective-permute-done.1.refs_4_ = bf16[512,256]{1,0:T(8,128)(2,1)S(1)} collective-permute-done((bf16[512,256]{1,0:T(8,128)(2,1)S(1)}, bf16[512,256]{1,0:T(8,128)(2,1)S(1)}, u32[]{:S(2)}, u32[]{:S(2)}) %collective-permute-start.1) | collective-permute-done | bytes 262176 | tf_op jit(solution)/shard_map/ppermute | solution.py:225
  11.7 1.7 %collective-permute-start.3 = (bf16[512,256]{1,0:T(8,128)(2,1)S(1)}, bf16[512,256]{1,0:T(8,128)(2,1)S(1)}, u32[]{:S(2)}, u32[]{:S(2)}) collective-permute-start(bf16[512,256]{1,0:T(8,128)(2,1)S(1)} %collective-permute-done.1.refs_4_), channel_id=1, source_target_pairs={{2,0},{4,2},{6,4},{7,6},{5,7},{3,5},{1,3},{0,1},{10,8},{12,10},{14... | collective-permute-start | bytes 786440 | tf_op jit(solution)/shard_map/ppermute | solution.py:225
  13.8 2.5 %collective-permute-start.9 = (bf16[512,256]{1,0:T(8,128)(2,1)S(1)}, bf16[512,256]{1,0:T(8,128)(2,1)S(1)}, u32[]{:S(2)}, u32[]{:S(2)}) collective-permute-start(bf16[512,256]{1,0:T(8,128)(2,1)S(1)} %collective-permute-done.1.refs_4_), channel_id=1, source_target_pairs={{0,8},{16,24},{8,0},{24,16},{1,9},{17,25},{9,1},{25,17},{2,10},{18... | collective-permute-start | bytes 786440 | tf_op jit(solution)/shard_map/ppermute | solution.py:228
  17.0 2.1 %collective-permute-start.8 = (bf16[512,256]{1,0:T(8,128)(2,1)S(1)}, bf16[512,256]{1,0:T(8,128)(2,1)S(1)}, u32[]{:S(2)}, u32[]{:S(2)}) collective-permute-start(bf16[512,256]{1,0:T(8,128)(2,1)S(1)} %collective-permute-done.refs_3_), channel_id=1, source_target_pairs={{0,8},{16,24},{8,0},{24,16},{1,9},{17,25},{9,1},{25,17},{2,10},{18... | collective-permute-start | bytes 786440 | tf_op jit(solution)/shard_map/ppermute | solution.py:228
  21.5 1.5 %collective-permute-start.5 = (bf16[512,256]{1,0:T(8,128)(2,1)S(1)}, bf16[512,256]{1,0:T(8,128)(2,1)}, u32[]{:S(2)}, u32[]{:S(2)}) collective-permute-start(bf16[512,256]{1,0:T(8,128)(2,1)S(1)} %collective-permute-done.3.refs_6_), channel_id=1, source_target_pairs={{2,0},{4,2},{6,4},{7,6},{5,7},{3,5},{1,3},{0,1},{10,8},{12,10},{14... | collective-permute-start | bytes 786440 | tf_op jit(solution)/shard_map/ppermute | solution.py:225
  23.0 1.7 %collective-permute-start.11 = (bf16[512,256]{1,0:T(8,128)(2,1)S(1)}, bf16[512,256]{1,0:T(8,128)(2,1)S(1)}, u32[]{:S(2)}, u32[]{:S(2)}) collective-permute-start(bf16[512,256]{1,0:T(8,128)(2,1)S(1)} %collective-permute-done.3.refs_6_), channel_id=1, source_target_pairs={{0,8},{16,24},{8,0},{24,16},{1,9},{17,25},{9,1},{25,17},{2,10},{18... | collective-permute-start | bytes 786440 | tf_op jit(solution)/shard_map/ppermute | solution.py:228
  25.4 3.7 %collective-permute-start.10 = (bf16[512,256]{1,0:T(8,128)(2,1)S(1)}, bf16[512,256]{1,0:T(8,128)(2,1)}, u32[]{:S(2)}, u32[]{:S(2)}) collective-permute-start(bf16[512,256]{1,0:T(8,128)(2,1)S(1)} %collective-permute-done.2.refs_5_), channel_id=1, source_target_pairs={{0,8},{16,24},{8,0},{24,16},{1,9},{17,25},{9,1},{25,17},{2,10},{18... | collective-permute-start | bytes 786440 | tf_op jit(solution)/shard_map/ppermute | solution.py:228
  29.1 1.3 %collective-permute-start.6 = (bf16[512,256]{1,0:T(8,128)(2,1)}, bf16[512,256]{1,0:T(8,128)(2,1)}, u32[]{:S(2)}, u32[]{:S(2)}) collective-permute-start(bf16[512,256]{1,0:T(8,128)(2,1)} %collective-permute-done.4.refs_7_), channel_id=1, source_target_pairs={{0,2},{2,4},{4,6},{6,7},{7,5},{5,3},{3,1},{1,0},{8,10},{10,12},{12... | collective-permute-start | bytes 786440 | tf_op jit(solution)/shard_map/ppermute | solution.py:221
  30.4 1.4 %collective-permute-start.21 = (bf16[512,256]{1,0:T(8,128)(2,1)}, bf16[512,256]{1,0:T(8,128)(2,1)}, u32[]{:S(2)}, u32[]{:S(2)}) collective-permute-start(bf16[512,256]{1,0:T(8,128)(2,1)} %collective-permute-done.5.refs_8_), channel_id=1, source_target_pairs={{8,16},{16,8},{9,17},{17,9},{10,18},{18,10},{11,19},{19,11},{12,20... | collective-permute-start | bytes 786440 | tf_op jit(solution)/shard_map/ppermute | solution.py:229
  32.6 5.3 %all-to-all-start = ((bf16[8,64,256]{2,1,0:T(8,128)(2,1)}), bf16[8,64,256]{2,1,0:T(8,128)(2,1)S(1)}, u32[]{:S(2)}, u32[]{:S(2)}) async-start(bf16[8,64,256]{2,1,0:T(8,128)(2,1)} %bitcast.2.start), calls=%async_computation | async-start | bytes 524288 | tf_op jit(solution)/shard_map/all_to_all | solution.py:215
  37.9 2.3 %collective-permute-start.13 = (bf16[512,256]{1,0:T(8,128)(2,1)}, bf16[512,256]{1,0:T(8,128)(2,1)S(1)}, u32[]{:S(2)}, u32[]{:S(2)}) collective-permute-start(bf16[512,256]{1,0:T(8,128)(2,1)} %collective-permute-done.5.refs_8_), channel_id=1, source_target_pairs={{0,8},{16,24},{8,0},{24,16},{1,9},{17,25},{9,1},{25,17},{2,10},{18... | collective-permute-start | bytes 786440 | tf_op jit(solution)/shard_map/ppermute | solution.py:228
  40.9 2.2 %collective-permute-start.12 = (bf16[512,256]{1,0:T(8,128)(2,1)}, bf16[512,256]{1,0:T(8,128)(2,1)S(1)}, u32[]{:S(2)}, u32[]{:S(2)}) collective-permute-start(bf16[512,256]{1,0:T(8,128)(2,1)} %collective-permute-done.4.refs_7_), channel_id=1, source_target_pairs={{0,8},{16,24},{8,0},{24,16},{1,9},{17,25},{9,1},{25,17},{2,10},{18... | collective-permute-start | bytes 786440 | tf_op jit(solution)/shard_map/ppermute | solution.py:228
  43.7 2.3 %collective-permute-start.14 = (bf16[512,256]{1,0:T(8,128)(2,1)}, bf16[512,256]{1,0:T(8,128)(2,1)S(1)}, u32[]{:S(2)}, u32[]{:S(2)}) collective-permute-start(bf16[512,256]{1,0:T(8,128)(2,1)} %collective-permute-done.6.refs_9_), channel_id=1, source_target_pairs={{0,8},{16,24},{8,0},{24,16},{1,9},{17,25},{9,1},{25,17},{2,10},{18... | collective-permute-start | bytes 786440 | tf_op jit(solution)/shard_map/ppermute | solution.py:228
  47.7 10.2 %maps.1 = (f32[2,64,768]{2,1,0:T(8,128)}, f32[2,64,768]{2,1,0:T(8,128)}, bf16[8,144,256]{2,1,0:T(8,128)(2,1)}, f32[8,128]{1,0:T(8,128)}) custom-call(s32[2,3]{1,0:T(2,128)} %refs_0_.1, bf16[8,64,256]{2,1,0:T(8,128)(2,1)} %copy-done.3, bf16[512,256]{1,0:T(8,128)(2,1)} %bitcast.16, bf16[512,256]{1,0:T(8,128)(2,1)} %copy-done.5, bf16[512,256]{1,0:T(8,128)(2,1)} %copy-done.4, ...), custom_call_target="tpu_custom_call" | custom-call | tf_op jit(solution)/shard_map/maps/pallas_call | solution.py:234
  57.9 5.6 %all-to-all-start.1 = ((bf16[8,144,256]{2,1,0:T(8,128)(2,1)}), bf16[8,144,256]{2,1,0:T(8,128)(2,1)S(1)}, u32[]{:S(2)}, u32[]{:S(2)}) async-start(bf16[8,144,256]{2,1,0:T(8,128)(2,1)} %get-tuple-element.7), calls=%async_computation.1 | async-start | bytes 1179648 | tf_op jit(solution)/shard_map/all_to_all | solution.py:259
  64.4 4.4 %collective-permute-start.24 = (f32[8,128]{1,0:T(8,128)S(1)}, f32[8,128]{1,0:T(8,128)S(1)}, u32[]{:S(2)}, u32[]{:S(2)}) collective-permute-start(f32[8,128]{1,0:T(8,128)S(1)} %copy-done.21), channel_id=1, source_target_pairs={{0,16},{8,24},{16,0},{24,8},{1,17},{9,25},{17,1},{25,9},{2,18},{10... | collective-permute-start | bytes 12296 | tf_op jit(solution)/shard_map/ppermute | solution.py:194
  68.9 1.6 %collective-permute-done.24 = f32[8,128]{1,0:T(8,128)S(1)} collective-permute-done((f32[8,128]{1,0:T(8,128)S(1)}, f32[8,128]{1,0:T(8,128)S(1)}, u32[]{:S(2)}, u32[]{:S(2)}) %collective-permute-start.24) | collective-permute-done | bytes 4128 | tf_op jit(solution)/shard_map/ppermute | solution.py:194
  70.5 2.6 %collective-permute-start.28 = (f32[8,128]{1,0:T(8,128)S(1)}, f32[8,128]{1,0:T(8,128)S(1)}, u32[]{:S(2)}, u32[]{:S(2)}) collective-permute-start(f32[8,128]{1,0:T(8,128)S(1)} %add_add_fusion.1), channel_id=1, source_target_pairs={{0,3},{1,2},{2,1},{3,0},{4,7},{5,6},{6,5},{7,4},{8,11},{9,10},{10,... | collective-permute-start | bytes 12296 | tf_op jit(solution)/shard_map/ppermute | solution.py:194
  75.3 1.8 %collective-permute-done.27 = f32[8,128]{1,0:T(8,128)S(1)} collective-permute-done((f32[8,128]{1,0:T(8,128)S(1)}, f32[8,128]{1,0:T(8,128)S(1)}, u32[]{:S(2)}, u32[]{:S(2)}) %collective-permute-start.27) | collective-permute-done | bytes 4128 | tf_op jit(solution)/shard_map/ppermute | solution.py:194
  77.3 2.4 %collective-permute-start.29 = (f32[8,128]{1,0:T(8,128)S(1)}, f32[8,128]{1,0:T(8,128)S(1)}, u32[]{:S(2)}, u32[]{:S(2)}) collective-permute-start(f32[8,128]{1,0:T(8,128)S(1)} %add_add_fusion), channel_id=1, source_target_pairs={{0,4},{1,5},{2,6},{3,7},{4,0},{5,1},{6,2},{7,3},{8,12},{9,13},{10,... | collective-permute-start | bytes 12296 | tf_op jit(solution)/shard_map/ppermute | solution.py:194
  79.8 2.1 %collective-permute-done.29 = f32[8,128]{1,0:T(8,128)S(1)} collective-permute-done((f32[8,128]{1,0:T(8,128)S(1)}, f32[8,128]{1,0:T(8,128)S(1)}, u32[]{:S(2)}, u32[]{:S(2)}) %collective-permute-start.29) | collective-permute-done | bytes 4128 | tf_op jit(solution)/shard_map/ppermute | solution.py:194
  81.9 2.5 %combine.1 = (f32[32,2,3,2,256]{4,3,2,1,0:T(2,128)}, f32[512,2,128]{2,1,0:T(2,128)}) custom-call(f32[8,128]{1,0:T(8,128)S(1)} %add.27.sums, bf16[8,144,256]{2,1,0:T(8,128)(2,1)S(1)} %all-to-all-done.1.images, f32[2,64,768]{2,1,0:T(8,128)S(1)} %copy-done, f32[2,64,768]{2,1,0:T(8,128)S(1)} %copy-done.1, bf16[8,64,256]{2,1,0:T(8,128)(2,1)} %bitcast.2.start), custom_call_target="tpu_custom_call" | custom-call | tf_op jit(solution)/shard_map/combine/pallas_call | solution.py:262
  (92 shorter events, 13.7 us)
Async XLA Ops:
  1.7 9.4 %collective-permute-start.1 = (bf16[512,256]{1,0:T(8,128)(2,1)S(1)}, bf16[512,256]{1,0:T(8,128)(2,1)S(1)}, u32[]{:S(2)}, u32[]{:S(2)}) collective-permute-start(bf16[512,256]{1,0:T(8,128)(2,1)S(1)} %bitcast.12), channel_id=1, source_target_pairs={{2,0},{4,2},{6,4},{7,6},{5,7},{3,5},{1,3},{0,1},{10,8},{12,10},{14... | collective-permute-start | bytes 786440 | tf_op jit(solution)/shard_map/ppermute | solution.py:225
  4.7 8.8 %collective-permute-start = (bf16[512,256]{1,0:T(8,128)(2,1)S(1)}, bf16[512,256]{1,0:T(8,128)(2,1)S(1)}, u32[]{:S(2)}, u32[]{:S(2)}) collective-permute-start(bf16[512,256]{1,0:T(8,128)(2,1)S(1)} %bitcast.13), channel_id=1, source_target_pairs={{0,2},{2,4},{4,6},{6,7},{7,5},{5,3},{3,1},{1,0},{8,10},{10,12},{12... | collective-permute-start | bytes 786440 | tf_op jit(solution)/shard_map/ppermute | solution.py:221
  4.8 9.0 %collective-permute-start.15 = (bf16[512,256]{1,0:T(8,128)(2,1)S(1)}, bf16[512,256]{1,0:T(8,128)(2,1)S(1)}, u32[]{:S(2)}, u32[]{:S(2)}) collective-permute-start(bf16[512,256]{1,0:T(8,128)(2,1)S(1)} %bitcast.14), channel_id=1, source_target_pairs={{8,16},{16,8},{9,17},{17,9},{10,18},{18,10},{11,19},{19,11},{12,20... | collective-permute-start | bytes 786440 | tf_op jit(solution)/shard_map/ppermute | solution.py:229
  5.5 10.8 %collective-permute-start.7 = (bf16[512,256]{1,0:T(8,128)(2,1)S(1)}, bf16[512,256]{1,0:T(8,128)(2,1)S(1)}, u32[]{:S(2)}, u32[]{:S(2)}) collective-permute-start(bf16[512,256]{1,0:T(8,128)(2,1)S(1)} %bitcast.15), channel_id=1, source_target_pairs={{0,8},{16,24},{8,0},{24,16},{1,9},{17,25},{9,1},{25,17},{2,10},{18... | collective-permute-start | bytes 786440 | tf_op jit(solution)/shard_map/ppermute | solution.py:228
  11.1 5.9 %collective-permute-start.17 = (bf16[512,256]{1,0:T(8,128)(2,1)S(1)}, bf16[512,256]{1,0:T(8,128)(2,1)S(1)}, u32[]{:S(2)}, u32[]{:S(2)}) collective-permute-start(bf16[512,256]{1,0:T(8,128)(2,1)S(1)} %collective-permute-done.1.refs_4_), channel_id=1, source_target_pairs={{8,16},{16,8},{9,17},{17,9},{10,18},{18,10},{11,19},{19,11},{12,20... | collective-permute-start | bytes 786440 | tf_op jit(solution)/shard_map/ppermute | solution.py:229
  11.7 7.4 %collective-permute-start.3 = (bf16[512,256]{1,0:T(8,128)(2,1)S(1)}, bf16[512,256]{1,0:T(8,128)(2,1)S(1)}, u32[]{:S(2)}, u32[]{:S(2)}) collective-permute-start(bf16[512,256]{1,0:T(8,128)(2,1)S(1)} %collective-permute-done.1.refs_4_), channel_id=1, source_target_pairs={{2,0},{4,2},{6,4},{7,6},{5,7},{3,5},{1,3},{0,1},{10,8},{12,10},{14... | collective-permute-start | bytes 786440 | tf_op jit(solution)/shard_map/ppermute | solution.py:225
  13.5 7.5 %collective-permute-start.2 = (bf16[512,256]{1,0:T(8,128)(2,1)S(1)}, bf16[512,256]{1,0:T(8,128)(2,1)S(1)}, u32[]{:S(2)}, u32[]{:S(2)}) collective-permute-start(bf16[512,256]{1,0:T(8,128)(2,1)S(1)} %collective-permute-done.refs_3_), channel_id=1, source_target_pairs={{0,2},{2,4},{4,6},{6,7},{7,5},{5,3},{3,1},{1,0},{8,10},{10,12},{12... | collective-permute-start | bytes 786440 | tf_op jit(solution)/shard_map/ppermute | solution.py:221
  13.8 7.7 %collective-permute-start.9 = (bf16[512,256]{1,0:T(8,128)(2,1)S(1)}, bf16[512,256]{1,0:T(8,128)(2,1)S(1)}, u32[]{:S(2)}, u32[]{:S(2)}) collective-permute-start(bf16[512,256]{1,0:T(8,128)(2,1)S(1)} %collective-permute-done.1.refs_4_), channel_id=1, source_target_pairs={{0,8},{16,24},{8,0},{24,16},{1,9},{17,25},{9,1},{25,17},{2,10},{18... | collective-permute-start | bytes 786440 | tf_op jit(solution)/shard_map/ppermute | solution.py:228
  16.3 6.7 %collective-permute-start.16 = (bf16[512,256]{1,0:T(8,128)(2,1)S(1)}, bf16[512,256]{1,0:T(8,128)(2,1)S(1)}, u32[]{:S(2)}, u32[]{:S(2)}) collective-permute-start(bf16[512,256]{1,0:T(8,128)(2,1)S(1)} %collective-permute-done.refs_3_), channel_id=1, source_target_pairs={{8,16},{16,8},{9,17},{17,9},{10,18},{18,10},{11,19},{19,11},{12,20... | collective-permute-start | bytes 786440 | tf_op jit(solution)/shard_map/ppermute | solution.py:229
  17.0 7.7 %collective-permute-start.8 = (bf16[512,256]{1,0:T(8,128)(2,1)S(1)}, bf16[512,256]{1,0:T(8,128)(2,1)S(1)}, u32[]{:S(2)}, u32[]{:S(2)}) collective-permute-start(bf16[512,256]{1,0:T(8,128)(2,1)S(1)} %collective-permute-done.refs_3_), channel_id=1, source_target_pairs={{0,8},{16,24},{8,0},{24,16},{1,9},{17,25},{9,1},{25,17},{2,10},{18... | collective-permute-start | bytes 786440 | tf_op jit(solution)/shard_map/ppermute | solution.py:228
  19.1 6.2 %collective-permute-start.19 = (bf16[512,256]{1,0:T(8,128)(2,1)S(1)}, bf16[512,256]{1,0:T(8,128)(2,1)S(1)}, u32[]{:S(2)}, u32[]{:S(2)}) collective-permute-start(bf16[512,256]{1,0:T(8,128)(2,1)S(1)} %collective-permute-done.3.refs_6_), channel_id=1, source_target_pairs={{8,16},{16,8},{9,17},{17,9},{10,18},{18,10},{11,19},{19,11},{12,20... | collective-permute-start | bytes 786440 | tf_op jit(solution)/shard_map/ppermute | solution.py:229
  21.0 8.1 %collective-permute-start.4 = (bf16[512,256]{1,0:T(8,128)(2,1)S(1)}, bf16[512,256]{1,0:T(8,128)(2,1)}, u32[]{:S(2)}, u32[]{:S(2)}) collective-permute-start(bf16[512,256]{1,0:T(8,128)(2,1)S(1)} %collective-permute-done.2.refs_5_), channel_id=1, source_target_pairs={{0,2},{2,4},{4,6},{6,7},{7,5},{5,3},{3,1},{1,0},{8,10},{10,12},{12... | collective-permute-start | bytes 786440 | tf_op jit(solution)/shard_map/ppermute | solution.py:221
  21.5 8.9 %collective-permute-start.5 = (bf16[512,256]{1,0:T(8,128)(2,1)S(1)}, bf16[512,256]{1,0:T(8,128)(2,1)}, u32[]{:S(2)}, u32[]{:S(2)}) collective-permute-start(bf16[512,256]{1,0:T(8,128)(2,1)S(1)} %collective-permute-done.3.refs_6_), channel_id=1, source_target_pairs={{2,0},{4,2},{6,4},{7,6},{5,7},{3,5},{1,3},{0,1},{10,8},{12,10},{14... | collective-permute-start | bytes 786440 | tf_op jit(solution)/shard_map/ppermute | solution.py:225
  23.0 14.9 %collective-permute-start.11 = (bf16[512,256]{1,0:T(8,128)(2,1)S(1)}, bf16[512,256]{1,0:T(8,128)(2,1)S(1)}, u32[]{:S(2)}, u32[]{:S(2)}) collective-permute-start(bf16[512,256]{1,0:T(8,128)(2,1)S(1)} %collective-permute-done.3.refs_6_), channel_id=1, source_target_pairs={{0,8},{16,24},{8,0},{24,16},{1,9},{17,25},{9,1},{25,17},{2,10},{18... | collective-permute-start | bytes 786440 | tf_op jit(solution)/shard_map/ppermute | solution.py:228
  24.7 15.5 %collective-permute-start.18 = (bf16[512,256]{1,0:T(8,128)(2,1)S(1)}, bf16[512,256]{1,0:T(8,128)(2,1)S(1)}, u32[]{:S(2)}, u32[]{:S(2)}) collective-permute-start(bf16[512,256]{1,0:T(8,128)(2,1)S(1)} %collective-permute-done.2.refs_5_), channel_id=1, source_target_pairs={{8,16},{16,8},{9,17},{17,9},{10,18},{18,10},{11,19},{19,11},{12,20... | collective-permute-start | bytes 786440 | tf_op jit(solution)/shard_map/ppermute | solution.py:229
  25.4 15.5 %collective-permute-start.10 = (bf16[512,256]{1,0:T(8,128)(2,1)S(1)}, bf16[512,256]{1,0:T(8,128)(2,1)}, u32[]{:S(2)}, u32[]{:S(2)}) collective-permute-start(bf16[512,256]{1,0:T(8,128)(2,1)S(1)} %collective-permute-done.2.refs_5_), channel_id=1, source_target_pairs={{0,8},{16,24},{8,0},{24,16},{1,9},{17,25},{9,1},{25,17},{2,10},{18... | collective-permute-start | bytes 786440 | tf_op jit(solution)/shard_map/ppermute | solution.py:228
  29.1 14.0 %collective-permute-start.6 = (bf16[512,256]{1,0:T(8,128)(2,1)}, bf16[512,256]{1,0:T(8,128)(2,1)}, u32[]{:S(2)}, u32[]{:S(2)}) collective-permute-start(bf16[512,256]{1,0:T(8,128)(2,1)} %collective-permute-done.4.refs_7_), channel_id=1, source_target_pairs={{0,2},{2,4},{4,6},{6,7},{7,5},{5,3},{3,1},{1,0},{8,10},{10,12},{12... | collective-permute-start | bytes 786440 | tf_op jit(solution)/shard_map/ppermute | solution.py:221
  30.4 13.3 %collective-permute-start.21 = (bf16[512,256]{1,0:T(8,128)(2,1)}, bf16[512,256]{1,0:T(8,128)(2,1)}, u32[]{:S(2)}, u32[]{:S(2)}) collective-permute-start(bf16[512,256]{1,0:T(8,128)(2,1)} %collective-permute-done.5.refs_8_), channel_id=1, source_target_pairs={{8,16},{16,8},{9,17},{17,9},{10,18},{18,10},{11,19},{19,11},{12,20... | collective-permute-start | bytes 786440 | tf_op jit(solution)/shard_map/ppermute | solution.py:229
  32.6 14.0 %all-to-all-start = ((bf16[8,64,256]{2,1,0:T(8,128)(2,1)}), bf16[8,64,256]{2,1,0:T(8,128)(2,1)S(1)}, u32[]{:S(2)}, u32[]{:S(2)}) async-start(bf16[8,64,256]{2,1,0:T(8,128)(2,1)} %bitcast.2.start), calls=%async_computation | async-start | bytes 524288 | tf_op jit(solution)/shard_map/all_to_all | solution.py:215
  37.9 8.7 %collective-permute-start.13 = (bf16[512,256]{1,0:T(8,128)(2,1)}, bf16[512,256]{1,0:T(8,128)(2,1)S(1)}, u32[]{:S(2)}, u32[]{:S(2)}) collective-permute-start(bf16[512,256]{1,0:T(8,128)(2,1)} %collective-permute-done.5.refs_8_), channel_id=1, source_target_pairs={{0,8},{16,24},{8,0},{24,16},{1,9},{17,25},{9,1},{25,17},{2,10},{18... | collective-permute-start | bytes 786440 | tf_op jit(solution)/shard_map/ppermute | solution.py:228
  40.2 6.5 %collective-permute-start.20 = (bf16[512,256]{1,0:T(8,128)(2,1)}, bf16[512,256]{1,0:T(8,128)(2,1)S(1)}, u32[]{:S(2)}, u32[]{:S(2)}) collective-permute-start(bf16[512,256]{1,0:T(8,128)(2,1)} %collective-permute-done.4.refs_7_), channel_id=1, source_target_pairs={{8,16},{16,8},{9,17},{17,9},{10,18},{18,10},{11,19},{19,11},{12,20... | collective-permute-start | bytes 786440 | tf_op jit(solution)/shard_map/ppermute | solution.py:229
  40.9 5.8 %collective-permute-start.12 = (bf16[512,256]{1,0:T(8,128)(2,1)}, bf16[512,256]{1,0:T(8,128)(2,1)S(1)}, u32[]{:S(2)}, u32[]{:S(2)}) collective-permute-start(bf16[512,256]{1,0:T(8,128)(2,1)} %collective-permute-done.4.refs_7_), channel_id=1, source_target_pairs={{0,8},{16,24},{8,0},{24,16},{1,9},{17,25},{9,1},{25,17},{2,10},{18... | collective-permute-start | bytes 786440 | tf_op jit(solution)/shard_map/ppermute | solution.py:228
  57.9 23.9 %all-to-all-start.1 = ((bf16[8,144,256]{2,1,0:T(8,128)(2,1)}), bf16[8,144,256]{2,1,0:T(8,128)(2,1)S(1)}, u32[]{:S(2)}, u32[]{:S(2)}) async-start(bf16[8,144,256]{2,1,0:T(8,128)(2,1)} %get-tuple-element.7), calls=%async_computation.1 | async-start | bytes 1179648 | tf_op jit(solution)/shard_map/all_to_all | solution.py:259
  64.4 6.1 %collective-permute-start.24 = (f32[8,128]{1,0:T(8,128)S(1)}, f32[8,128]{1,0:T(8,128)S(1)}, u32[]{:S(2)}, u32[]{:S(2)}) collective-permute-start(f32[8,128]{1,0:T(8,128)S(1)} %copy-done.21), channel_id=1, source_target_pairs={{0,16},{8,24},{16,0},{24,8},{1,17},{9,25},{17,1},{25,9},{2,18},{10... | collective-permute-start | bytes 12296 | tf_op jit(solution)/shard_map/ppermute | solution.py:194
  (30 other events, 308.6 us)

commit v3 on v2

--- a/solution.py
+++ b/solution.py
@@ -13,6 +13,7 @@
 ROWS_X = 2
 SHARE_ROWS = 16
 PAIR = 2
+IN_PLACE = 8
 
 
 def ring_order(count):
@@ -53,9 +54,17 @@
     where = [ring_place(n_src, me_src, shift) for shift in shifts]
 
     fetches = [
-        [pltpu.make_async_copy(chunk, held.at[g, slot], sems.at[g, slot]) for slot, chunk in enumerate(group)]
+        [
+            pltpu.make_async_copy(source, held.at[g, slot], sems.at[g, slot])
+            for slot, source in enumerate(group)
+            if g or slot >= IN_PLACE
+        ]
         for g, group in enumerate(sources)
     ]
+
+    def chunk(g, slot):
+        return held[g, slot] if g or slot >= IN_PLACE else sources[0][slot][...]
+
     band_fetch = pltpu.make_async_copy(band_in, band, band_sem)
     band_fetch.start()
     for fetch in sum(fetches, []):
@@ -90,7 +99,7 @@
             if first:
                 for fetch in fetches[g]:
                     fetch.wait()
-            chunks = jnp.concatenate([held[g, slot] for slot in range(n_src)], axis=1)
+            chunks = jnp.concatenate([chunk(g, slot) for slot in range(n_src)], axis=1)
             both = lax.dot_general(lhs[...], chunks, (((1,), (1,)), ((), ())), preferred_element_type=jnp.float32)
             for inside in range(blocks_here):
                 every[g * blocks_here + inside] = both[:, inside * BLOCK : (inside + 1) * BLOCK]
@@ -106,7 +115,7 @@
         for base in range(0, n_src, PAIR):
             slots = range(base, min(base + PAIR, n_src))
             columns = [
-                jnp.concatenate([held[g, slot] for g in range(len(sources))], axis=0) for slot in slots
+                jnp.concatenate([chunk(g, slot) for g in range(len(sources))], axis=0) for slot in slots
             ]
             prod = jnp.dot(wide, jnp.concatenate(columns, axis=1), preferred_element_type=jnp.float32)
             for slot in slots:
@@ -230,7 +239,7 @@
     near[-1], far[-1] = [pltpu.with_memory_space_constraint(x, pltpu.VMEM) for x in (near[-1], far[-1])]
     any_spec = pl.BlockSpec(memory_space=pl.ANY)
     vmem = pl.BlockSpec(memory_space=pltpu.VMEM)
-    band_cols = NEIGH * BLOCK
+    band_cols, kept = NEIGH * BLOCK, min(IN_PLACE, n_src)
     grad, hess, images, sums = pl.pallas_call(
         functools.partial(maps_kernel, n_src, shifts),
         out_shape=(
@@ -239,7 +248,7 @@
             jax.ShapeDtypeStruct((n_src, 2 * blocks_here * rows + SHARE_ROWS, cols), jnp.bfloat16),
             jax.ShapeDtypeStruct((8, 128), jnp.float32),
         ),
-        in_specs=[any_spec, vmem] + [any_spec] * n_src + 2 * ([any_spec] * (n_src - 1) + [vmem]),
+        in_specs=[any_spec, vmem] + [vmem] * kept + [any_spec] * (n_src - kept) + 2 * ([any_spec] * (n_src - 1) + [vmem]),
         out_specs=[vmem] * 4,
         scratch_shapes=[
             pltpu.SMEM(band.shape, jnp.int32),
@@ -252,9 +261,9 @@
             pltpu.SemaphoreType.DMA((3, n_src)),
             pltpu.SemaphoreType.DMA,
         ],
-        compiler_params=pltpu.CompilerParams(vmem_limit_bytes=60 << 20),
+        compiler_params=pltpu.CompilerParams(vmem_limit_bytes=58 << 20),
         name="maps",
-    )(band, field, *chunks, *near, *far)
+    )(band, field, *[pltpu.with_memory_space_constraint(c, pltpu.VMEM) for c in chunks[:kept]], *chunks[kept:], *near, *far)
 
     images = lax.all_to_all(images, "src", 0, 0, tiled=True)
     sums = summed(summed(sums, "rcv", n_rcv), "src", n_src)

time: 84.9 us -> 83.8 us (0.987)
  no operation moved by 1% of the time
where the time goes in v3:
time: 83.8 us; the launch traced here: 83.2 us
  starting transfers between devices  56.5 us (67%)
  Pallas kernels  12 us (14%)
  waiting for transfers between devices  11.6 us (14%)
  local copies, waits for them, and re-layouts  2.3 us (3%)
  between operations  0.87 us (1%)
    ppermute x8, starting transfers between devices, per_device(): near = [lax.ppermute(c, 'rcv', swaps(0)) for c in chunks]  19.2 us
    ppermute x7, starting transfers between devices, summed(): lax.ppermute(x, axis, [(d, d ^ bit * m) for d in range(count)])  11.3 us
    pallas_call x1, Pallas kernels, per_device(): pl.pallas_call(functools.partial(maps_kernel, n_src, shifts), out_shape=(...  9.55 us
    ppermute x7, waiting for transfers between devices, summed(): lax.ppermute(x, axis, [(d, d ^ bit * m) for d in range(count)])  7 us
    ppermute x8, starting transfers between devices, per_device(): far = [lax.ppermute(c, 'rcv', swaps(1)) for c in chunks]  6.71 us
    ppermute x3, starting transfers between devices, per_device(): bwd = lax.ppermute(bwd, 'src', behind)  6.19 us
    all_to_all x1, starting transfers between devices, per_device(): images = lax.all_to_all(images, 'src', 0, 0, tiled=True)  5.43 us
    all_to_all x1, starting transfers between devices, per_device(): field = lax.all_to_all(start, 'src', 0, 0, tiled=True)  5.27 us
  transfers between devices with their start and end apart: 32, of which 9 were waited for; matrix products, arithmetic and copies ran while one was open for 1% of the time, Pallas kernels for 0%

profile of v3, /device:TPU:0, one launch (start us, length us, event | category | flops | bytes accessed | tf_op | source)
XLA Modules:
  0.0 83.2 jit_solution(15214282841639108348)
XLA Ops:
  1.7 3.0 %collective-permute-start.1 = (bf16[512,256]{1,0:T(8,128)(2,1)S(1)}, bf16[512,256]{1,0:T(8,128)(2,1)S(1)}, u32[]{:S(2)}, u32[]{:S(2)}) collective-permute-start(bf16[512,256]{1,0:T(8,128)(2,1)S(1)} %bitcast.12), channel_id=1, source_target_pairs={{2,0},{4,2},{6,4},{7,6},{5,7},{3,5},{1,3},{0,1},{10,8},{12,10},{14... | collective-permute-start | bytes 786440 | tf_op jit(solution)/shard_map/ppermute | solution.py:234
  5.5 3.3 %collective-permute-start.7 = (bf16[512,256]{1,0:T(8,128)(2,1)S(1)}, bf16[512,256]{1,0:T(8,128)(2,1)S(1)}, u32[]{:S(2)}, u32[]{:S(2)}) collective-permute-start(bf16[512,256]{1,0:T(8,128)(2,1)S(1)} %bitcast.15), channel_id=1, source_target_pairs={{0,8},{16,24},{8,0},{24,16},{1,9},{17,25},{9,1},{25,17},{2,10},{18... | collective-permute-start | bytes 786440 | tf_op jit(solution)/shard_map/ppermute | solution.py:237
  8.8 2.3 %collective-permute-done.1.refs_4_ = bf16[512,256]{1,0:T(8,128)(2,1)S(1)} collective-permute-done((bf16[512,256]{1,0:T(8,128)(2,1)S(1)}, bf16[512,256]{1,0:T(8,128)(2,1)S(1)}, u32[]{:S(2)}, u32[]{:S(2)}) %collective-permute-start.1) | collective-permute-done | bytes 262176 | tf_op jit(solution)/shard_map/ppermute | solution.py:234
  11.7 1.7 %collective-permute-start.3 = (bf16[512,256]{1,0:T(8,128)(2,1)S(1)}, bf16[512,256]{1,0:T(8,128)(2,1)S(1)}, u32[]{:S(2)}, u32[]{:S(2)}) collective-permute-start(bf16[512,256]{1,0:T(8,128)(2,1)S(1)} %collective-permute-done.1.refs_4_), channel_id=1, source_target_pairs={{2,0},{4,2},{6,4},{7,6},{5,7},{3,5},{1,3},{0,1},{10,8},{12,10},{14... | collective-permute-start | bytes 786440 | tf_op jit(solution)/shard_map/ppermute | solution.py:234
  13.8 2.5 %collective-permute-start.9 = (bf16[512,256]{1,0:T(8,128)(2,1)S(1)}, bf16[512,256]{1,0:T(8,128)(2,1)}, u32[]{:S(2)}, u32[]{:S(2)}) collective-permute-start(bf16[512,256]{1,0:T(8,128)(2,1)S(1)} %collective-permute-done.1.refs_4_), channel_id=1, source_target_pairs={{0,8},{16,24},{8,0},{24,16},{1,9},{17,25},{9,1},{25,17},{2,10},{18... | collective-permute-start | bytes 786440 | tf_op jit(solution)/shard_map/ppermute | solution.py:237
  17.0 2.1 %collective-permute-start.8 = (bf16[512,256]{1,0:T(8,128)(2,1)S(1)}, bf16[512,256]{1,0:T(8,128)(2,1)S(1)}, u32[]{:S(2)}, u32[]{:S(2)}) collective-permute-start(bf16[512,256]{1,0:T(8,128)(2,1)S(1)} %collective-permute-done.refs_3_), channel_id=1, source_target_pairs={{0,8},{16,24},{8,0},{24,16},{1,9},{17,25},{9,1},{25,17},{2,10},{18... | collective-permute-start | bytes 786440 | tf_op jit(solution)/shard_map/ppermute | solution.py:237
  21.5 1.5 %collective-permute-start.5 = (bf16[512,256]{1,0:T(8,128)(2,1)S(1)}, bf16[512,256]{1,0:T(8,128)(2,1)S(1)}, u32[]{:S(2)}, u32[]{:S(2)}) collective-permute-start(bf16[512,256]{1,0:T(8,128)(2,1)S(1)} %collective-permute-done.3.refs_6_), channel_id=1, source_target_pairs={{2,0},{4,2},{6,4},{7,6},{5,7},{3,5},{1,3},{0,1},{10,8},{12,10},{14... | collective-permute-start | bytes 786440 | tf_op jit(solution)/shard_map/ppermute | solution.py:234
  23.0 1.7 %collective-permute-start.11 = (bf16[512,256]{1,0:T(8,128)(2,1)S(1)}, bf16[512,256]{1,0:T(8,128)(2,1)S(1)}, u32[]{:S(2)}, u32[]{:S(2)}) collective-permute-start(bf16[512,256]{1,0:T(8,128)(2,1)S(1)} %collective-permute-done.3.refs_6_), channel_id=1, source_target_pairs={{0,8},{16,24},{8,0},{24,16},{1,9},{17,25},{9,1},{25,17},{2,10},{18... | collective-permute-start | bytes 786440 | tf_op jit(solution)/shard_map/ppermute | solution.py:237
  24.6 1.4 %collective-permute-start.18 = (bf16[512,256]{1,0:T(8,128)(2,1)S(1)}, bf16[512,256]{1,0:T(8,128)(2,1)}, u32[]{:S(2)}, u32[]{:S(2)}) collective-permute-start(bf16[512,256]{1,0:T(8,128)(2,1)S(1)} %collective-permute-done.2.refs_5_), channel_id=1, source_target_pairs={{8,16},{16,8},{9,17},{17,9},{10,18},{18,10},{11,19},{19,11},{12,20... | collective-permute-start | bytes 786440 | tf_op jit(solution)/shard_map/ppermute | solution.py:238
  26.0 2.9 %collective-permute-start.10 = (bf16[512,256]{1,0:T(8,128)(2,1)S(1)}, bf16[512,256]{1,0:T(8,128)(2,1)}, u32[]{:S(2)}, u32[]{:S(2)}) collective-permute-start(bf16[512,256]{1,0:T(8,128)(2,1)S(1)} %collective-permute-done.2.refs_5_), channel_id=1, source_target_pairs={{0,8},{16,24},{8,0},{24,16},{1,9},{17,25},{9,1},{25,17},{2,10},{18... | collective-permute-start | bytes 786440 | tf_op jit(solution)/shard_map/ppermute | solution.py:237
  30.3 1.4 %collective-permute-start.21 = (bf16[512,256]{1,0:T(8,128)(2,1)S(1)}, bf16[512,256]{1,0:T(8,128)(2,1)}, u32[]{:S(2)}, u32[]{:S(2)}) collective-permute-start(bf16[512,256]{1,0:T(8,128)(2,1)S(1)} %collective-permute-done.5.refs_8_), channel_id=1, source_target_pairs={{8,16},{16,8},{9,17},{17,9},{10,18},{18,10},{11,19},{19,11},{12,20... | collective-permute-start | bytes 786440 | tf_op jit(solution)/shard_map/ppermute | solution.py:238
  32.5 5.3 %all-to-all-start = ((bf16[8,64,256]{2,1,0:T(8,128)(2,1)}), bf16[8,64,256]{2,1,0:T(8,128)(2,1)S(1)}, u32[]{:S(2)}, u32[]{:S(2)}) async-start(bf16[8,64,256]{2,1,0:T(8,128)(2,1)} %bitcast.2.start), calls=%async_computation | async-start | bytes 524288 | tf_op jit(solution)/shard_map/all_to_all | solution.py:224
  37.8 2.3 %collective-permute-start.13 = (bf16[512,256]{1,0:T(8,128)(2,1)S(1)}, bf16[512,256]{1,0:T(8,128)(2,1)S(1)}, u32[]{:S(2)}, u32[]{:S(2)}) collective-permute-start(bf16[512,256]{1,0:T(8,128)(2,1)S(1)} %collective-permute-done.5.refs_8_), channel_id=1, source_target_pairs={{0,8},{16,24},{8,0},{24,16},{1,9},{17,25},{9,1},{25,17},{2,10},{18... | collective-permute-start | bytes 786440 | tf_op jit(solution)/shard_map/ppermute | solution.py:237
  40.7 2.2 %collective-permute-start.12 = (bf16[512,256]{1,0:T(8,128)(2,1)S(1)}, bf16[512,256]{1,0:T(8,128)(2,1)}, u32[]{:S(2)}, u32[]{:S(2)}) collective-permute-start(bf16[512,256]{1,0:T(8,128)(2,1)S(1)} %collective-permute-done.4.refs_7_), channel_id=1, source_target_pairs={{0,8},{16,24},{8,0},{24,16},{1,9},{17,25},{9,1},{25,17},{2,10},{18... | collective-permute-start | bytes 786440 | tf_op jit(solution)/shard_map/ppermute | solution.py:237
  43.6 2.2 %collective-permute-start.14 = (bf16[512,256]{1,0:T(8,128)(2,1)S(1)}, bf16[512,256]{1,0:T(8,128)(2,1)S(1)}, u32[]{:S(2)}, u32[]{:S(2)}) collective-permute-start(bf16[512,256]{1,0:T(8,128)(2,1)S(1)} %collective-permute-done.6.refs_9_), channel_id=1, source_target_pairs={{0,8},{16,24},{8,0},{24,16},{1,9},{17,25},{9,1},{25,17},{2,10},{18... | collective-permute-start | bytes 786440 | tf_op jit(solution)/shard_map/ppermute | solution.py:237
  47.4 9.5 %maps.1 = (f32[2,64,768]{2,1,0:T(8,128)}, f32[2,64,768]{2,1,0:T(8,128)}, bf16[8,144,256]{2,1,0:T(8,128)(2,1)}, f32[8,128]{1,0:T(8,128)}) custom-call(s32[2,3]{1,0:T(2,128)} %refs_0_.1, bf16[8,64,256]{2,1,0:T(8,128)(2,1)} %copy-done.2, bf16[512,256]{1,0:T(8,128)(2,1)S(1)} %bitcast.16, bf16[512,256]{1,0:T(8,128)(2,1)S(1)} %collective-permute-done.refs_3_, ...), custom_call_target="tpu_custom_call" | custom-call | tf_op jit(solution)/shard_map/maps/pallas_call | solution.py:243
  57.0 5.4 %all-to-all-start.1 = ((bf16[8,144,256]{2,1,0:T(8,128)(2,1)}), bf16[8,144,256]{2,1,0:T(8,128)(2,1)S(1)}, u32[]{:S(2)}, u32[]{:S(2)}) async-start(bf16[8,144,256]{2,1,0:T(8,128)(2,1)} %get-tuple-element.7), calls=%async_computation.1 | async-start | bytes 1179648 | tf_op jit(solution)/shard_map/all_to_all | solution.py:268
  63.3 4.5 %collective-permute-start.24 = (f32[8,128]{1,0:T(8,128)S(1)}, f32[8,128]{1,0:T(8,128)S(1)}, u32[]{:S(2)}, u32[]{:S(2)}) collective-permute-start(f32[8,128]{1,0:T(8,128)S(1)} %copy-done.13), channel_id=1, source_target_pairs={{0,16},{8,24},{16,0},{24,8},{1,17},{9,25},{17,1},{25,9},{2,18},{10... | collective-permute-start | bytes 12296 | tf_op jit(solution)/shard_map/ppermute | solution.py:203
  67.8 1.6 %collective-permute-done.24 = f32[8,128]{1,0:T(8,128)S(1)} collective-permute-done((f32[8,128]{1,0:T(8,128)S(1)}, f32[8,128]{1,0:T(8,128)S(1)}, u32[]{:S(2)}, u32[]{:S(2)}) %collective-permute-start.24) | collective-permute-done | bytes 4128 | tf_op jit(solution)/shard_map/ppermute | solution.py:203
  69.4 2.6 %collective-permute-start.28 = (f32[8,128]{1,0:T(8,128)S(1)}, f32[8,128]{1,0:T(8,128)S(1)}, u32[]{:S(2)}, u32[]{:S(2)}) collective-permute-start(f32[8,128]{1,0:T(8,128)S(1)} %add_add_fusion.1), channel_id=1, source_target_pairs={{0,3},{1,2},{2,1},{3,0},{4,7},{5,6},{6,5},{7,4},{8,11},{9,10},{10,... | collective-permute-start | bytes 12296 | tf_op jit(solution)/shard_map/ppermute | solution.py:203
  74.1 1.8 %collective-permute-done.27 = f32[8,128]{1,0:T(8,128)S(1)} collective-permute-done((f32[8,128]{1,0:T(8,128)S(1)}, f32[8,128]{1,0:T(8,128)S(1)}, u32[]{:S(2)}, u32[]{:S(2)}) %collective-permute-start.27) | collective-permute-done | bytes 4128 | tf_op jit(solution)/shard_map/ppermute | solution.py:203
  76.3 2.4 %collective-permute-start.29 = (f32[8,128]{1,0:T(8,128)S(1)}, f32[8,128]{1,0:T(8,128)S(1)}, u32[]{:S(2)}, u32[]{:S(2)}) collective-permute-start(f32[8,128]{1,0:T(8,128)S(1)} %add_add_fusion), channel_id=1, source_target_pairs={{0,4},{1,5},{2,6},{3,7},{4,0},{5,1},{6,2},{7,3},{8,12},{9,13},{10,... | collective-permute-start | bytes 12296 | tf_op jit(solution)/shard_map/ppermute | solution.py:203
  78.6 2.1 %collective-permute-done.29 = f32[8,128]{1,0:T(8,128)S(1)} collective-permute-done((f32[8,128]{1,0:T(8,128)S(1)}, f32[8,128]{1,0:T(8,128)S(1)}, u32[]{:S(2)}, u32[]{:S(2)}) %collective-permute-start.29) | collective-permute-done | bytes 4128 | tf_op jit(solution)/shard_map/ppermute | solution.py:203
  80.8 2.5 %combine.1 = (f32[32,2,3,2,256]{4,3,2,1,0:T(2,128)}, f32[512,2,128]{2,1,0:T(2,128)}) custom-call(f32[8,128]{1,0:T(8,128)S(1)} %add.27.sums, bf16[8,144,256]{2,1,0:T(8,128)(2,1)S(1)} %all-to-all-done.1.images, f32[2,64,768]{2,1,0:T(8,128)S(1)} %copy-done, f32[2,64,768]{2,1,0:T(8,128)S(1)} %copy-done.1, bf16[8,64,256]{2,1,0:T(8,128)(2,1)} %bitcast.2.start), custom_call_target="tpu_custom_call" | custom-call | tf_op jit(solution)/shard_map/combine/pallas_call | solution.py:271
  (76 shorter events, 14.3 us)
Async XLA Ops:
  1.7 9.4 %collective-permute-start.1 = (bf16[512,256]{1,0:T(8,128)(2,1)S(1)}, bf16[512,256]{1,0:T(8,128)(2,1)S(1)}, u32[]{:S(2)}, u32[]{:S(2)}) collective-permute-start(bf16[512,256]{1,0:T(8,128)(2,1)S(1)} %bitcast.12), channel_id=1, source_target_pairs={{2,0},{4,2},{6,4},{7,6},{5,7},{3,5},{1,3},{0,1},{10,8},{12,10},{14... | collective-permute-start | bytes 786440 | tf_op jit(solution)/shard_map/ppermute | solution.py:234
  4.7 8.8 %collective-permute-start = (bf16[512,256]{1,0:T(8,128)(2,1)S(1)}, bf16[512,256]{1,0:T(8,128)(2,1)S(1)}, u32[]{:S(2)}, u32[]{:S(2)}) collective-permute-start(bf16[512,256]{1,0:T(8,128)(2,1)S(1)} %bitcast.13), channel_id=1, source_target_pairs={{0,2},{2,4},{4,6},{6,7},{7,5},{5,3},{3,1},{1,0},{8,10},{10,12},{12... | collective-permute-start | bytes 786440 | tf_op jit(solution)/shard_map/ppermute | solution.py:230
  4.8 9.0 %collective-permute-start.15 = (bf16[512,256]{1,0:T(8,128)(2,1)S(1)}, bf16[512,256]{1,0:T(8,128)(2,1)S(1)}, u32[]{:S(2)}, u32[]{:S(2)}) collective-permute-start(bf16[512,256]{1,0:T(8,128)(2,1)S(1)} %bitcast.14), channel_id=1, source_target_pairs={{8,16},{16,8},{9,17},{17,9},{10,18},{18,10},{11,19},{19,11},{12,20... | collective-permute-start | bytes 786440 | tf_op jit(solution)/shard_map/ppermute | solution.py:238
  5.5 10.8 %collective-permute-start.7 = (bf16[512,256]{1,0:T(8,128)(2,1)S(1)}, bf16[512,256]{1,0:T(8,128)(2,1)S(1)}, u32[]{:S(2)}, u32[]{:S(2)}) collective-permute-start(bf16[512,256]{1,0:T(8,128)(2,1)S(1)} %bitcast.15), channel_id=1, source_target_pairs={{0,8},{16,24},{8,0},{24,16},{1,9},{17,25},{9,1},{25,17},{2,10},{18... | collective-permute-start | bytes 786440 | tf_op jit(solution)/shard_map/ppermute | solution.py:237
  11.1 5.9 %collective-permute-start.17 = (bf16[512,256]{1,0:T(8,128)(2,1)S(1)}, bf16[512,256]{1,0:T(8,128)(2,1)S(1)}, u32[]{:S(2)}, u32[]{:S(2)}) collective-permute-start(bf16[512,256]{1,0:T(8,128)(2,1)S(1)} %collective-permute-done.1.refs_4_), channel_id=1, source_target_pairs={{8,16},{16,8},{9,17},{17,9},{10,18},{18,10},{11,19},{19,11},{12,20... | collective-permute-start | bytes 786440 | tf_op jit(solution)/shard_map/ppermute | solution.py:238
  11.7 7.4 %collective-permute-start.3 = (bf16[512,256]{1,0:T(8,128)(2,1)S(1)}, bf16[512,256]{1,0:T(8,128)(2,1)S(1)}, u32[]{:S(2)}, u32[]{:S(2)}) collective-permute-start(bf16[512,256]{1,0:T(8,128)(2,1)S(1)} %collective-permute-done.1.refs_4_), channel_id=1, source_target_pairs={{2,0},{4,2},{6,4},{7,6},{5,7},{3,5},{1,3},{0,1},{10,8},{12,10},{14... | collective-permute-start | bytes 786440 | tf_op jit(solution)/shard_map/ppermute | solution.py:234
  13.4 7.5 %collective-permute-start.2 = (bf16[512,256]{1,0:T(8,128)(2,1)S(1)}, bf16[512,256]{1,0:T(8,128)(2,1)S(1)}, u32[]{:S(2)}, u32[]{:S(2)}) collective-permute-start(bf16[512,256]{1,0:T(8,128)(2,1)S(1)} %collective-permute-done.refs_3_), channel_id=1, source_target_pairs={{0,2},{2,4},{4,6},{6,7},{7,5},{5,3},{3,1},{1,0},{8,10},{10,12},{12... | collective-permute-start | bytes 786440 | tf_op jit(solution)/shard_map/ppermute | solution.py:230
  13.8 7.7 %collective-permute-start.9 = (bf16[512,256]{1,0:T(8,128)(2,1)S(1)}, bf16[512,256]{1,0:T(8,128)(2,1)}, u32[]{:S(2)}, u32[]{:S(2)}) collective-permute-start(bf16[512,256]{1,0:T(8,128)(2,1)S(1)} %collective-permute-done.1.refs_4_), channel_id=1, source_target_pairs={{0,8},{16,24},{8,0},{24,16},{1,9},{17,25},{9,1},{25,17},{2,10},{18... | collective-permute-start | bytes 786440 | tf_op jit(solution)/shard_map/ppermute | solution.py:237
  16.3 6.7 %collective-permute-start.16 = (bf16[512,256]{1,0:T(8,128)(2,1)S(1)}, bf16[512,256]{1,0:T(8,128)(2,1)S(1)}, u32[]{:S(2)}, u32[]{:S(2)}) collective-permute-start(bf16[512,256]{1,0:T(8,128)(2,1)S(1)} %collective-permute-done.refs_3_), channel_id=1, source_target_pairs={{8,16},{16,8},{9,17},{17,9},{10,18},{18,10},{11,19},{19,11},{12,20... | collective-permute-start | bytes 786440 | tf_op jit(solution)/shard_map/ppermute | solution.py:238
  17.0 7.7 %collective-permute-start.8 = (bf16[512,256]{1,0:T(8,128)(2,1)S(1)}, bf16[512,256]{1,0:T(8,128)(2,1)S(1)}, u32[]{:S(2)}, u32[]{:S(2)}) collective-permute-start(bf16[512,256]{1,0:T(8,128)(2,1)S(1)} %collective-permute-done.refs_3_), channel_id=1, source_target_pairs={{0,8},{16,24},{8,0},{24,16},{1,9},{17,25},{9,1},{25,17},{2,10},{18... | collective-permute-start | bytes 786440 | tf_op jit(solution)/shard_map/ppermute | solution.py:237
  19.1 6.9 %collective-permute-start.19 = (bf16[512,256]{1,0:T(8,128)(2,1)S(1)}, bf16[512,256]{1,0:T(8,128)(2,1)S(1)}, u32[]{:S(2)}, u32[]{:S(2)}) collective-permute-start(bf16[512,256]{1,0:T(8,128)(2,1)S(1)} %collective-permute-done.3.refs_6_), channel_id=1, source_target_pairs={{8,16},{16,8},{9,17},{17,9},{10,18},{18,10},{11,19},{19,11},{12,20... | collective-permute-start | bytes 786440 | tf_op jit(solution)/shard_map/ppermute | solution.py:238
  20.9 8.0 %collective-permute-start.4 = (bf16[512,256]{1,0:T(8,128)(2,1)S(1)}, bf16[512,256]{1,0:T(8,128)(2,1)S(1)}, u32[]{:S(2)}, u32[]{:S(2)}) collective-permute-start(bf16[512,256]{1,0:T(8,128)(2,1)S(1)} %collective-permute-done.2.refs_5_), channel_id=1, source_target_pairs={{0,2},{2,4},{4,6},{6,7},{7,5},{5,3},{3,1},{1,0},{8,10},{10,12},{12... | collective-permute-start | bytes 786440 | tf_op jit(solution)/shard_map/ppermute | solution.py:230
  21.5 8.8 %collective-permute-start.5 = (bf16[512,256]{1,0:T(8,128)(2,1)S(1)}, bf16[512,256]{1,0:T(8,128)(2,1)S(1)}, u32[]{:S(2)}, u32[]{:S(2)}) collective-permute-start(bf16[512,256]{1,0:T(8,128)(2,1)S(1)} %collective-permute-done.3.refs_6_), channel_id=1, source_target_pairs={{2,0},{4,2},{6,4},{7,6},{5,7},{3,5},{1,3},{0,1},{10,8},{12,10},{14... | collective-permute-start | bytes 786440 | tf_op jit(solution)/shard_map/ppermute | solution.py:234
  23.0 14.8 %collective-permute-start.11 = (bf16[512,256]{1,0:T(8,128)(2,1)S(1)}, bf16[512,256]{1,0:T(8,128)(2,1)S(1)}, u32[]{:S(2)}, u32[]{:S(2)}) collective-permute-start(bf16[512,256]{1,0:T(8,128)(2,1)S(1)} %collective-permute-done.3.refs_6_), channel_id=1, source_target_pairs={{0,8},{16,24},{8,0},{24,16},{1,9},{17,25},{9,1},{25,17},{2,10},{18... | collective-permute-start | bytes 786440 | tf_op jit(solution)/shard_map/ppermute | solution.py:237
  24.6 15.4 %collective-permute-start.18 = (bf16[512,256]{1,0:T(8,128)(2,1)S(1)}, bf16[512,256]{1,0:T(8,128)(2,1)}, u32[]{:S(2)}, u32[]{:S(2)}) collective-permute-start(bf16[512,256]{1,0:T(8,128)(2,1)S(1)} %collective-permute-done.2.refs_5_), channel_id=1, source_target_pairs={{8,16},{16,8},{9,17},{17,9},{10,18},{18,10},{11,19},{19,11},{12,20... | collective-permute-start | bytes 786440 | tf_op jit(solution)/shard_map/ppermute | solution.py:238
  26.0 14.7 %collective-permute-start.10 = (bf16[512,256]{1,0:T(8,128)(2,1)S(1)}, bf16[512,256]{1,0:T(8,128)(2,1)}, u32[]{:S(2)}, u32[]{:S(2)}) collective-permute-start(bf16[512,256]{1,0:T(8,128)(2,1)S(1)} %collective-permute-done.2.refs_5_), channel_id=1, source_target_pairs={{0,8},{16,24},{8,0},{24,16},{1,9},{17,25},{9,1},{25,17},{2,10},{18... | collective-permute-start | bytes 786440 | tf_op jit(solution)/shard_map/ppermute | solution.py:237
  29.0 13.9 %collective-permute-start.6 = (bf16[512,256]{1,0:T(8,128)(2,1)S(1)}, bf16[512,256]{1,0:T(8,128)(2,1)S(1)}, u32[]{:S(2)}, u32[]{:S(2)}) collective-permute-start(bf16[512,256]{1,0:T(8,128)(2,1)S(1)} %collective-permute-done.4.refs_7_), channel_id=1, source_target_pairs={{0,2},{2,4},{4,6},{6,7},{7,5},{5,3},{3,1},{1,0},{8,10},{10,12},{12... | collective-permute-start | bytes 786440 | tf_op jit(solution)/shard_map/ppermute | solution.py:230
  30.3 13.2 %collective-permute-start.21 = (bf16[512,256]{1,0:T(8,128)(2,1)S(1)}, bf16[512,256]{1,0:T(8,128)(2,1)}, u32[]{:S(2)}, u32[]{:S(2)}) collective-permute-start(bf16[512,256]{1,0:T(8,128)(2,1)S(1)} %collective-permute-done.5.refs_8_), channel_id=1, source_target_pairs={{8,16},{16,8},{9,17},{17,9},{10,18},{18,10},{11,19},{19,11},{12,20... | collective-permute-start | bytes 786440 | tf_op jit(solution)/shard_map/ppermute | solution.py:238
  32.5 14.0 %all-to-all-start = ((bf16[8,64,256]{2,1,0:T(8,128)(2,1)}), bf16[8,64,256]{2,1,0:T(8,128)(2,1)S(1)}, u32[]{:S(2)}, u32[]{:S(2)}) async-start(bf16[8,64,256]{2,1,0:T(8,128)(2,1)} %bitcast.2.start), calls=%async_computation | async-start | bytes 524288 | tf_op jit(solution)/shard_map/all_to_all | solution.py:224
  37.8 8.7 %collective-permute-start.13 = (bf16[512,256]{1,0:T(8,128)(2,1)S(1)}, bf16[512,256]{1,0:T(8,128)(2,1)S(1)}, u32[]{:S(2)}, u32[]{:S(2)}) collective-permute-start(bf16[512,256]{1,0:T(8,128)(2,1)S(1)} %collective-permute-done.5.refs_8_), channel_id=1, source_target_pairs={{0,8},{16,24},{8,0},{24,16},{1,9},{17,25},{9,1},{25,17},{2,10},{18... | collective-permute-start | bytes 786440 | tf_op jit(solution)/shard_map/ppermute | solution.py:237
  40.0 6.5 %collective-permute-start.20 = (bf16[512,256]{1,0:T(8,128)(2,1)S(1)}, bf16[512,256]{1,0:T(8,128)(2,1)S(1)}, u32[]{:S(2)}, u32[]{:S(2)}) collective-permute-start(bf16[512,256]{1,0:T(8,128)(2,1)S(1)} %collective-permute-done.4.refs_7_), channel_id=1, source_target_pairs={{8,16},{16,8},{9,17},{17,9},{10,18},{18,10},{11,19},{19,11},{12,20... | collective-permute-start | bytes 786440 | tf_op jit(solution)/shard_map/ppermute | solution.py:238
  40.7 5.8 %collective-permute-start.12 = (bf16[512,256]{1,0:T(8,128)(2,1)S(1)}, bf16[512,256]{1,0:T(8,128)(2,1)}, u32[]{:S(2)}, u32[]{:S(2)}) collective-permute-start(bf16[512,256]{1,0:T(8,128)(2,1)S(1)} %collective-permute-done.4.refs_7_), channel_id=1, source_target_pairs={{0,8},{16,24},{8,0},{24,16},{1,9},{17,25},{9,1},{25,17},{2,10},{18... | collective-permute-start | bytes 786440 | tf_op jit(solution)/shard_map/ppermute | solution.py:237
  57.0 23.8 %all-to-all-start.1 = ((bf16[8,144,256]{2,1,0:T(8,128)(2,1)}), bf16[8,144,256]{2,1,0:T(8,128)(2,1)S(1)}, u32[]{:S(2)}, u32[]{:S(2)}) async-start(bf16[8,144,256]{2,1,0:T(8,128)(2,1)} %get-tuple-element.7), calls=%async_computation.1 | async-start | bytes 1179648 | tf_op jit(solution)/shard_map/all_to_all | solution.py:268
  63.3 6.1 %collective-permute-start.24 = (f32[8,128]{1,0:T(8,128)S(1)}, f32[8,128]{1,0:T(8,128)S(1)}, u32[]{:S(2)}, u32[]{:S(2)}) collective-permute-start(f32[8,128]{1,0:T(8,128)S(1)} %copy-done.13), channel_id=1, source_target_pairs={{0,16},{8,24},{16,0},{24,8},{1,17},{9,25},{17,1},{25,9},{2,18},{10... | collective-permute-start | bytes 12296 | tf_op jit(solution)/shard_map/ppermute | solution.py:203
  (22 other events, 191.4 us)

commit v4 on v3

--- a/solution.py
+++ b/solution.py
@@ -14,6 +14,7 @@
 SHARE_ROWS = 16
 PAIR = 2
 IN_PLACE = 8
+LATE = 3
 
 
 def ring_order(count):
@@ -36,6 +37,10 @@
     total = jnp.sum(sums, axis=1, keepdims=True)
     qq, qw = total[1:2], total[4:5]
     return jnp.where(qq > 0, qw / jnp.where(qq > 0, qq, 1.0), 0.0)
+
+
+def in_place(n_src, g, slot):
+    return slot >= n_src - LATE if g else slot < IN_PLACE
 
 
 def maps_kernel(n_src, shifts, *refs):
@@ -57,13 +62,13 @@
         [
             pltpu.make_async_copy(source, held.at[g, slot], sems.at[g, slot])
             for slot, source in enumerate(group)
-            if g or slot >= IN_PLACE
+            if not in_place(n_src, g, slot)
         ]
         for g, group in enumerate(sources)
     ]
 
     def chunk(g, slot):
-        return held[g, slot] if g or slot >= IN_PLACE else sources[0][slot][...]
+        return sources[g][slot][...] if in_place(n_src, g, slot) else held[g, slot]
 
     band_fetch = pltpu.make_async_copy(band_in, band, band_sem)
     band_fetch.start()
@@ -236,10 +241,14 @@
             shifts.append(step)
     near = [lax.ppermute(c, "rcv", swaps(0)) for c in chunks]
     far = [lax.ppermute(c, "rcv", swaps(1)) for c in chunks]
-    near[-1], far[-1] = [pltpu.with_memory_space_constraint(x, pltpu.VMEM) for x in (near[-1], far[-1])]
+    gathered = [
+        pltpu.with_memory_space_constraint(x, pltpu.VMEM) if in_place(n_src, g, slot) else x
+        for g, group in enumerate((chunks, near, far))
+        for slot, x in enumerate(group)
+    ]
     any_spec = pl.BlockSpec(memory_space=pl.ANY)
     vmem = pl.BlockSpec(memory_space=pltpu.VMEM)
-    band_cols, kept = NEIGH * BLOCK, min(IN_PLACE, n_src)
+    band_cols = NEIGH * BLOCK
     grad, hess, images, sums = pl.pallas_call(
         functools.partial(maps_kernel, n_src, shifts),
         out_shape=(
@@ -248,7 +257,8 @@
             jax.ShapeDtypeStruct((n_src, 2 * blocks_here * rows + SHARE_ROWS, cols), jnp.bfloat16),
             jax.ShapeDtypeStruct((8, 128), jnp.float32),
         ),
-        in_specs=[any_spec, vmem] + [vmem] * kept + [any_spec] * (n_src - kept) + 2 * ([any_spec] * (n_src - 1) + [vmem]),
+        in_specs=[any_spec, vmem]
+        + [vmem if in_place(n_src, g, slot) else any_spec for g in range(3) for slot in range(n_src)],
         out_specs=[vmem] * 4,
         scratch_shapes=[
             pltpu.SMEM(band.shape, jnp.int32),
@@ -261,9 +271,9 @@
             pltpu.SemaphoreType.DMA((3, n_src)),
             pltpu.SemaphoreType.DMA,
         ],
-        compiler_params=pltpu.CompilerParams(vmem_limit_bytes=58 << 20),
+        compiler_params=pltpu.CompilerParams(vmem_limit_bytes=56 << 20),
         name="maps",
-    )(band, field, *[pltpu.with_memory_space_constraint(c, pltpu.VMEM) for c in chunks[:kept]], *chunks[kept:], *near, *far)
+    )(band, field, *gathered)
 
     images = lax.all_to_all(images, "src", 0, 0, tiled=True)
     sums = summed(summed(sums, "rcv", n_rcv), "src", n_src)

time: 83.8 us -> 83.8 us (level)
  transfers between devices with their start and end apart: 32 -> 32, of which waited for: 9 -> 8; matrix products, arithmetic and copies ran while one was open for 1% -> 1% of each run, Pallas kernels for 0% -> 0%
where the time goes in v4:
time: 83.8 us; the launch traced here: 83.2 us
  starting transfers between devices  56.6 us (68%)
  Pallas kernels  12.1 us (14%)
  waiting for transfers between devices  11.7 us (14%)
  local copies, waits for them, and re-layouts  1.85 us (2%)
  between operations  0.9 us (1%)
    ppermute x8, starting transfers between devices, per_device(): near = [lax.ppermute(c, 'rcv', swaps(0)) for c in chunks]  19.8 us
    ppermute x7, starting transfers between devices, summed(): lax.ppermute(x, axis, [(d, d ^ bit * m) for d in range(count)])  11.1 us
    pallas_call x1, Pallas kernels, per_device(): pl.pallas_call(functools.partial(maps_kernel, n_src, shifts), out_shape=(...  9.63 us
    ppermute x7, waiting for transfers between devices, summed(): lax.ppermute(x, axis, [(d, d ^ bit * m) for d in range(count)])  7.01 us
    ppermute x3, starting transfers between devices, per_device(): bwd = lax.ppermute(bwd, 'src', behind)  6.19 us
    ppermute x8, starting transfers between devices, per_device(): far = [lax.ppermute(c, 'rcv', swaps(1)) for c in chunks]  6.01 us
    all_to_all x1, starting transfers between devices, per_device(): images = lax.all_to_all(images, 'src', 0, 0, tiled=True)  5.78 us
    all_to_all x1, starting transfers between devices, per_device(): field = lax.all_to_all(start, 'src', 0, 0, tiled=True)  5.28 us
  transfers between devices with their start and end apart: 32, of which 8 were waited for; matrix products, arithmetic and copies ran while one was open for 1% of the time, Pallas kernels for 0%

profile of v4, /device:TPU:0, one launch (start us, length us, event | category | flops | bytes accessed | tf_op | source)
XLA Modules:
  0.0 83.2 jit_solution(2024777182344598618)
XLA Ops:
  1.7 3.0 %collective-permute-start.1 = (bf16[512,256]{1,0:T(8,128)(2,1)S(1)}, bf16[512,256]{1,0:T(8,128)(2,1)S(1)}, u32[]{:S(2)}, u32[]{:S(2)}) collective-permute-start(bf16[512,256]{1,0:T(8,128)(2,1)S(1)} %bitcast.12), channel_id=1, source_target_pairs={{2,0},{4,2},{6,4},{7,6},{5,7},{3,5},{1,3},{0,1},{10,8},{12,10},{14... | collective-permute-start | bytes 786440 | tf_op jit(solution)/shard_map/ppermute | solution.py:239
  5.5 3.3 %collective-permute-start.7 = (bf16[512,256]{1,0:T(8,128)(2,1)S(1)}, bf16[512,256]{1,0:T(8,128)(2,1)S(1)}, u32[]{:S(2)}, u32[]{:S(2)}) collective-permute-start(bf16[512,256]{1,0:T(8,128)(2,1)S(1)} %bitcast.15), channel_id=1, source_target_pairs={{0,8},{16,24},{8,0},{24,16},{1,9},{17,25},{9,1},{25,17},{2,10},{18... | collective-permute-start | bytes 786440 | tf_op jit(solution)/shard_map/ppermute | solution.py:242
  8.8 2.3 %collective-permute-done.1.refs_4_ = bf16[512,256]{1,0:T(8,128)(2,1)S(1)} collective-permute-done((bf16[512,256]{1,0:T(8,128)(2,1)S(1)}, bf16[512,256]{1,0:T(8,128)(2,1)S(1)}, u32[]{:S(2)}, u32[]{:S(2)}) %collective-permute-start.1) | collective-permute-done | bytes 262176 | tf_op jit(solution)/shard_map/ppermute | solution.py:239
  11.7 1.7 %collective-permute-start.3 = (bf16[512,256]{1,0:T(8,128)(2,1)S(1)}, bf16[512,256]{1,0:T(8,128)(2,1)S(1)}, u32[]{:S(2)}, u32[]{:S(2)}) collective-permute-start(bf16[512,256]{1,0:T(8,128)(2,1)S(1)} %collective-permute-done.1.refs_4_), channel_id=1, source_target_pairs={{2,0},{4,2},{6,4},{7,6},{5,7},{3,5},{1,3},{0,1},{10,8},{12,10},{14... | collective-permute-start | bytes 786440 | tf_op jit(solution)/shard_map/ppermute | solution.py:239
  13.8 2.5 %collective-permute-start.9 = (bf16[512,256]{1,0:T(8,128)(2,1)S(1)}, bf16[512,256]{1,0:T(8,128)(2,1)S(1)}, u32[]{:S(2)}, u32[]{:S(2)}) collective-permute-start(bf16[512,256]{1,0:T(8,128)(2,1)S(1)} %collective-permute-done.1.refs_4_), channel_id=1, source_target_pairs={{0,8},{16,24},{8,0},{24,16},{1,9},{17,25},{9,1},{25,17},{2,10},{18... | collective-permute-start | bytes 786440 | tf_op jit(solution)/shard_map/ppermute | solution.py:242
  17.0 2.1 %collective-permute-start.8 = (bf16[512,256]{1,0:T(8,128)(2,1)S(1)}, bf16[512,256]{1,0:T(8,128)(2,1)S(1)}, u32[]{:S(2)}, u32[]{:S(2)}) collective-permute-start(bf16[512,256]{1,0:T(8,128)(2,1)S(1)} %collective-permute-done.refs_3_), channel_id=1, source_target_pairs={{0,8},{16,24},{8,0},{24,16},{1,9},{17,25},{9,1},{25,17},{2,10},{18... | collective-permute-start | bytes 786440 | tf_op jit(solution)/shard_map/ppermute | solution.py:242
  21.5 1.5 %collective-permute-start.5 = (bf16[512,256]{1,0:T(8,128)(2,1)S(1)}, bf16[512,256]{1,0:T(8,128)(2,1)S(1)}, u32[]{:S(2)}, u32[]{:S(2)}) collective-permute-start(bf16[512,256]{1,0:T(8,128)(2,1)S(1)} %collective-permute-done.3.refs_6_), channel_id=1, source_target_pairs={{2,0},{4,2},{6,4},{7,6},{5,7},{3,5},{1,3},{0,1},{10,8},{12,10},{14... | collective-permute-start | bytes 786440 | tf_op jit(solution)/shard_map/ppermute | solution.py:239
  23.0 1.7 %collective-permute-start.11 = (bf16[512,256]{1,0:T(8,128)(2,1)S(1)}, bf16[512,256]{1,0:T(8,128)(2,1)}, u32[]{:S(2)}, u32[]{:S(2)}) collective-permute-start(bf16[512,256]{1,0:T(8,128)(2,1)S(1)} %collective-permute-done.3.refs_6_), channel_id=1, source_target_pairs={{0,8},{16,24},{8,0},{24,16},{1,9},{17,25},{9,1},{25,17},{2,10},{18... | collective-permute-start | bytes 786440 | tf_op jit(solution)/shard_map/ppermute | solution.py:242
  24.6 1.3 %collective-permute-start.18 = (bf16[512,256]{1,0:T(8,128)(2,1)S(1)}, bf16[512,256]{1,0:T(8,128)(2,1)}, u32[]{:S(2)}, u32[]{:S(2)}) collective-permute-start(bf16[512,256]{1,0:T(8,128)(2,1)S(1)} %collective-permute-done.2.refs_5_), channel_id=1, source_target_pairs={{8,16},{16,8},{9,17},{17,9},{10,18},{18,10},{11,19},{19,11},{12,20... | collective-permute-start | bytes 786440 | tf_op jit(solution)/shard_map/ppermute | solution.py:243
  26.0 2.9 %collective-permute-start.10 = (bf16[512,256]{1,0:T(8,128)(2,1)S(1)}, bf16[512,256]{1,0:T(8,128)(2,1)}, u32[]{:S(2)}, u32[]{:S(2)}) collective-permute-start(bf16[512,256]{1,0:T(8,128)(2,1)S(1)} %collective-permute-done.2.refs_5_), channel_id=1, source_target_pairs={{0,8},{16,24},{8,0},{24,16},{1,9},{17,25},{9,1},{25,17},{2,10},{18... | collective-permute-start | bytes 786440 | tf_op jit(solution)/shard_map/ppermute | solution.py:242
  28.9 1.4 %collective-permute-start.6 = (bf16[512,256]{1,0:T(8,128)(2,1)S(1)}, bf16[512,256]{1,0:T(8,128)(2,1)S(1)}, u32[]{:S(2)}, u32[]{:S(2)}) collective-permute-start(bf16[512,256]{1,0:T(8,128)(2,1)S(1)} %collective-permute-done.4.refs_7_), channel_id=1, source_target_pairs={{0,2},{2,4},{4,6},{6,7},{7,5},{5,3},{3,1},{1,0},{8,10},{10,12},{12... | collective-permute-start | bytes 786440 | tf_op jit(solution)/shard_map/ppermute | solution.py:235
  31.8 5.3 %all-to-all-start = ((bf16[8,64,256]{2,1,0:T(8,128)(2,1)}), bf16[8,64,256]{2,1,0:T(8,128)(2,1)}, u32[]{:S(2)}, u32[]{:S(2)}) async-start(bf16[8,64,256]{2,1,0:T(8,128)(2,1)} %bitcast.2.start), calls=%async_computation | async-start | bytes 524288 | tf_op jit(solution)/shard_map/all_to_all | solution.py:229
  37.1 2.9 %collective-permute-start.13 = (bf16[512,256]{1,0:T(8,128)(2,1)S(1)}, bf16[512,256]{1,0:T(8,128)(2,1)S(1)}, u32[]{:S(2)}, u32[]{:S(2)}) collective-permute-start(bf16[512,256]{1,0:T(8,128)(2,1)S(1)} %collective-permute-done.5.refs_8_), channel_id=1, source_target_pairs={{0,8},{16,24},{8,0},{24,16},{1,9},{17,25},{9,1},{25,17},{2,10},{18... | collective-permute-start | bytes 786440 | tf_op jit(solution)/shard_map/ppermute | solution.py:242
  40.7 2.2 %collective-permute-start.12 = (bf16[512,256]{1,0:T(8,128)(2,1)S(1)}, bf16[512,256]{1,0:T(8,128)(2,1)S(1)}, u32[]{:S(2)}, u32[]{:S(2)}) collective-permute-start(bf16[512,256]{1,0:T(8,128)(2,1)S(1)} %collective-permute-done.4.refs_7_), channel_id=1, source_target_pairs={{0,8},{16,24},{8,0},{24,16},{1,9},{17,25},{9,1},{25,17},{2,10},{18... | collective-permute-start | bytes 786440 | tf_op jit(solution)/shard_map/ppermute | solution.py:242
  43.6 2.2 %collective-permute-start.14 = (bf16[512,256]{1,0:T(8,128)(2,1)S(1)}, bf16[512,256]{1,0:T(8,128)(2,1)}, u32[]{:S(2)}, u32[]{:S(2)}) collective-permute-start(bf16[512,256]{1,0:T(8,128)(2,1)S(1)} %collective-permute-done.6.refs_9_), channel_id=1, source_target_pairs={{0,8},{16,24},{8,0},{24,16},{1,9},{17,25},{9,1},{25,17},{2,10},{18... | collective-permute-start | bytes 786440 | tf_op jit(solution)/shard_map/ppermute | solution.py:242
  47.1 9.6 %maps.1 = (f32[2,64,768]{2,1,0:T(8,128)}, f32[2,64,768]{2,1,0:T(8,128)}, bf16[8,144,256]{2,1,0:T(8,128)(2,1)}, f32[8,128]{1,0:T(8,128)}) custom-call(s32[2,3]{1,0:T(2,128)} %refs_0_.1, bf16[8,64,256]{2,1,0:T(8,128)(2,1)} %all-to-all-done.refs_1_, bf16[512,256]{1,0:T(8,128)(2,1)S(1)} %bitcast.16, bf16[512,256]{1,0:T(8,128)(2,1)S(1)} %collective-permute-done.refs_3_, ...), custom_call_target="tpu_custom_call" | custom-call | tf_op jit(solution)/shard_map/maps/pallas_call | solution.py:252
  56.8 5.8 %all-to-all-start.1 = ((bf16[8,144,256]{2,1,0:T(8,128)(2,1)}), bf16[8,144,256]{2,1,0:T(8,128)(2,1)S(1)}, u32[]{:S(2)}, u32[]{:S(2)}) async-start(bf16[8,144,256]{2,1,0:T(8,128)(2,1)} %get-tuple-element.7), calls=%async_computation.1 | async-start | bytes 1179648 | tf_op jit(solution)/shard_map/all_to_all | solution.py:278
  63.5 4.3 %collective-permute-start.24 = (f32[8,128]{1,0:T(8,128)S(1)}, f32[8,128]{1,0:T(8,128)S(1)}, u32[]{:S(2)}, u32[]{:S(2)}) collective-permute-start(f32[8,128]{1,0:T(8,128)S(1)} %copy-done.10), channel_id=1, source_target_pairs={{0,16},{8,24},{16,0},{24,8},{1,17},{9,25},{17,1},{25,9},{2,18},{10... | collective-permute-start | bytes 12296 | tf_op jit(solution)/shard_map/ppermute | solution.py:208
  67.8 1.6 %collective-permute-done.24 = f32[8,128]{1,0:T(8,128)S(1)} collective-permute-done((f32[8,128]{1,0:T(8,128)S(1)}, f32[8,128]{1,0:T(8,128)S(1)}, u32[]{:S(2)}, u32[]{:S(2)}) %collective-permute-start.24) | collective-permute-done | bytes 4128 | tf_op jit(solution)/shard_map/ppermute | solution.py:208
  69.4 2.6 %collective-permute-start.28 = (f32[8,128]{1,0:T(8,128)S(1)}, f32[8,128]{1,0:T(8,128)S(1)}, u32[]{:S(2)}, u32[]{:S(2)}) collective-permute-start(f32[8,128]{1,0:T(8,128)S(1)} %add_add_fusion.1), channel_id=1, source_target_pairs={{0,3},{1,2},{2,1},{3,0},{4,7},{5,6},{6,5},{7,4},{8,11},{9,10},{10,... | collective-permute-start | bytes 12296 | tf_op jit(solution)/shard_map/ppermute | solution.py:208
  74.1 1.9 %collective-permute-done.27 = f32[8,128]{1,0:T(8,128)S(1)} collective-permute-done((f32[8,128]{1,0:T(8,128)S(1)}, f32[8,128]{1,0:T(8,128)S(1)}, u32[]{:S(2)}, u32[]{:S(2)}) %collective-permute-start.27) | collective-permute-done | bytes 4128 | tf_op jit(solution)/shard_map/ppermute | solution.py:208
  76.2 2.4 %collective-permute-start.29 = (f32[8,128]{1,0:T(8,128)S(1)}, f32[8,128]{1,0:T(8,128)S(1)}, u32[]{:S(2)}, u32[]{:S(2)}) collective-permute-start(f32[8,128]{1,0:T(8,128)S(1)} %add_add_fusion), channel_id=1, source_target_pairs={{0,4},{1,5},{2,6},{3,7},{4,0},{5,1},{6,2},{7,3},{8,12},{9,13},{10,... | collective-permute-start | bytes 12296 | tf_op jit(solution)/shard_map/ppermute | solution.py:208
  78.6 2.1 %collective-permute-done.29 = f32[8,128]{1,0:T(8,128)S(1)} collective-permute-done((f32[8,128]{1,0:T(8,128)S(1)}, f32[8,128]{1,0:T(8,128)S(1)}, u32[]{:S(2)}, u32[]{:S(2)}) %collective-permute-start.29) | collective-permute-done | bytes 4128 | tf_op jit(solution)/shard_map/ppermute | solution.py:208
  80.8 2.5 %combine.1 = (f32[32,2,3,2,256]{4,3,2,1,0:T(2,128)}, f32[512,2,128]{2,1,0:T(2,128)}) custom-call(f32[8,128]{1,0:T(8,128)S(1)} %add.27.sums, bf16[8,144,256]{2,1,0:T(8,128)(2,1)S(1)} %all-to-all-done.1.images, f32[2,64,768]{2,1,0:T(8,128)S(1)} %copy-done, f32[2,64,768]{2,1,0:T(8,128)S(1)} %copy-done.1, bf16[8,64,256]{2,1,0:T(8,128)(2,1)} %bitcast.2.start), custom_call_target="tpu_custom_call" | custom-call | tf_op jit(solution)/shard_map/combine/pallas_call | solution.py:281
  (70 shorter events, 13.2 us)
Async XLA Ops:
  1.7 9.4 %collective-permute-start.1 = (bf16[512,256]{1,0:T(8,128)(2,1)S(1)}, bf16[512,256]{1,0:T(8,128)(2,1)S(1)}, u32[]{:S(2)}, u32[]{:S(2)}) collective-permute-start(bf16[512,256]{1,0:T(8,128)(2,1)S(1)} %bitcast.12), channel_id=1, source_target_pairs={{2,0},{4,2},{6,4},{7,6},{5,7},{3,5},{1,3},{0,1},{10,8},{12,10},{14... | collective-permute-start | bytes 786440 | tf_op jit(solution)/shard_map/ppermute | solution.py:239
  4.7 8.8 %collective-permute-start = (bf16[512,256]{1,0:T(8,128)(2,1)S(1)}, bf16[512,256]{1,0:T(8,128)(2,1)S(1)}, u32[]{:S(2)}, u32[]{:S(2)}) collective-permute-start(bf16[512,256]{1,0:T(8,128)(2,1)S(1)} %bitcast.13), channel_id=1, source_target_pairs={{0,2},{2,4},{4,6},{6,7},{7,5},{5,3},{3,1},{1,0},{8,10},{10,12},{12... | collective-permute-start | bytes 786440 | tf_op jit(solution)/shard_map/ppermute | solution.py:235
  4.8 9.0 %collective-permute-start.15 = (bf16[512,256]{1,0:T(8,128)(2,1)S(1)}, bf16[512,256]{1,0:T(8,128)(2,1)S(1)}, u32[]{:S(2)}, u32[]{:S(2)}) collective-permute-start(bf16[512,256]{1,0:T(8,128)(2,1)S(1)} %bitcast.14), channel_id=1, source_target_pairs={{8,16},{16,8},{9,17},{17,9},{10,18},{18,10},{11,19},{19,11},{12,20... | collective-permute-start | bytes 786440 | tf_op jit(solution)/shard_map/ppermute | solution.py:243
  5.5 10.8 %collective-permute-start.7 = (bf16[512,256]{1,0:T(8,128)(2,1)S(1)}, bf16[512,256]{1,0:T(8,128)(2,1)S(1)}, u32[]{:S(2)}, u32[]{:S(2)}) collective-permute-start(bf16[512,256]{1,0:T(8,128)(2,1)S(1)} %bitcast.15), channel_id=1, source_target_pairs={{0,8},{16,24},{8,0},{24,16},{1,9},{17,25},{9,1},{25,17},{2,10},{18... | collective-permute-start | bytes 786440 | tf_op jit(solution)/shard_map/ppermute | solution.py:242
  11.1 5.9 %collective-permute-start.17 = (bf16[512,256]{1,0:T(8,128)(2,1)S(1)}, bf16[512,256]{1,0:T(8,128)(2,1)S(1)}, u32[]{:S(2)}, u32[]{:S(2)}) collective-permute-start(bf16[512,256]{1,0:T(8,128)(2,1)S(1)} %collective-permute-done.1.refs_4_), channel_id=1, source_target_pairs={{8,16},{16,8},{9,17},{17,9},{10,18},{18,10},{11,19},{19,11},{12,20... | collective-permute-start | bytes 786440 | tf_op jit(solution)/shard_map/ppermute | solution.py:243
  11.7 7.4 %collective-permute-start.3 = (bf16[512,256]{1,0:T(8,128)(2,1)S(1)}, bf16[512,256]{1,0:T(8,128)(2,1)S(1)}, u32[]{:S(2)}, u32[]{:S(2)}) collective-permute-start(bf16[512,256]{1,0:T(8,128)(2,1)S(1)} %collective-permute-done.1.refs_4_), channel_id=1, source_target_pairs={{2,0},{4,2},{6,4},{7,6},{5,7},{3,5},{1,3},{0,1},{10,8},{12,10},{14... | collective-permute-start | bytes 786440 | tf_op jit(solution)/shard_map/ppermute | solution.py:239
  13.4 7.5 %collective-permute-start.2 = (bf16[512,256]{1,0:T(8,128)(2,1)S(1)}, bf16[512,256]{1,0:T(8,128)(2,1)S(1)}, u32[]{:S(2)}, u32[]{:S(2)}) collective-permute-start(bf16[512,256]{1,0:T(8,128)(2,1)S(1)} %collective-permute-done.refs_3_), channel_id=1, source_target_pairs={{0,2},{2,4},{4,6},{6,7},{7,5},{5,3},{3,1},{1,0},{8,10},{10,12},{12... | collective-permute-start | bytes 786440 | tf_op jit(solution)/shard_map/ppermute | solution.py:235
  13.8 7.7 %collective-permute-start.9 = (bf16[512,256]{1,0:T(8,128)(2,1)S(1)}, bf16[512,256]{1,0:T(8,128)(2,1)S(1)}, u32[]{:S(2)}, u32[]{:S(2)}) collective-permute-start(bf16[512,256]{1,0:T(8,128)(2,1)S(1)} %collective-permute-done.1.refs_4_), channel_id=1, source_target_pairs={{0,8},{16,24},{8,0},{24,16},{1,9},{17,25},{9,1},{25,17},{2,10},{18... | collective-permute-start | bytes 786440 | tf_op jit(solution)/shard_map/ppermute | solution.py:242
  16.3 6.7 %collective-permute-start.16 = (bf16[512,256]{1,0:T(8,128)(2,1)S(1)}, bf16[512,256]{1,0:T(8,128)(2,1)S(1)}, u32[]{:S(2)}, u32[]{:S(2)}) collective-permute-start(bf16[512,256]{1,0:T(8,128)(2,1)S(1)} %collective-permute-done.refs_3_), channel_id=1, source_target_pairs={{8,16},{16,8},{9,17},{17,9},{10,18},{18,10},{11,19},{19,11},{12,20... | collective-permute-start | bytes 786440 | tf_op jit(solution)/shard_map/ppermute | solution.py:243
  17.0 7.7 %collective-permute-start.8 = (bf16[512,256]{1,0:T(8,128)(2,1)S(1)}, bf16[512,256]{1,0:T(8,128)(2,1)S(1)}, u32[]{:S(2)}, u32[]{:S(2)}) collective-permute-start(bf16[512,256]{1,0:T(8,128)(2,1)S(1)} %collective-permute-done.refs_3_), channel_id=1, source_target_pairs={{0,8},{16,24},{8,0},{24,16},{1,9},{17,25},{9,1},{25,17},{2,10},{18... | collective-permute-start | bytes 786440 | tf_op jit(solution)/shard_map/ppermute | solution.py:242
  19.1 6.9 %collective-permute-start.19 = (bf16[512,256]{1,0:T(8,128)(2,1)S(1)}, bf16[512,256]{1,0:T(8,128)(2,1)S(1)}, u32[]{:S(2)}, u32[]{:S(2)}) collective-permute-start(bf16[512,256]{1,0:T(8,128)(2,1)S(1)} %collective-permute-done.3.refs_6_), channel_id=1, source_target_pairs={{8,16},{16,8},{9,17},{17,9},{10,18},{18,10},{11,19},{19,11},{12,20... | collective-permute-start | bytes 786440 | tf_op jit(solution)/shard_map/ppermute | solution.py:243
  20.9 8.0 %collective-permute-start.4 = (bf16[512,256]{1,0:T(8,128)(2,1)S(1)}, bf16[512,256]{1,0:T(8,128)(2,1)S(1)}, u32[]{:S(2)}, u32[]{:S(2)}) collective-permute-start(bf16[512,256]{1,0:T(8,128)(2,1)S(1)} %collective-permute-done.2.refs_5_), channel_id=1, source_target_pairs={{0,2},{2,4},{4,6},{6,7},{7,5},{5,3},{3,1},{1,0},{8,10},{10,12},{12... | collective-permute-start | bytes 786440 | tf_op jit(solution)/shard_map/ppermute | solution.py:235
  21.5 8.8 %collective-permute-start.5 = (bf16[512,256]{1,0:T(8,128)(2,1)S(1)}, bf16[512,256]{1,0:T(8,128)(2,1)S(1)}, u32[]{:S(2)}, u32[]{:S(2)}) collective-permute-start(bf16[512,256]{1,0:T(8,128)(2,1)S(1)} %collective-permute-done.3.refs_6_), channel_id=1, source_target_pairs={{2,0},{4,2},{6,4},{7,6},{5,7},{3,5},{1,3},{0,1},{10,8},{12,10},{14... | collective-permute-start | bytes 786440 | tf_op jit(solution)/shard_map/ppermute | solution.py:239
  23.0 14.2 %collective-permute-start.11 = (bf16[512,256]{1,0:T(8,128)(2,1)S(1)}, bf16[512,256]{1,0:T(8,128)(2,1)}, u32[]{:S(2)}, u32[]{:S(2)}) collective-permute-start(bf16[512,256]{1,0:T(8,128)(2,1)S(1)} %collective-permute-done.3.refs_6_), channel_id=1, source_target_pairs={{0,8},{16,24},{8,0},{24,16},{1,9},{17,25},{9,1},{25,17},{2,10},{18... | collective-permute-start | bytes 786440 | tf_op jit(solution)/shard_map/ppermute | solution.py:242
  24.6 15.4 %collective-permute-start.18 = (bf16[512,256]{1,0:T(8,128)(2,1)S(1)}, bf16[512,256]{1,0:T(8,128)(2,1)}, u32[]{:S(2)}, u32[]{:S(2)}) collective-permute-start(bf16[512,256]{1,0:T(8,128)(2,1)S(1)} %collective-permute-done.2.refs_5_), channel_id=1, source_target_pairs={{8,16},{16,8},{9,17},{17,9},{10,18},{18,10},{11,19},{19,11},{12,20... | collective-permute-start | bytes 786440 | tf_op jit(solution)/shard_map/ppermute | solution.py:243
  26.0 14.7 %collective-permute-start.10 = (bf16[512,256]{1,0:T(8,128)(2,1)S(1)}, bf16[512,256]{1,0:T(8,128)(2,1)}, u32[]{:S(2)}, u32[]{:S(2)}) collective-permute-start(bf16[512,256]{1,0:T(8,128)(2,1)S(1)} %collective-permute-done.2.refs_5_), channel_id=1, source_target_pairs={{0,8},{16,24},{8,0},{24,16},{1,9},{17,25},{9,1},{25,17},{2,10},{18... | collective-permute-start | bytes 786440 | tf_op jit(solution)/shard_map/ppermute | solution.py:242
  28.9 13.9 %collective-permute-start.6 = (bf16[512,256]{1,0:T(8,128)(2,1)S(1)}, bf16[512,256]{1,0:T(8,128)(2,1)S(1)}, u32[]{:S(2)}, u32[]{:S(2)}) collective-permute-start(bf16[512,256]{1,0:T(8,128)(2,1)S(1)} %collective-permute-done.4.refs_7_), channel_id=1, source_target_pairs={{0,2},{2,4},{4,6},{6,7},{7,5},{5,3},{3,1},{1,0},{8,10},{10,12},{12... | collective-permute-start | bytes 786440 | tf_op jit(solution)/shard_map/ppermute | solution.py:235
  30.3 13.3 %collective-permute-start.21 = (bf16[512,256]{1,0:T(8,128)(2,1)S(1)}, bf16[512,256]{1,0:T(8,128)(2,1)S(1)}, u32[]{:S(2)}, u32[]{:S(2)}) collective-permute-start(bf16[512,256]{1,0:T(8,128)(2,1)S(1)} %collective-permute-done.5.refs_8_), channel_id=1, source_target_pairs={{8,16},{16,8},{9,17},{17,9},{10,18},{18,10},{11,19},{19,11},{12,20... | collective-permute-start | bytes 786440 | tf_op jit(solution)/shard_map/ppermute | solution.py:243
  31.8 14.0 %all-to-all-start = ((bf16[8,64,256]{2,1,0:T(8,128)(2,1)}), bf16[8,64,256]{2,1,0:T(8,128)(2,1)}, u32[]{:S(2)}, u32[]{:S(2)}) async-start(bf16[8,64,256]{2,1,0:T(8,128)(2,1)} %bitcast.2.start), calls=%async_computation | async-start | bytes 524288 | tf_op jit(solution)/shard_map/all_to_all | solution.py:229
  37.1 8.7 %collective-permute-start.13 = (bf16[512,256]{1,0:T(8,128)(2,1)S(1)}, bf16[512,256]{1,0:T(8,128)(2,1)S(1)}, u32[]{:S(2)}, u32[]{:S(2)}) collective-permute-start(bf16[512,256]{1,0:T(8,128)(2,1)S(1)} %collective-permute-done.5.refs_8_), channel_id=1, source_target_pairs={{0,8},{16,24},{8,0},{24,16},{1,9},{17,25},{9,1},{25,17},{2,10},{18... | collective-permute-start | bytes 786440 | tf_op jit(solution)/shard_map/ppermute | solution.py:242
  40.0 5.8 %collective-permute-start.20 = (bf16[512,256]{1,0:T(8,128)(2,1)S(1)}, bf16[512,256]{1,0:T(8,128)(2,1)S(1)}, u32[]{:S(2)}, u32[]{:S(2)}) collective-permute-start(bf16[512,256]{1,0:T(8,128)(2,1)S(1)} %collective-permute-done.4.refs_7_), channel_id=1, source_target_pairs={{8,16},{16,8},{9,17},{17,9},{10,18},{18,10},{11,19},{19,11},{12,20... | collective-permute-start | bytes 786440 | tf_op jit(solution)/shard_map/ppermute | solution.py:243
  56.8 24.0 %all-to-all-start.1 = ((bf16[8,144,256]{2,1,0:T(8,128)(2,1)}), bf16[8,144,256]{2,1,0:T(8,128)(2,1)S(1)}, u32[]{:S(2)}, u32[]{:S(2)}) async-start(bf16[8,144,256]{2,1,0:T(8,128)(2,1)} %get-tuple-element.7), calls=%async_computation.1 | async-start | bytes 1179648 | tf_op jit(solution)/shard_map/all_to_all | solution.py:278
  62.6 5.2 %collective-permute-start.25 = (f32[8,128]{1,0:T(8,128)S(1)}, f32[8,128]{1,0:T(8,128)S(1)}, u32[]{:S(2)}, u32[]{:S(2)}) collective-permute-start(f32[8,128]{1,0:T(8,128)S(1)} %copy-done.10), channel_id=1, source_target_pairs={{0,24},{8,16},{16,8},{24,0},{1,25},{9,17},{17,9},{25,1},{2,26},{10... | collective-permute-start | bytes 12296 | tf_op jit(solution)/shard_map/ppermute | solution.py:208
  63.5 5.9 %collective-permute-start.24 = (f32[8,128]{1,0:T(8,128)S(1)}, f32[8,128]{1,0:T(8,128)S(1)}, u32[]{:S(2)}, u32[]{:S(2)}) collective-permute-start(f32[8,128]{1,0:T(8,128)S(1)} %copy-done.10), channel_id=1, source_target_pairs={{0,16},{8,24},{16,0},{24,8},{1,17},{9,25},{17,1},{25,9},{2,18},{10... | collective-permute-start | bytes 12296 | tf_op jit(solution)/shard_map/ppermute | solution.py:208
  (19 other events, 189.2 us)

commit v5 on v4

--- a/solution.py
+++ b/solution.py
@@ -14,7 +14,7 @@
 SHARE_ROWS = 16
 PAIR = 2
 IN_PLACE = 8
-LATE = 3
+LATE = 4
 
 
 def ring_order(count):
@@ -271,7 +271,7 @@
             pltpu.SemaphoreType.DMA((3, n_src)),
             pltpu.SemaphoreType.DMA,
         ],
-        compiler_params=pltpu.CompilerParams(vmem_limit_bytes=56 << 20),
+        compiler_params=pltpu.CompilerParams(vmem_limit_bytes=55 << 20),
         name="maps",
     )(band, field, *gathered)
 

time: 83.8 us -> 84.1 us (level)
  no operation moved by 1% of the time
where the time goes in v5:
time: 84.1 us; the launch traced here: 83.5 us
  starting transfers between devices  56.8 us (68%)
  Pallas kernels  12.2 us (15%)
  waiting for transfers between devices  11.7 us (14%)
  local copies, waits for them, and re-layouts  1.85 us (2%)
  between operations  0.88 us (1%)
    ppermute x8, starting transfers between devices, per_device(): near = [lax.ppermute(c, 'rcv', swaps(0)) for c in chunks]  19.1 us
    ppermute x7, starting transfers between devices, summed(): lax.ppermute(x, axis, [(d, d ^ bit * m) for d in range(count)])  11.2 us
    pallas_call x1, Pallas kernels, per_device(): pl.pallas_call(functools.partial(maps_kernel, n_src, shifts), out_shape=(...  9.77 us
    ppermute x7, waiting for transfers between devices, summed(): lax.ppermute(x, axis, [(d, d ^ bit * m) for d in range(count)])  7.01 us
    ppermute x8, starting transfers between devices, per_device(): far = [lax.ppermute(c, 'rcv', swaps(1)) for c in chunks]  6.72 us
    ppermute x3, starting transfers between devices, per_device(): bwd = lax.ppermute(bwd, 'src', behind)  6.19 us
    all_to_all x1, starting transfers between devices, per_device(): images = lax.all_to_all(images, 'src', 0, 0, tiled=True)  5.78 us
    all_to_all x1, starting transfers between devices, per_device(): field = lax.all_to_all(start, 'src', 0, 0, tiled=True)  5.29 us
  transfers between devices with their start and end apart: 32, of which 8 were waited for; matrix products, arithmetic and copies ran while one was open for 1% of the time, Pallas kernels for 0%

profile of v5, /device:TPU:0, one launch (start us, length us, event | category | flops | bytes accessed | tf_op | source)
XLA Modules:
  0.0 83.5 jit_solution(10716330675160714861)
XLA Ops:
  1.7 3.0 %collective-permute-start.1 = (bf16[512,256]{1,0:T(8,128)(2,1)S(1)}, bf16[512,256]{1,0:T(8,128)(2,1)S(1)}, u32[]{:S(2)}, u32[]{:S(2)}) collective-permute-start(bf16[512,256]{1,0:T(8,128)(2,1)S(1)} %bitcast.12), channel_id=1, source_target_pairs={{2,0},{4,2},{6,4},{7,6},{5,7},{3,5},{1,3},{0,1},{10,8},{12,10},{14... | collective-permute-start | bytes 786440 | tf_op jit(solution)/shard_map/ppermute | solution.py:239
  5.5 3.3 %collective-permute-start.7 = (bf16[512,256]{1,0:T(8,128)(2,1)S(1)}, bf16[512,256]{1,0:T(8,128)(2,1)S(1)}, u32[]{:S(2)}, u32[]{:S(2)}) collective-permute-start(bf16[512,256]{1,0:T(8,128)(2,1)S(1)} %bitcast.15), channel_id=1, source_target_pairs={{0,8},{16,24},{8,0},{24,16},{1,9},{17,25},{9,1},{25,17},{2,10},{18... | collective-permute-start | bytes 786440 | tf_op jit(solution)/shard_map/ppermute | solution.py:242
  8.8 2.3 %collective-permute-done.1.refs_4_ = bf16[512,256]{1,0:T(8,128)(2,1)S(1)} collective-permute-done((bf16[512,256]{1,0:T(8,128)(2,1)S(1)}, bf16[512,256]{1,0:T(8,128)(2,1)S(1)}, u32[]{:S(2)}, u32[]{:S(2)}) %collective-permute-start.1) | collective-permute-done | bytes 262176 | tf_op jit(solution)/shard_map/ppermute | solution.py:239
  11.7 1.7 %collective-permute-start.3 = (bf16[512,256]{1,0:T(8,128)(2,1)S(1)}, bf16[512,256]{1,0:T(8,128)(2,1)S(1)}, u32[]{:S(2)}, u32[]{:S(2)}) collective-permute-start(bf16[512,256]{1,0:T(8,128)(2,1)S(1)} %collective-permute-done.1.refs_4_), channel_id=1, source_target_pairs={{2,0},{4,2},{6,4},{7,6},{5,7},{3,5},{1,3},{0,1},{10,8},{12,10},{14... | collective-permute-start | bytes 786440 | tf_op jit(solution)/shard_map/ppermute | solution.py:239
  13.8 2.5 %collective-permute-start.9 = (bf16[512,256]{1,0:T(8,128)(2,1)S(1)}, bf16[512,256]{1,0:T(8,128)(2,1)S(1)}, u32[]{:S(2)}, u32[]{:S(2)}) collective-permute-start(bf16[512,256]{1,0:T(8,128)(2,1)S(1)} %collective-permute-done.1.refs_4_), channel_id=1, source_target_pairs={{0,8},{16,24},{8,0},{24,16},{1,9},{17,25},{9,1},{25,17},{2,10},{18... | collective-permute-start | bytes 786440 | tf_op jit(solution)/shard_map/ppermute | solution.py:242
  17.0 2.1 %collective-permute-start.8 = (bf16[512,256]{1,0:T(8,128)(2,1)S(1)}, bf16[512,256]{1,0:T(8,128)(2,1)S(1)}, u32[]{:S(2)}, u32[]{:S(2)}) collective-permute-start(bf16[512,256]{1,0:T(8,128)(2,1)S(1)} %collective-permute-done.refs_3_), channel_id=1, source_target_pairs={{0,8},{16,24},{8,0},{24,16},{1,9},{17,25},{9,1},{25,17},{2,10},{18... | collective-permute-start | bytes 786440 | tf_op jit(solution)/shard_map/ppermute | solution.py:242
  21.5 1.5 %collective-permute-start.5 = (bf16[512,256]{1,0:T(8,128)(2,1)S(1)}, bf16[512,256]{1,0:T(8,128)(2,1)S(1)}, u32[]{:S(2)}, u32[]{:S(2)}) collective-permute-start(bf16[512,256]{1,0:T(8,128)(2,1)S(1)} %collective-permute-done.3.refs_6_), channel_id=1, source_target_pairs={{2,0},{4,2},{6,4},{7,6},{5,7},{3,5},{1,3},{0,1},{10,8},{12,10},{14... | collective-permute-start | bytes 786440 | tf_op jit(solution)/shard_map/ppermute | solution.py:239
  23.0 1.7 %collective-permute-start.11 = (bf16[512,256]{1,0:T(8,128)(2,1)S(1)}, bf16[512,256]{1,0:T(8,128)(2,1)S(1)}, u32[]{:S(2)}, u32[]{:S(2)}) collective-permute-start(bf16[512,256]{1,0:T(8,128)(2,1)S(1)} %collective-permute-done.3.refs_6_), channel_id=1, source_target_pairs={{0,8},{16,24},{8,0},{24,16},{1,9},{17,25},{9,1},{25,17},{2,10},{18... | collective-permute-start | bytes 786440 | tf_op jit(solution)/shard_map/ppermute | solution.py:242
  24.6 1.4 %collective-permute-start.18 = (bf16[512,256]{1,0:T(8,128)(2,1)S(1)}, bf16[512,256]{1,0:T(8,128)(2,1)}, u32[]{:S(2)}, u32[]{:S(2)}) collective-permute-start(bf16[512,256]{1,0:T(8,128)(2,1)S(1)} %collective-permute-done.2.refs_5_), channel_id=1, source_target_pairs={{8,16},{16,8},{9,17},{17,9},{10,18},{18,10},{11,19},{19,11},{12,20... | collective-permute-start | bytes 786440 | tf_op jit(solution)/shard_map/ppermute | solution.py:243
  26.0 2.9 %collective-permute-start.10 = (bf16[512,256]{1,0:T(8,128)(2,1)S(1)}, bf16[512,256]{1,0:T(8,128)(2,1)}, u32[]{:S(2)}, u32[]{:S(2)}) collective-permute-start(bf16[512,256]{1,0:T(8,128)(2,1)S(1)} %collective-permute-done.2.refs_5_), channel_id=1, source_target_pairs={{0,8},{16,24},{8,0},{24,16},{1,9},{17,25},{9,1},{25,17},{2,10},{18... | collective-permute-start | bytes 786440 | tf_op jit(solution)/shard_map/ppermute | solution.py:242
  31.8 5.3 %all-to-all-start = ((bf16[8,64,256]{2,1,0:T(8,128)(2,1)}), bf16[8,64,256]{2,1,0:T(8,128)(2,1)}, u32[]{:S(2)}, u32[]{:S(2)}) async-start(bf16[8,64,256]{2,1,0:T(8,128)(2,1)} %bitcast.2.start), calls=%async_computation | async-start | bytes 524288 | tf_op jit(solution)/shard_map/all_to_all | solution.py:229
  37.1 2.9 %collective-permute-start.13 = (bf16[512,256]{1,0:T(8,128)(2,1)S(1)}, bf16[512,256]{1,0:T(8,128)(2,1)S(1)}, u32[]{:S(2)}, u32[]{:S(2)}) collective-permute-start(bf16[512,256]{1,0:T(8,128)(2,1)S(1)} %collective-permute-done.5.refs_8_), channel_id=1, source_target_pairs={{0,8},{16,24},{8,0},{24,16},{1,9},{17,25},{9,1},{25,17},{2,10},{18... | collective-permute-start | bytes 786440 | tf_op jit(solution)/shard_map/ppermute | solution.py:242
  40.7 2.2 %collective-permute-start.12 = (bf16[512,256]{1,0:T(8,128)(2,1)S(1)}, bf16[512,256]{1,0:T(8,128)(2,1)}, u32[]{:S(2)}, u32[]{:S(2)}) collective-permute-start(bf16[512,256]{1,0:T(8,128)(2,1)S(1)} %collective-permute-done.4.refs_7_), channel_id=1, source_target_pairs={{0,8},{16,24},{8,0},{24,16},{1,9},{17,25},{9,1},{25,17},{2,10},{18... | collective-permute-start | bytes 786440 | tf_op jit(solution)/shard_map/ppermute | solution.py:242
  42.9 1.4 %collective-permute-start.22 = (bf16[512,256]{1,0:T(8,128)(2,1)S(1)}, bf16[512,256]{1,0:T(8,128)(2,1)}, u32[]{:S(2)}, u32[]{:S(2)}) collective-permute-start(bf16[512,256]{1,0:T(8,128)(2,1)S(1)} %collective-permute-done.6.refs_9_), channel_id=1, source_target_pairs={{8,16},{16,8},{9,17},{17,9},{10,18},{18,10},{11,19},{19,11},{12,20... | collective-permute-start | bytes 786440 | tf_op jit(solution)/shard_map/ppermute | solution.py:243
  44.2 1.6 %collective-permute-start.14 = (bf16[512,256]{1,0:T(8,128)(2,1)S(1)}, bf16[512,256]{1,0:T(8,128)(2,1)}, u32[]{:S(2)}, u32[]{:S(2)}) collective-permute-start(bf16[512,256]{1,0:T(8,128)(2,1)S(1)} %collective-permute-done.6.refs_9_), channel_id=1, source_target_pairs={{0,8},{16,24},{8,0},{24,16},{1,9},{17,25},{9,1},{25,17},{2,10},{18... | collective-permute-start | bytes 786440 | tf_op jit(solution)/shard_map/ppermute | solution.py:242
  47.1 9.8 %maps.1 = (f32[2,64,768]{2,1,0:T(8,128)}, f32[2,64,768]{2,1,0:T(8,128)}, bf16[8,144,256]{2,1,0:T(8,128)(2,1)}, f32[8,128]{1,0:T(8,128)}) custom-call(s32[2,3]{1,0:T(2,128)} %refs_0_.1, bf16[8,64,256]{2,1,0:T(8,128)(2,1)} %all-to-all-done.refs_1_, bf16[512,256]{1,0:T(8,128)(2,1)S(1)} %bitcast.16, bf16[512,256]{1,0:T(8,128)(2,1)S(1)} %collective-permute-done.refs_3_, ...), custom_call_target="tpu_custom_call" | custom-call | tf_op jit(solution)/shard_map/maps/pallas_call | solution.py:252
  56.9 5.8 %all-to-all-start.1 = ((bf16[8,144,256]{2,1,0:T(8,128)(2,1)}), bf16[8,144,256]{2,1,0:T(8,128)(2,1)S(1)}, u32[]{:S(2)}, u32[]{:S(2)}) async-start(bf16[8,144,256]{2,1,0:T(8,128)(2,1)} %get-tuple-element.7), calls=%async_computation.1 | async-start | bytes 1179648 | tf_op jit(solution)/shard_map/all_to_all | solution.py:278
  63.6 4.4 %collective-permute-start.24 = (f32[8,128]{1,0:T(8,128)S(1)}, f32[8,128]{1,0:T(8,128)S(1)}, u32[]{:S(2)}, u32[]{:S(2)}) collective-permute-start(f32[8,128]{1,0:T(8,128)S(1)} %copy-done.9), channel_id=1, source_target_pairs={{0,16},{8,24},{16,0},{24,8},{1,17},{9,25},{17,1},{25,9},{2,18},{10... | collective-permute-start | bytes 12296 | tf_op jit(solution)/shard_map/ppermute | solution.py:208
  68.0 1.6 %collective-permute-done.24 = f32[8,128]{1,0:T(8,128)S(1)} collective-permute-done((f32[8,128]{1,0:T(8,128)S(1)}, f32[8,128]{1,0:T(8,128)S(1)}, u32[]{:S(2)}, u32[]{:S(2)}) %collective-permute-start.24) | collective-permute-done | bytes 4128 | tf_op jit(solution)/shard_map/ppermute | solution.py:208
  69.7 2.6 %collective-permute-start.28 = (f32[8,128]{1,0:T(8,128)S(1)}, f32[8,128]{1,0:T(8,128)S(1)}, u32[]{:S(2)}, u32[]{:S(2)}) collective-permute-start(f32[8,128]{1,0:T(8,128)S(1)} %add_add_fusion.1), channel_id=1, source_target_pairs={{0,3},{1,2},{2,1},{3,0},{4,7},{5,6},{6,5},{7,4},{8,11},{9,10},{10,... | collective-permute-start | bytes 12296 | tf_op jit(solution)/shard_map/ppermute | solution.py:208
  74.4 1.8 %collective-permute-done.27 = f32[8,128]{1,0:T(8,128)S(1)} collective-permute-done((f32[8,128]{1,0:T(8,128)S(1)}, f32[8,128]{1,0:T(8,128)S(1)}, u32[]{:S(2)}, u32[]{:S(2)}) %collective-permute-start.27) | collective-permute-done | bytes 4128 | tf_op jit(solution)/shard_map/ppermute | solution.py:208
  76.5 2.4 %collective-permute-start.29 = (f32[8,128]{1,0:T(8,128)S(1)}, f32[8,128]{1,0:T(8,128)S(1)}, u32[]{:S(2)}, u32[]{:S(2)}) collective-permute-start(f32[8,128]{1,0:T(8,128)S(1)} %add_add_fusion), channel_id=1, source_target_pairs={{0,4},{1,5},{2,6},{3,7},{4,0},{5,1},{6,2},{7,3},{8,12},{9,13},{10,... | collective-permute-start | bytes 12296 | tf_op jit(solution)/shard_map/ppermute | solution.py:208
  78.9 2.1 %collective-permute-done.29 = f32[8,128]{1,0:T(8,128)S(1)} collective-permute-done((f32[8,128]{1,0:T(8,128)S(1)}, f32[8,128]{1,0:T(8,128)S(1)}, u32[]{:S(2)}, u32[]{:S(2)}) %collective-permute-start.29) | collective-permute-done | bytes 4128 | tf_op jit(solution)/shard_map/ppermute | solution.py:208
  81.0 2.5 %combine.1 = (f32[32,2,3,2,256]{4,3,2,1,0:T(2,128)}, f32[512,2,128]{2,1,0:T(2,128)}) custom-call(f32[8,128]{1,0:T(8,128)S(1)} %add.27.sums, bf16[8,144,256]{2,1,0:T(8,128)(2,1)S(1)} %all-to-all-done.1.images, f32[2,64,768]{2,1,0:T(8,128)S(1)} %copy-done, f32[2,64,768]{2,1,0:T(8,128)S(1)} %copy-done.1, bf16[8,64,256]{2,1,0:T(8,128)(2,1)} %bitcast.2.start), custom_call_target="tpu_custom_call" | custom-call | tf_op jit(solution)/shard_map/combine/pallas_call | solution.py:281
  (68 shorter events, 14.0 us)
Async XLA Ops:
  1.7 9.4 %collective-permute-start.1 = (bf16[512,256]{1,0:T(8,128)(2,1)S(1)}, bf16[512,256]{1,0:T(8,128)(2,1)S(1)}, u32[]{:S(2)}, u32[]{:S(2)}) collective-permute-start(bf16[512,256]{1,0:T(8,128)(2,1)S(1)} %bitcast.12), channel_id=1, source_target_pairs={{2,0},{4,2},{6,4},{7,6},{5,7},{3,5},{1,3},{0,1},{10,8},{12,10},{14... | collective-permute-start | bytes 786440 | tf_op jit(solution)/shard_map/ppermute | solution.py:239
  4.7 8.8 %collective-permute-start = (bf16[512,256]{1,0:T(8,128)(2,1)S(1)}, bf16[512,256]{1,0:T(8,128)(2,1)S(1)}, u32[]{:S(2)}, u32[]{:S(2)}) collective-permute-start(bf16[512,256]{1,0:T(8,128)(2,1)S(1)} %bitcast.13), channel_id=1, source_target_pairs={{0,2},{2,4},{4,6},{6,7},{7,5},{5,3},{3,1},{1,0},{8,10},{10,12},{12... | collective-permute-start | bytes 786440 | tf_op jit(solution)/shard_map/ppermute | solution.py:235
  4.8 9.0 %collective-permute-start.15 = (bf16[512,256]{1,0:T(8,128)(2,1)S(1)}, bf16[512,256]{1,0:T(8,128)(2,1)S(1)}, u32[]{:S(2)}, u32[]{:S(2)}) collective-permute-start(bf16[512,256]{1,0:T(8,128)(2,1)S(1)} %bitcast.14), channel_id=1, source_target_pairs={{8,16},{16,8},{9,17},{17,9},{10,18},{18,10},{11,19},{19,11},{12,20... | collective-permute-start | bytes 786440 | tf_op jit(solution)/shard_map/ppermute | solution.py:243
  5.5 10.8 %collective-permute-start.7 = (bf16[512,256]{1,0:T(8,128)(2,1)S(1)}, bf16[512,256]{1,0:T(8,128)(2,1)S(1)}, u32[]{:S(2)}, u32[]{:S(2)}) collective-permute-start(bf16[512,256]{1,0:T(8,128)(2,1)S(1)} %bitcast.15), channel_id=1, source_target_pairs={{0,8},{16,24},{8,0},{24,16},{1,9},{17,25},{9,1},{25,17},{2,10},{18... | collective-permute-start | bytes 786440 | tf_op jit(solution)/shard_map/ppermute | solution.py:242
  11.1 5.9 %collective-permute-start.17 = (bf16[512,256]{1,0:T(8,128)(2,1)S(1)}, bf16[512,256]{1,0:T(8,128)(2,1)S(1)}, u32[]{:S(2)}, u32[]{:S(2)}) collective-permute-start(bf16[512,256]{1,0:T(8,128)(2,1)S(1)} %collective-permute-done.1.refs_4_), channel_id=1, source_target_pairs={{8,16},{16,8},{9,17},{17,9},{10,18},{18,10},{11,19},{19,11},{12,20... | collective-permute-start | bytes 786440 | tf_op jit(solution)/shard_map/ppermute | solution.py:243
  11.7 7.4 %collective-permute-start.3 = (bf16[512,256]{1,0:T(8,128)(2,1)S(1)}, bf16[512,256]{1,0:T(8,128)(2,1)S(1)}, u32[]{:S(2)}, u32[]{:S(2)}) collective-permute-start(bf16[512,256]{1,0:T(8,128)(2,1)S(1)} %collective-permute-done.1.refs_4_), channel_id=1, source_target_pairs={{2,0},{4,2},{6,4},{7,6},{5,7},{3,5},{1,3},{0,1},{10,8},{12,10},{14... | collective-permute-start | bytes 786440 | tf_op jit(solution)/shard_map/ppermute | solution.py:239
  13.4 7.5 %collective-permute-start.2 = (bf16[512,256]{1,0:T(8,128)(2,1)S(1)}, bf16[512,256]{1,0:T(8,128)(2,1)S(1)}, u32[]{:S(2)}, u32[]{:S(2)}) collective-permute-start(bf16[512,256]{1,0:T(8,128)(2,1)S(1)} %collective-permute-done.refs_3_), channel_id=1, source_target_pairs={{0,2},{2,4},{4,6},{6,7},{7,5},{5,3},{3,1},{1,0},{8,10},{10,12},{12... | collective-permute-start | bytes 786440 | tf_op jit(solution)/shard_map/ppermute | solution.py:235
  13.8 7.7 %collective-permute-start.9 = (bf16[512,256]{1,0:T(8,128)(2,1)S(1)}, bf16[512,256]{1,0:T(8,128)(2,1)S(1)}, u32[]{:S(2)}, u32[]{:S(2)}) collective-permute-start(bf16[512,256]{1,0:T(8,128)(2,1)S(1)} %collective-permute-done.1.refs_4_), channel_id=1, source_target_pairs={{0,8},{16,24},{8,0},{24,16},{1,9},{17,25},{9,1},{25,17},{2,10},{18... | collective-permute-start | bytes 786440 | tf_op jit(solution)/shard_map/ppermute | solution.py:242
  16.3 6.7 %collective-permute-start.16 = (bf16[512,256]{1,0:T(8,128)(2,1)S(1)}, bf16[512,256]{1,0:T(8,128)(2,1)S(1)}, u32[]{:S(2)}, u32[]{:S(2)}) collective-permute-start(bf16[512,256]{1,0:T(8,128)(2,1)S(1)} %collective-permute-done.refs_3_), channel_id=1, source_target_pairs={{8,16},{16,8},{9,17},{17,9},{10,18},{18,10},{11,19},{19,11},{12,20... | collective-permute-start | bytes 786440 | tf_op jit(solution)/shard_map/ppermute | solution.py:243
  17.0 7.7 %collective-permute-start.8 = (bf16[512,256]{1,0:T(8,128)(2,1)S(1)}, bf16[512,256]{1,0:T(8,128)(2,1)S(1)}, u32[]{:S(2)}, u32[]{:S(2)}) collective-permute-start(bf16[512,256]{1,0:T(8,128)(2,1)S(1)} %collective-permute-done.refs_3_), channel_id=1, source_target_pairs={{0,8},{16,24},{8,0},{24,16},{1,9},{17,25},{9,1},{25,17},{2,10},{18... | collective-permute-start | bytes 786440 | tf_op jit(solution)/shard_map/ppermute | solution.py:242
  19.1 6.9 %collective-permute-start.19 = (bf16[512,256]{1,0:T(8,128)(2,1)S(1)}, bf16[512,256]{1,0:T(8,128)(2,1)S(1)}, u32[]{:S(2)}, u32[]{:S(2)}) collective-permute-start(bf16[512,256]{1,0:T(8,128)(2,1)S(1)} %collective-permute-done.3.refs_6_), channel_id=1, source_target_pairs={{8,16},{16,8},{9,17},{17,9},{10,18},{18,10},{11,19},{19,11},{12,20... | collective-permute-start | bytes 786440 | tf_op jit(solution)/shard_map/ppermute | solution.py:243
  20.9 8.0 %collective-permute-start.4 = (bf16[512,256]{1,0:T(8,128)(2,1)S(1)}, bf16[512,256]{1,0:T(8,128)(2,1)S(1)}, u32[]{:S(2)}, u32[]{:S(2)}) collective-permute-start(bf16[512,256]{1,0:T(8,128)(2,1)S(1)} %collective-permute-done.2.refs_5_), channel_id=1, source_target_pairs={{0,2},{2,4},{4,6},{6,7},{7,5},{5,3},{3,1},{1,0},{8,10},{10,12},{12... | collective-permute-start | bytes 786440 | tf_op jit(solution)/shard_map/ppermute | solution.py:235
  21.5 8.8 %collective-permute-start.5 = (bf16[512,256]{1,0:T(8,128)(2,1)S(1)}, bf16[512,256]{1,0:T(8,128)(2,1)S(1)}, u32[]{:S(2)}, u32[]{:S(2)}) collective-permute-start(bf16[512,256]{1,0:T(8,128)(2,1)S(1)} %collective-permute-done.3.refs_6_), channel_id=1, source_target_pairs={{2,0},{4,2},{6,4},{7,6},{5,7},{3,5},{1,3},{0,1},{10,8},{12,10},{14... | collective-permute-start | bytes 786440 | tf_op jit(solution)/shard_map/ppermute | solution.py:239
  23.0 14.1 %collective-permute-start.11 = (bf16[512,256]{1,0:T(8,128)(2,1)S(1)}, bf16[512,256]{1,0:T(8,128)(2,1)S(1)}, u32[]{:S(2)}, u32[]{:S(2)}) collective-permute-start(bf16[512,256]{1,0:T(8,128)(2,1)S(1)} %collective-permute-done.3.refs_6_), channel_id=1, source_target_pairs={{0,8},{16,24},{8,0},{24,16},{1,9},{17,25},{9,1},{25,17},{2,10},{18... | collective-permute-start | bytes 786440 | tf_op jit(solution)/shard_map/ppermute | solution.py:242
  24.6 15.4 %collective-permute-start.18 = (bf16[512,256]{1,0:T(8,128)(2,1)S(1)}, bf16[512,256]{1,0:T(8,128)(2,1)}, u32[]{:S(2)}, u32[]{:S(2)}) collective-permute-start(bf16[512,256]{1,0:T(8,128)(2,1)S(1)} %collective-permute-done.2.refs_5_), channel_id=1, source_target_pairs={{8,16},{16,8},{9,17},{17,9},{10,18},{18,10},{11,19},{19,11},{12,20... | collective-permute-start | bytes 786440 | tf_op jit(solution)/shard_map/ppermute | solution.py:243
  26.0 14.7 %collective-permute-start.10 = (bf16[512,256]{1,0:T(8,128)(2,1)S(1)}, bf16[512,256]{1,0:T(8,128)(2,1)}, u32[]{:S(2)}, u32[]{:S(2)}) collective-permute-start(bf16[512,256]{1,0:T(8,128)(2,1)S(1)} %collective-permute-done.2.refs_5_), channel_id=1, source_target_pairs={{0,8},{16,24},{8,0},{24,16},{1,9},{17,25},{9,1},{25,17},{2,10},{18... | collective-permute-start | bytes 786440 | tf_op jit(solution)/shard_map/ppermute | solution.py:242
  28.9 13.9 %collective-permute-start.6 = (bf16[512,256]{1,0:T(8,128)(2,1)S(1)}, bf16[512,256]{1,0:T(8,128)(2,1)S(1)}, u32[]{:S(2)}, u32[]{:S(2)}) collective-permute-start(bf16[512,256]{1,0:T(8,128)(2,1)S(1)} %collective-permute-done.4.refs_7_), channel_id=1, source_target_pairs={{0,2},{2,4},{4,6},{6,7},{7,5},{5,3},{3,1},{1,0},{8,10},{10,12},{12... | collective-permute-start | bytes 786440 | tf_op jit(solution)/shard_map/ppermute | solution.py:235
  30.3 13.9 %collective-permute-start.21 = (bf16[512,256]{1,0:T(8,128)(2,1)S(1)}, bf16[512,256]{1,0:T(8,128)(2,1)S(1)}, u32[]{:S(2)}, u32[]{:S(2)}) collective-permute-start(bf16[512,256]{1,0:T(8,128)(2,1)S(1)} %collective-permute-done.5.refs_8_), channel_id=1, source_target_pairs={{8,16},{16,8},{9,17},{17,9},{10,18},{18,10},{11,19},{19,11},{12,20... | collective-permute-start | bytes 786440 | tf_op jit(solution)/shard_map/ppermute | solution.py:243
  31.8 14.0 %all-to-all-start = ((bf16[8,64,256]{2,1,0:T(8,128)(2,1)}), bf16[8,64,256]{2,1,0:T(8,128)(2,1)}, u32[]{:S(2)}, u32[]{:S(2)}) async-start(bf16[8,64,256]{2,1,0:T(8,128)(2,1)} %bitcast.2.start), calls=%async_computation | async-start | bytes 524288 | tf_op jit(solution)/shard_map/all_to_all | solution.py:229
  37.1 8.7 %collective-permute-start.13 = (bf16[512,256]{1,0:T(8,128)(2,1)S(1)}, bf16[512,256]{1,0:T(8,128)(2,1)S(1)}, u32[]{:S(2)}, u32[]{:S(2)}) collective-permute-start(bf16[512,256]{1,0:T(8,128)(2,1)S(1)} %collective-permute-done.5.refs_8_), channel_id=1, source_target_pairs={{0,8},{16,24},{8,0},{24,16},{1,9},{17,25},{9,1},{25,17},{2,10},{18... | collective-permute-start | bytes 786440 | tf_op jit(solution)/shard_map/ppermute | solution.py:242
  40.0 5.8 %collective-permute-start.20 = (bf16[512,256]{1,0:T(8,128)(2,1)S(1)}, bf16[512,256]{1,0:T(8,128)(2,1)S(1)}, u32[]{:S(2)}, u32[]{:S(2)}) collective-permute-start(bf16[512,256]{1,0:T(8,128)(2,1)S(1)} %collective-permute-done.4.refs_7_), channel_id=1, source_target_pairs={{8,16},{16,8},{9,17},{17,9},{10,18},{18,10},{11,19},{19,11},{12,20... | collective-permute-start | bytes 786440 | tf_op jit(solution)/shard_map/ppermute | solution.py:243
  56.9 24.1 %all-to-all-start.1 = ((bf16[8,144,256]{2,1,0:T(8,128)(2,1)}), bf16[8,144,256]{2,1,0:T(8,128)(2,1)S(1)}, u32[]{:S(2)}, u32[]{:S(2)}) async-start(bf16[8,144,256]{2,1,0:T(8,128)(2,1)} %get-tuple-element.7), calls=%async_computation.1 | async-start | bytes 1179648 | tf_op jit(solution)/shard_map/all_to_all | solution.py:278
  62.7 5.3 %collective-permute-start.25 = (f32[8,128]{1,0:T(8,128)S(1)}, f32[8,128]{1,0:T(8,128)S(1)}, u32[]{:S(2)}, u32[]{:S(2)}) collective-permute-start(f32[8,128]{1,0:T(8,128)S(1)} %copy-done.9), channel_id=1, source_target_pairs={{0,24},{8,16},{16,8},{24,0},{1,25},{9,17},{17,9},{25,1},{2,26},{10... | collective-permute-start | bytes 12296 | tf_op jit(solution)/shard_map/ppermute | solution.py:208
  63.6 6.0 %collective-permute-start.24 = (f32[8,128]{1,0:T(8,128)S(1)}, f32[8,128]{1,0:T(8,128)S(1)}, u32[]{:S(2)}, u32[]{:S(2)}) collective-permute-start(f32[8,128]{1,0:T(8,128)S(1)} %copy-done.9), channel_id=1, source_target_pairs={{0,16},{8,24},{16,0},{24,8},{1,17},{9,25},{17,1},{25,9},{2,18},{10... | collective-permute-start | bytes 12296 | tf_op jit(solution)/shard_map/ppermute | solution.py:208
  (18 other events, 183.6 us)
